TPU v7x, 32 devices: a whole 2x2x4 slice. The times are simulated.
32 devices in a mesh: dp: 8 (over y, x, core), tensor: 4 (over z).
Axes of the slice: x: 2, y: 2, z: 4, core: 2. Of those that a mesh axis runs over, the one named last changes fastest.
Arguments:
- cand_gate: bfloat16 [2048, 28672], P('dp', 'tensor'), may hold values from -6 to 6
- cand_up: bfloat16 [2048, 28672], P('dp', 'tensor'), may hold values from -6 to 6
- cand_dh: bfloat16 [2048, 28672], P('dp', 'tensor'), may hold values from -6 to 6
- cand_x: bfloat16 [2048, 8192], P('dp', 'tensor'), may hold values from -6 to 6
- cand_dy: bfloat16 [2048, 8192], P('dp', 'tensor'), may hold values from -6 to 6
- val_gate: bfloat16 [2048, 28672], P('dp', 'tensor'), may hold values from -6 to 6
- val_up: bfloat16 [2048, 28672], P('dp', 'tensor'), may hold values from -6 to 6
- val_dh: bfloat16 [2048, 28672], P('dp', 'tensor'), may hold values from -6 to 6
- val_x: bfloat16 [2048, 8192], P('dp', 'tensor'), may hold values from -6 to 6
- val_dy: bfloat16 [2048, 8192], P('dp', 'tensor'), may hold values from -6 to 6
- cand_lengths: int32 [8, 8], P('dp'), may hold values from 1 to 64, 256 in all within a row
- val_lengths: int32 [8, 8], replicated, may hold values from 1 to 64, 256 in all within a row
- round_owner: int32 [2], replicated, may hold values from 0 to 7
Outputs:
- scores: float32 [2, 64, 8], P(None, 'dp')
Inputs may be any that keep to these rules, and one draw needn't show every extreme that they name: Each row of cand_lengths sums to 256, and its largest entry is 64. Each row of val_lengths sums to 256, and its largest entry is 64.
All inputs are finite; a program needn't handle non-finite values.
Results may differ from a plain program's by a relative error of at most 0.0042.
Values may be sent and summed in bfloat16 or wider, within the bound.
No kernel may reach another device: no remote copies, remote signals or barrier semaphores. Data moves between devices by JAX's collectives and lax.ppermute only.
A program may use at most 128 MiB of HBM per device.

v0:
```python
import functools
import math

import jax
import jax.numpy as jnp
from jax import lax
from jax.experimental import pallas as pl
from jax.experimental.pallas import tpu as pltpu
from jax.sharding import PartitionSpec as P

D = 8192
FF = 28672
ROUNDS = 2
FB = 512
W = 3 * FB
VMEM = 60 * 1024 * 1024

START = 10
NT = (((1,), (1,)), ((), ()))


def derive(gate, up, grad_hidden):
    gate_f = gate.astype(jnp.float32)
    up_f = up.astype(jnp.float32)
    grad_f = grad_hidden.astype(jnp.float32)
    sigmoid_gate = jax.nn.sigmoid(gate_f)
    activated = gate_f * sigmoid_gate
    hidden = (activated * up_f).astype(jnp.bfloat16)
    grad_gate = (grad_f * up_f * sigmoid_gate * (1.0 + gate_f * (1.0 - sigmoid_gate))).astype(
        jnp.bfloat16
    )
    grad_up = (grad_f * activated).astype(jnp.bfloat16)
    return (grad_gate, grad_up, hidden)


def segment_of(lengths, total):
    bounds = jnp.cumsum(lengths)
    position = jnp.arange(total, dtype=jnp.int32)
    return jnp.sum((position[:, None] >= bounds[None, :]).astype(jnp.int32), axis=1)


def segments(j, width):
    out = []
    for which in (0, 1):
        lo = max(j * W, which * width)
        hi = min((j + 1) * W, (which + 1) * width)
        if hi > lo:
            out.append((which, lo - which * width, lo - j * W, hi - lo))
    return out


def pack_body(groups, width, first, transform, half, gate, up, dh, x, dy, *rest):
    out = rest[-2]
    k = pl.program_id(0) + first

    @pl.when(k < groups)
    def _():
        if transform:
            a, b, c = derive(gate[...], up[...], dh[...])
        else:
            a, b, c = gate[...], up[...], dh[...]
        out[0, :, 0:FB] = a
        out[0, :, FB : 2 * FB] = b
        out[0, :, 2 * FB : 3 * FB] = c

    for j in range(-(-2 * width // W)):

        @pl.when(k == groups + j)
        def _():
            end = 0
            for which, src, dst, cols in segments(j, width):
                out[0, :, dst : dst + cols] = (x, dy)[which][:, src : src + cols]
                end = dst + cols
            if end < W:
                out[0, :, end:W] = jnp.zeros((out.shape[1], W - end), out.dtype)


ANYWHERE = pl.BlockSpec(memory_space=pl.ANY)
IN_HBM = pl.BlockSpec(memory_space=pltpu.HBM)
MARK = jax.ShapeDtypeStruct((8, 128), jnp.float32)


def pack(half, rows, base, first, count, size, transform, held, deps, *arrays):
    groups, width = arrays[0].shape[1] // FB, arrays[3].shape[1]
    shift = first - base
    extra = ([] if held is None else [held]) + list(deps)
    wide = pl.BlockSpec(
        (rows, FB), lambda k, half: (half[0], jnp.minimum(k + first, groups - 1))
    )
    flat = pl.BlockSpec((rows, width), lambda k, half: (half[0], 0))
    return pl.pallas_call(
        functools.partial(pack_body, groups, width, first, transform),
        grid_spec=pltpu.PrefetchScalarGridSpec(
            num_scalar_prefetch=1,
            grid=(count,),
            in_specs=[wide, wide, wide, flat, flat] + [ANYWHERE] * len(extra),
            out_specs=[pl.BlockSpec((1, rows, W), lambda k, half: (k + shift, 0, 0)), IN_HBM],
        ),
        out_shape=[jax.ShapeDtypeStruct((size, rows, W), jnp.bfloat16), MARK],
        input_output_aliases={} if held is None else {6: 0},
        cost_estimate=pl.CostEstimate(
            flops=20 * count * rows * W if transform else 0,
            bytes_accessed=4 * count * rows * W,
            transcendentals=count * rows * FB if transform else 0,
        ),
        compiler_params=pltpu.CompilerParams(vmem_limit_bytes=VMEM),
    )(half, *arrays, *extra)


def inject_body(t, at, groups, width, always, info, gate, up, dh, x, dy, sib, *rest):
    out, room, sem = rest[-3:]
    rows = out.shape[0]
    start = pl.multiple_of(info[2] * rows, rows)
    mine = info[1] == 1
    first = jnp.logical_or(always, info[0] == 0)

    if t < groups:
        parts = [
            (ref.at[pl.ds(start, rows), pl.ds(t * FB, FB)], room.at[:, pl.ds(i * FB, FB)])
            for i, ref in enumerate((gate, up, dh))
        ]
    else:
        parts = [
            (
                (x, dy)[which].at[pl.ds(start, rows), pl.ds(src, cols)],
                room.at[:, pl.ds(dst, cols)],
            )
            for which, src, dst, cols in segments(t - groups, width)
        ]

    @pl.when(first)
    def _():
        @pl.when(mine)
        def _():
            copies = [pltpu.make_async_copy(a, b, sem.at[i]) for i, (a, b) in enumerate(parts)]
            for copy in copies:
                copy.start()
            for copy in copies:
                copy.wait()

        @pl.when(jnp.logical_not(mine))
        def _():
            copy = pltpu.make_async_copy(sib.at[at], room, sem.at[0])
            copy.start()
            copy.wait()

        copy = pltpu.make_async_copy(room, out, sem.at[0])
        copy.start()
        copy.wait()


def inject(t, at, rows, info, vals, sib, held, deps):
    groups, width = vals[0].shape[1] // FB, vals[3].shape[1]
    extra = ([] if held is None else [held]) + list(deps)
    return pl.pallas_call(
        functools.partial(inject_body, t, at, groups, width, held is None),
        in_specs=[pl.BlockSpec(memory_space=pltpu.SMEM)]
        + [IN_HBM] * (6 if held is None else 7)
        + [ANYWHERE] * len(deps),
        out_specs=IN_HBM,
        out_shape=jax.ShapeDtypeStruct((rows, W), jnp.bfloat16),
        scratch_shapes=[pltpu.VMEM((rows, W), jnp.bfloat16), pltpu.SemaphoreType.DMA((3,))],
        input_output_aliases={} if held is None else {7: 0},
        cost_estimate=pl.CostEstimate(
            flops=0, bytes_accessed=4 * rows * W, transcendentals=0
        ),
        compiler_params=pltpu.CompilerParams(vmem_limit_bytes=VMEM),
    )(info, *vals, sib, *extra)


def use_body(t, groups, width, bounds, info, *refs):
    r = pl.program_id(0)
    vals, pieces = refs[:ROUNDS], refs[ROUNDS : ROUNDS + 2 * len(bounds)]
    acc_in, acc = refs[ROUNDS + 2 * len(bounds)], refs[-2]
    k = t - info[r]
    acc[...] = acc_in[...]
    rows = pieces[0].shape[1]

    def add(slot, pair, cols, right):
        for side in (0, 1):
            left = pair[side][0, :, cols]
            acc[0, 0, slot, side * rows : (side + 1) * rows, :] += lax.dot_general(
                left, right, NT, preferred_element_type=jnp.float32
            )

    for i, (lo, hi) in enumerate(bounds):
        pair = pieces[2 * i : 2 * i + 2]
        for q in range(ROUNDS):
            val = vals[q]

            @pl.when((r == q) & (k >= lo) & (k < min(hi, groups)))
            def _():
                gd, ud, hidden = derive(val[:, 0:FB], val[:, FB : 2 * FB], val[:, 2 * FB : 3 * FB])
                add(0, pair, slice(0, FB), gd)
                add(0, pair, slice(FB, 2 * FB), ud)
                add(1, pair, slice(2 * FB, 3 * FB), hidden)

            for j in range(-(-2 * width // W)):
                if lo <= groups + j < hi:

                    @pl.when((r == q) & (k == groups + j))
                    def _():
                        for which, _, dst, cols in segments(j, width):
                            add(which, pair, slice(dst, dst + cols), val[:, dst : dst + cols])


def use(t, info, groups, width, vals, bounds, pieces, acc, deps):
    rows = pieces[0].shape[1]
    in_specs = [pl.BlockSpec(vals[0].shape, lambda r, info: (0, 0))] * ROUNDS
    for lo, hi in bounds:

        def chunk(r, info, lo=lo, hi=hi):
            return (jnp.clip(t - info[r], lo, hi - 1) - lo, 0, 0)

        in_specs += [pl.BlockSpec((1, rows, W), chunk)] * 2

    def kind(r, info):
        return (r, jnp.where(t - info[r] < groups, 0, 1), 0, 0, 0)

    tile = pl.BlockSpec((1, 1) + acc.shape[2:], kind)
    return pl.pallas_call(
        functools.partial(use_body, t, groups, width, bounds),
        grid_spec=pltpu.PrefetchScalarGridSpec(
            num_scalar_prefetch=1,
            grid=(ROUNDS,),
            in_specs=in_specs + [tile] + [ANYWHERE] * len(deps),
            out_specs=[tile, IN_HBM],
        ),
        out_shape=[jax.ShapeDtypeStruct(acc.shape, acc.dtype), MARK],
        input_output_aliases={len(in_specs) + 1: 0},
        cost_estimate=pl.CostEstimate(
            flops=8 * rows * vals[0].shape[0] * W,
            bytes_accessed=4 * (2 * rows + vals[0].shape[0]) * W,
            transcendentals=ROUNDS * vals[0].shape[0] * FB,
        ),
        compiler_params=pltpu.CompilerParams(vmem_limit_bytes=VMEM),
    )(info, *vals, *pieces, acc, *deps)


def cut_body(pieces, at, acc, own, *others):
    block = own.shape[2]
    for m in range(pieces):
        rows = pl.ds(pl.multiple_of(lax.rem(at[0] + m, pieces) * block, block), block)
        for r in range(ROUNDS):
            for slot in (0, 1):
                tile = acc[r, 0, slot, rows, :]
                if m == 0:
                    own[r, slot] = tile
                else:
                    others[m - 1][r, slot] = tile.astype(jnp.bfloat16)


def cut(kind, at_z, pieces, acc):
    block, half = acc.shape[3] // pieces, acc.shape[4]
    shape = (ROUNDS, 2, block, half)
    whole = pl.BlockSpec(shape, lambda i, at: (0, 0, 0, 0))
    return pl.pallas_call(
        functools.partial(cut_body, pieces),
        grid_spec=pltpu.PrefetchScalarGridSpec(
            num_scalar_prefetch=1,
            grid=(1,),
            in_specs=[
                pl.BlockSpec((ROUNDS, 1) + acc.shape[2:], lambda i, at: (0, kind, 0, 0, 0))
            ],
            out_specs=[whole] * pieces,
        ),
        out_shape=[jax.ShapeDtypeStruct(shape, jnp.float32)]
        + [jax.ShapeDtypeStruct(shape, jnp.bfloat16)] * (pieces - 1),
        cost_estimate=pl.CostEstimate(flops=0, bytes_accessed=8 * acc.size, transcendentals=0),
        compiler_params=pltpu.CompilerParams(vmem_limit_bytes=VMEM),
    )(at_z[None], acc)


def score_body(pieces, cand_hot, val_hot, *refs):
    out = refs[-1]
    kinds = (refs[:pieces], refs[pieces : 2 * pieces])
    for r in range(ROUNDS):
        sums = []
        for refs_of in kinds:
            for slot in (0, 1):
                total = refs_of[0][r, slot]
                for ref in refs_of[1:]:
                    total = total + ref[r, slot].astype(jnp.float32)
                sums.append(total)
        pair = sums[2] * sums[0] + sums[1] * sums[3]
        summed = jnp.dot(
            cand_hot[...],
            pair,
            precision=lax.Precision.HIGHEST,
            preferred_element_type=jnp.float32,
        )
        out[r] = jnp.dot(
            summed,
            val_hot[r],
            precision=lax.Precision.HIGHEST,
            preferred_element_type=jnp.float32,
        )


def score(cand_hot, val_hot, hidden_parts, input_parts):
    pieces = len(hidden_parts)
    return pl.pallas_call(
        functools.partial(score_body, pieces),
        out_shape=jax.ShapeDtypeStruct(
            (ROUNDS, cand_hot.shape[0], val_hot.shape[2]), jnp.float32
        ),
        compiler_params=pltpu.CompilerParams(vmem_limit_bytes=VMEM),
    )(cand_hot, val_hot, *hidden_parts, *input_parts)


def local(
    n_dp,
    n_tensor,
    cand_gate,
    cand_up,
    cand_dh,
    cand_x,
    cand_dy,
    val_gate,
    val_up,
    val_dh,
    val_x,
    val_dy,
    cand_lengths,
    val_lengths,
    round_owner,
):
    chips = n_dp // 2
    ring = list(range(chips // 2)) + list(range(chips - 1, chips // 2 - 1, -1))
    place = [ring.index(chip) for chip in range(chips)]
    along = []
    for i, chip in enumerate(ring):
        along.append((2 * chip, 2 * ring[(i + 1) % chips]))
        along.append((2 * chip + 1, 2 * ring[(i - 1) % chips] + 1))
    across = [(i, i ^ 1) for i in range(n_dp)]

    me = lax.axis_index("dp")
    at_z = lax.axis_index("tensor")
    core = me % 2
    places = jnp.asarray(place, jnp.int32)
    my_place = places[me // 2]

    cand_rows, val_rows = cand_x.shape[0], val_x.shape[0]
    half = val_rows // 2
    groups, width = cand_gate.shape[1] // FB, cand_x.shape[1]
    count = groups + -(-2 * width // W)
    vals = (val_gate, val_up, val_dh, val_x, val_dy)

    away, core_of = [], []
    for r in range(ROUNDS):
        owner = round_owner[r]
        behind = my_place - places[owner // 2]
        away.append(jnp.where(core == 0, behind, -behind) % chips)
        core_of.append((owner % 2 == core).astype(jnp.int32))

    sib_lengths = lax.ppermute(cand_lengths, "dp", across)

    info = [jnp.stack([away[r], core_of[r], core]) for r in range(ROUNDS)]
    aways = jnp.stack(away)
    other = (1 - core)[None]
    both = jnp.zeros((1,), jnp.int32)

    sib_parts = [None] * count

    def send_half(lo, hi, deps):
        part, mark = pack(other, half, lo, lo, hi - lo, hi - lo, False, None, deps, *vals)
        part = lax.ppermute(part, "dp", across)
        for t in range(lo, hi):
            sib_parts[t] = (part, t - lo)
        return mark

    middle = min(groups, max(1, count // 2))
    bounds = [(0, middle), (middle, count)]
    cand_own, cand_sib = [None, None], [None, None]

    def derive_some(i, lo, hi, deps):
        base, end = bounds[i]
        cand_own[i], mark = pack(
            both, cand_rows, base, lo, hi - lo, end - base, True, cand_own[i], deps,
            cand_gate, cand_up, cand_dh, cand_x, cand_dy,
        )
        if hi == end:
            cand_sib[i] = lax.ppermute(cand_own[i], "dp", across)
        return mark

    grams = [jnp.zeros((ROUNDS, 2, 2, 2 * cand_rows, half), jnp.float32)]
    steps = count + chips - 1
    held = [[None] * steps for _ in range(ROUNDS)]
    got = [None] * ROUNDS
    parts, wait_for = [], []

    def scatter(kind):
        pieces = cut(kind, at_z, n_tensor, grams[0])
        wait_for[:] = [pieces[0]]
        return [pieces[0]] + [
            lax.ppermute(pieces[m], "tensor", [(z, (z + m) % n_tensor) for z in range(n_tensor)])
            for m in range(1, n_tensor)
        ]

    def consume(t, deps):
        low, high = t - (chips - 1), t
        needed = [i for i, (lo, hi) in enumerate(bounds) if low < hi and high >= lo]
        pieces = []
        for i in needed:
            pieces += [cand_own[i], cand_sib[i]]
        grams[0], mark = use(
            t, aways, groups, width, [held[r][t] for r in range(ROUNDS)],
            [bounds[i] for i in needed], pieces, grams[0], deps + wait_for,
        )
        wait_for[:] = []
        if t == groups + chips - 2:
            parts.append(scatter(0))
        return mark

    work = []
    cuts = [c for c in (4, 8, 12) if c < count] + [count]
    for lo, hi in zip(cuts[:-1], cuts[1:]):
        work.append((0, functools.partial(send_half, lo, hi)))
    for i, (lo, hi) in enumerate(bounds):
        for a in range(lo, hi, 3):
            work.append((0, functools.partial(derive_some, i, a, min(a + 3, hi))))
    for t in range(steps):
        work.append((max(t * ROUNDS + ROUNDS - 1, START), functools.partial(consume, t)))

    mark = send_half(0, 1, [])
    mark = send_half(1, min(4, count), [mark])
    slot = 0
    for t in range(steps):
        for r in range(ROUNDS):
            if t < count:
                part, at = sib_parts[t]
                held[r][t] = inject(t, at, half, info[r], vals, part, got[r], [mark])
            else:
                held[r][t] = got[r]
            if t < steps - 1:
                got[r] = lax.ppermute(held[r][t], "dp", along)
            if work and work[0][0] <= slot:
                mark = work.pop(0)[1]([held[r][t]])
            slot += 1
    while work:
        mark = work.pop(0)[1]([mark])
    parts.append(scatter(1))
    block = 2 * cand_rows // n_tensor

    samples = cand_lengths.shape[1]
    segs = jnp.concatenate(
        [
            segment_of(cand_lengths[0], cand_rows),
            segment_of(sib_lengths[0], cand_rows) + samples,
        ]
    )
    segs = lax.dynamic_slice_in_dim(segs, at_z * block, block, 0)
    cand_hot = (jnp.arange(2 * samples, dtype=jnp.int32)[:, None] == segs[None, :]).astype(
        jnp.float32
    )
    hots, weights = [], []
    for r in range(ROUNDS):
        lengths = lax.dynamic_index_in_dim(val_lengths, round_owner[r], 0, keepdims=False)
        seg = lax.dynamic_slice_in_dim(segment_of(lengths, val_rows), core * half, half, 0)
        hots.append((seg[:, None] == jnp.arange(128, dtype=jnp.int32)[None, :]).astype(jnp.float32))
        weights.append(
            1.0
            / math.sqrt(D * FF)
            / jnp.sqrt(
                cand_lengths[0].astype(jnp.float32)[:, None]
                * lengths.astype(jnp.float32)[None, :]
            )
        )
    partial = score(cand_hot, jnp.stack(hots, axis=0), *parts)

    total = partial[:, :samples]
    for m in range(n_tensor):
        turn = [(z, (z + m) % n_tensor) for z in range(n_tensor)]
        if m > 0:
            total = total + lax.ppermute(partial[:, :samples], "tensor", turn)
        both = [
            (i * n_tensor + z, (i ^ 1) * n_tensor + (z + m) % n_tensor)
            for i in range(n_dp)
            for z in range(n_tensor)
        ]
        total = total + lax.ppermute(partial[:, samples:], ("dp", "tensor"), both)
    return total[:, :, : val_lengths.shape[1]] * jnp.stack(weights, axis=0)


def solution(mesh):
    n_dp, n_tensor = mesh.shape["dp"], mesh.shape["tensor"]
    in_specs = (P("dp", "tensor"),) * 10 + (P("dp", None), P(), P())
    return jax.shard_map(
        functools.partial(local, n_dp, n_tensor),
        mesh=mesh,
        in_specs=in_specs,
        out_specs=P(None, "dp", None),
        check_vma=False,
    )
```

profile of v0, /device:TPU:0, one launch (start us, length us, event | category | flops | bytes accessed | tf_op | source)
XLA Modules:
  0.0 336.9 jit_solution(10446938125116553041)
XLA Ops:
  31.0 4.1 %shard_map.141 = (bf16[4,128,1536]{2,1,0:T(8,128)(2,1)}, f32[8,128]{1,0:T(8,128)}) custom-call(s32[1]{0:T(128)} %bitcast.17.half, bf16[256,7168]{1,0:T(8,128)(2,1)} %gate.89, bf16[256,7168]{1,0:T(8,128)(2,1)} %up.89, bf16[256,7168]{1,0:T(8,128)(2,1)} %dh.89, bf16[256,2048]{1,0:T(8,128)(2,1)} %x.89, bf16[256,2048]{1,0:T(8,128)(2,1)} %dy.89, ...), custom_call_target="tpu_custom_call" | custom-call | bytes 3145728 | tf_op jit(solution)/shard_map/pallas_call | solution.py:91
  46.5 5.1 %shard_map.145 = (bf16[8,256,1536]{2,1,0:T(8,128)(2,1)}, f32[8,128]{1,0:T(8,128)}) custom-call(s32[1]{0:T(128)} %constant.96.clone.1.half, bf16[256,7168]{1,0:T(8,128)(2,1)} %gate.64, bf16[256,7168]{1,0:T(8,128)(2,1)} %up.64, bf16[256,7168]{1,0:T(8,128)(2,1)} %dh.64, bf16[256,2048]{1,0:T(8,128)(2,1)} %x.64, bf16[256,2048]{1,0:T(8,128)(2,1)} %dy.64, ...), custom_call_target="tpu_custom_call" | custom-call | flops 23592960 | bytes 4718592 | tf_op jit(solution)/shard_map/pallas_call | solution.py:91
  55.0 5.1 %shard_map.147 = (bf16[8,256,1536]{2,1,0:T(8,128)(2,1)}, f32[8,128]{1,0:T(8,128)}) custom-call(s32[1]{0:T(128)} %constant.96.clone.1.half, bf16[256,7168]{1,0:T(8,128)(2,1)} %gate.64, bf16[256,7168]{1,0:T(8,128)(2,1)} %up.64, bf16[256,7168]{1,0:T(8,128)(2,1)} %dh.64, bf16[256,2048]{1,0:T(8,128)(2,1)} %x.64, ...), custom_call_target="tpu_custom_call", output_to_operand_aliasing={{0}: (6, {})} | custom-call | flops 23592960 | bytes 4718592 | tf_op jit(solution)/shard_map/pallas_call | solution.py:91
  70.9 5.1 %shard_map.151 = (bf16[9,256,1536]{2,1,0:T(8,128)(2,1)}, f32[8,128]{1,0:T(8,128)}) custom-call(s32[1]{0:T(128)} %constant.96.clone.1.half, bf16[256,7168]{1,0:T(8,128)(2,1)} %gate.64, bf16[256,7168]{1,0:T(8,128)(2,1)} %up.64, bf16[256,7168]{1,0:T(8,128)(2,1)} %dh.64, bf16[256,2048]{1,0:T(8,128)(2,1)} %x.64, bf16[256,2048]{1,0:T(8,128)(2,1)} %dy.64, ...), custom_call_target="tpu_custom_call" | custom-call | flops 23592960 | bytes 4718592 | tf_op jit(solution)/shard_map/pallas_call | solution.py:91
  77.5 5.2 %shard_map.153 = (bf16[9,256,1536]{2,1,0:T(8,128)(2,1)}, f32[8,128]{1,0:T(8,128)}) custom-call(s32[1]{0:T(128)} %constant.96.clone.1.half, bf16[256,7168]{1,0:T(8,128)(2,1)} %gate.64, bf16[256,7168]{1,0:T(8,128)(2,1)} %up.64, bf16[256,7168]{1,0:T(8,128)(2,1)} %dh.64, bf16[256,2048]{1,0:T(8,128)(2,1)} %x.64, ...), custom_call_target="tpu_custom_call", output_to_operand_aliasing={{0}: (6, {})} | custom-call | flops 23592960 | bytes 4718592 | tf_op jit(solution)/shard_map/pallas_call | solution.py:91
  92.2 5.2 %collective-permute-done.16.rest_0_ = bf16[128,1536]{1,0:T(8,128)(2,1)S(1)} collective-permute-done((bf16[128,1536]{1,0:T(8,128)(2,1)S(1)}, bf16[128,1536]{1,0:T(8,128)(2,1)S(1)}, u32[]{:S(2)}, u32[]{:S(2)}) %collective-permute-start.16) | collective-permute-done | bytes 393248 | tf_op jit(solution)/shard_map/ppermute | solution.py:436
  98.9 4.3 %collective-permute-start.17 = (bf16[128,1536]{1,0:T(8,128)(2,1)}, bf16[128,1536]{1,0:T(8,128)(2,1)S(1)}, u32[]{:S(2)}, u32[]{:S(2)}) collective-permute-start(bf16[128,1536]{1,0:T(8,128)(2,1)} %shard_map.158.refs_1_), channel_id=1, source_target_pairs={{0,8},{4,20},{8,24},{12,4},{24,16},{28,12},{16,0},{20,28},{1,9},{5... | collective-permute-start | bytes 1179656 | tf_op jit(solution)/shard_map/ppermute | solution.py:436
  132.8 4.7 %shard_map.164 = (f32[2,2,2,512,128]{4,3,2,1,0:T(8,128)}, f32[8,128]{1,0:T(8,128)}) custom-call(s32[2]{0:T(128)} %pad_add_fusion.1.info, bf16[128,1536]{1,0:T(8,128)(2,1)} %shard_map.150.rest_0_.refs_0_, bf16[128,1536]{1,0:T(8,128)(2,1)} %shard_map.152.rest_1_.refs_1_, ...), custom_call_target="tpu_custom_call", output_to_operand_aliasing={{0}: (5, {})} | custom-call | flops 402653184 | bytes 3932160 | tf_op jit(solution)/shard_map/pallas_call | solution.py:221
  141.0 4.7 %shard_map.166 = (f32[2,2,2,512,128]{4,3,2,1,0:T(8,128)}, f32[8,128]{1,0:T(8,128)}) custom-call(s32[2]{0:T(128)} %pad_add_fusion.1.info, bf16[128,1536]{1,0:T(8,128)(2,1)} %shard_map.154.rest_1_.refs_0_, bf16[128,1536]{1,0:T(8,128)(2,1)} %shard_map.158.refs_1_, bf16[8,256,1536]{2,1,0:T(8,128)(2,1)} %get-tuple-element.91.refs_2_, ...), custom_call_target="tpu_custom_call", output_to_operand_aliasing={{0}: (5, {})} | custom-call | flops 402653184 | bytes 3932160 | tf_op jit(solution)/shard_map/pallas_call | solution.py:221
  149.0 4.7 %shard_map.168 = (f32[2,2,2,512,128]{4,3,2,1,0:T(8,128)}, f32[8,128]{1,0:T(8,128)}) custom-call(s32[2]{0:T(128)} %pad_add_fusion.1.info, bf16[128,1536]{1,0:T(8,128)(2,1)} %shard_map.156.refs_5_.refs_0_, bf16[128,1536]{1,0:T(8,128)(2,1)} %shard_map.159.refs_5_.refs_1_, ...), custom_call_target="tpu_custom_call", output_to_operand_aliasing={{0}: (5, {})} | custom-call | flops 402653184 | bytes 3932160 | tf_op jit(solution)/shard_map/pallas_call | solution.py:221
  157.5 4.7 %shard_map.170 = (f32[2,2,2,512,128]{4,3,2,1,0:T(8,128)}, f32[8,128]{1,0:T(8,128)}) custom-call(s32[2]{0:T(128)} %pad_add_fusion.1.info, bf16[128,1536]{1,0:T(8,128)(2,1)} %shard_map.161.refs_5_.refs_0_, bf16[128,1536]{1,0:T(8,128)(2,1)} %shard_map.163.refs_5_.refs_1_, ...), custom_call_target="tpu_custom_call", output_to_operand_aliasing={{0}: (5, {})} | custom-call | flops 402653184 | bytes 3932160 | tf_op jit(solution)/shard_map/pallas_call | solution.py:221
  164.7 4.7 %shard_map.172 = (f32[2,2,2,512,128]{4,3,2,1,0:T(8,128)}, f32[8,128]{1,0:T(8,128)}) custom-call(s32[2]{0:T(128)} %pad_add_fusion.1.info, bf16[128,1536]{1,0:T(8,128)(2,1)} %shard_map.165.refs_5_.refs_0_, bf16[128,1536]{1,0:T(8,128)(2,1)} %shard_map.167.refs_5_.refs_1_, ...), custom_call_target="tpu_custom_call", output_to_operand_aliasing={{0}: (5, {})} | custom-call | flops 402653184 | bytes 3932160 | tf_op jit(solution)/shard_map/pallas_call | solution.py:221
  172.7 5.3 %shard_map.174 = (f32[2,2,2,512,128]{4,3,2,1,0:T(8,128)}, f32[8,128]{1,0:T(8,128)}) custom-call(s32[2]{0:T(128)} %pad_add_fusion.1.info, bf16[128,1536]{1,0:T(8,128)(2,1)} %shard_map.169.refs_5_.refs_0_, bf16[128,1536]{1,0:T(8,128)(2,1)} %shard_map.171.refs_5_.refs_1_, ...), custom_call_target="tpu_custom_call", output_to_operand_aliasing={{0}: (7, {})} | custom-call | flops 402653184 | bytes 3932160 | tf_op jit(solution)/shard_map/pallas_call | solution.py:221
  181.7 5.3 %shard_map.176 = (f32[2,2,2,512,128]{4,3,2,1,0:T(8,128)}, f32[8,128]{1,0:T(8,128)}) custom-call(s32[2]{0:T(128)} %pad_add_fusion.1.info, bf16[128,1536]{1,0:T(8,128)(2,1)} %shard_map.173.refs_7_.refs_0_, bf16[128,1536]{1,0:T(8,128)(2,1)} %shard_map.175.refs_1_.refs_7_, ...), custom_call_target="tpu_custom_call", output_to_operand_aliasing={{0}: (7, {})} | custom-call | flops 402653184 | bytes 3932160 | tf_op jit(solution)/shard_map/pallas_call | solution.py:221
  193.6 5.3 %shard_map.179 = (f32[2,2,2,512,128]{4,3,2,1,0:T(8,128)}, f32[8,128]{1,0:T(8,128)}) custom-call(s32[2]{0:T(128)} %pad_add_fusion.1.info, bf16[128,1536]{1,0:T(8,128)(2,1)} %shard_map.177.refs_0_, bf16[128,1536]{1,0:T(8,128)(2,1)} %shard_map.178.refs_1_.refs_7_, bf16[8,256,1536]{2,1,0:T(8,128)(2,1)} %get-tuple-element.91.refs_2_, ...), custom_call_target="tpu_custom_call", output_to_operand_aliasing={{0}: (7, {})} | custom-call | flops 402653184 | bytes 3932160 | tf_op jit(solution)/shard_map/pallas_call | solution.py:221
  205.9 4.7 %shard_map.182 = (f32[2,2,2,512,128]{4,3,2,1,0:T(8,128)}, f32[8,128]{1,0:T(8,128)}) custom-call(s32[2]{0:T(128)} %pad_add_fusion.1.info, bf16[128,1536]{1,0:T(8,128)(2,1)} %shard_map.180.refs_0_, bf16[128,1536]{1,0:T(8,128)(2,1)} %shard_map.181.refs_1_.refs_5_, ...), custom_call_target="tpu_custom_call", output_to_operand_aliasing={{0}: (5, {})} | custom-call | flops 402653184 | bytes 3932160 | tf_op jit(solution)/shard_map/pallas_call | solution.py:221
  217.9 4.7 %shard_map.185 = (f32[2,2,2,512,128]{4,3,2,1,0:T(8,128)}, f32[8,128]{1,0:T(8,128)}) custom-call(s32[2]{0:T(128)} %pad_add_fusion.1.info, bf16[128,1536]{1,0:T(8,128)(2,1)} %shard_map.183.refs_0_, bf16[128,1536]{1,0:T(8,128)(2,1)} %shard_map.184.refs_1_.refs_5_, ...), custom_call_target="tpu_custom_call", output_to_operand_aliasing={{0}: (5, {})} | custom-call | flops 402653184 | bytes 3932160 | tf_op jit(solution)/shard_map/pallas_call | solution.py:221
  230.0 4.7 %shard_map.188 = (f32[2,2,2,512,128]{4,3,2,1,0:T(8,128)}, f32[8,128]{1,0:T(8,128)}) custom-call(s32[2]{0:T(128)} %pad_add_fusion.1.info, bf16[128,1536]{1,0:T(8,128)(2,1)} %shard_map.186.refs_0_, bf16[128,1536]{1,0:T(8,128)(2,1)} %shard_map.187.refs_1_.refs_5_, ...), custom_call_target="tpu_custom_call", output_to_operand_aliasing={{0}: (5, {})} | custom-call | flops 402653184 | bytes 3932160 | tf_op jit(solution)/shard_map/pallas_call | solution.py:221
  241.6 4.7 %shard_map.191 = (f32[2,2,2,512,128]{4,3,2,1,0:T(8,128)}, f32[8,128]{1,0:T(8,128)}) custom-call(s32[2]{0:T(128)} %pad_add_fusion.1.info, bf16[128,1536]{1,0:T(8,128)(2,1)} %shard_map.189.refs_0_, bf16[128,1536]{1,0:T(8,128)(2,1)} %shard_map.190.refs_1_.refs_5_, ...), custom_call_target="tpu_custom_call", output_to_operand_aliasing={{0}: (5, {})} | custom-call | flops 402653184 | bytes 3932160 | tf_op jit(solution)/shard_map/pallas_call | solution.py:221
  253.5 4.7 %shard_map.194 = (f32[2,2,2,512,128]{4,3,2,1,0:T(8,128)}, f32[8,128]{1,0:T(8,128)}) custom-call(s32[2]{0:T(128)} %pad_add_fusion.1.info, bf16[128,1536]{1,0:T(8,128)(2,1)} %shard_map.192.refs_0_, bf16[128,1536]{1,0:T(8,128)(2,1)} %shard_map.193.refs_1_.refs_5_, ...), custom_call_target="tpu_custom_call", output_to_operand_aliasing={{0}: (5, {})} | custom-call | flops 402653184 | bytes 3932160 | tf_op jit(solution)/shard_map/pallas_call | solution.py:221
  282.0 4.7 %shard_map.197 = (f32[2,2,2,512,128]{4,3,2,1,0:T(8,128)}, f32[8,128]{1,0:T(8,128)}) custom-call(s32[2]{0:T(128)} %pad_add_fusion.1.info, bf16[128,1536]{1,0:T(8,128)(2,1)} %shard_map.195.refs_0_, bf16[128,1536]{1,0:T(8,128)(2,1)} %shard_map.196.refs_1_.refs_5_, ...), custom_call_target="tpu_custom_call", output_to_operand_aliasing={{0}: (5, {})} | custom-call | flops 402653184 | bytes 3932160 | tf_op jit(solution)/shard_map/pallas_call | solution.py:221
  294.7 4.6 %shard_map.199 = (f32[2,2,2,512,128]{4,3,2,1,0:T(8,128)}, f32[8,128]{1,0:T(8,128)}) custom-call(s32[2]{0:T(128)} %pad_add_fusion.1.info, bf16[128,1536]{1,0:T(8,128)(2,1)} %copy-done.42, bf16[128,1536]{1,0:T(8,128)(2,1)} %copy-done.32, bf16[9,256,1536]{2,1,0:T(8,128)(2,1)} %get-tuple-element.107.refs_4_.refs_2_, ...), custom_call_target="tpu_custom_call", output_to_operand_aliasing={{0}: (5, {})} | custom-call | flops 402653184 | bytes 3932160 | tf_op jit(solution)/shard_map/pallas_call | solution.py:221
  299.3 4.6 %shard_map.200 = (f32[2,2,2,512,128]{4,3,2,1,0:T(8,128)}, f32[8,128]{1,0:T(8,128)}) custom-call(s32[2]{0:T(128)} %pad_add_fusion.1.info, bf16[128,1536]{1,0:T(8,128)(2,1)} %copy-done.43, bf16[128,1536]{1,0:T(8,128)(2,1)} %copy-done.33, bf16[9,256,1536]{2,1,0:T(8,128)(2,1)} %get-tuple-element.107.refs_4_.refs_2_, ...), custom_call_target="tpu_custom_call", output_to_operand_aliasing={{0}: (5, {})} | custom-call | flops 402653184 | bytes 3932160 | tf_op jit(solution)/shard_map/pallas_call | solution.py:221
  304.8 4.3 %shard_map.201 = (f32[2,2,2,512,128]{4,3,2,1,0:T(8,128)}, f32[8,128]{1,0:T(8,128)}) custom-call(s32[2]{0:T(128)} %pad_add_fusion.1.info, bf16[128,1536]{1,0:T(8,128)(2,1)} %copy-done.44, bf16[128,1536]{1,0:T(8,128)(2,1)} %copy-done.34, bf16[9,256,1536]{2,1,0:T(8,128)(2,1)} %get-tuple-element.107.refs_4_.refs_2_, ...), custom_call_target="tpu_custom_call", output_to_operand_aliasing={{0}: (5, {})} | custom-call | flops 402653184 | bytes 3932160 | tf_op jit(solution)/shard_map/pallas_call | solution.py:221
  (300 shorter events, 210.0 us)
Async XLA Ops:
  5.8 29.3 %collective-permute-start.1 = (bf16[3,128,1536]{2,1,0:T(8,128)(2,1)}, bf16[3,128,1536]{2,1,0:T(8,128)(2,1)S(1)}, u32[]{:S(2)}, u32[]{:S(2)}) collective-permute-start(bf16[3,128,1536]{2,1,0:T(8,128)(2,1)} %get-tuple-element.72), channel_id=1, source_target_pairs={{0,4},{4,0},{8,12},{12,8},{16,20},{20,16},{24,28},{28,24},{1,5},{5... | collective-permute-start | bytes 3538952 | tf_op jit(solution)/shard_map/ppermute | solution.py:367
  19.3 15.8 %collective-permute-start.3 = (bf16[128,1536]{1,0:T(8,128)(2,1)}, bf16[128,1536]{1,0:T(8,128)(2,1)S(1)}, u32[]{:S(2)}, u32[]{:S(2)}) collective-permute-start(bf16[128,1536]{1,0:T(8,128)(2,1)} %shard_map.138.rest_0_.refs_0_), channel_id=1, source_target_pairs={{0,8},{4,20},{8,24},{12,4},{24,16},{28,12},{16,0},{20,28},{1,9},{5... | collective-permute-start | bytes 1179656 | tf_op jit(solution)/shard_map/ppermute | solution.py:436
  29.4 13.8 %collective-permute-start.8 = (bf16[128,1536]{1,0:T(8,128)(2,1)}, bf16[128,1536]{1,0:T(8,128)(2,1)S(1)}, u32[]{:S(2)}, u32[]{:S(2)}) collective-permute-start(bf16[128,1536]{1,0:T(8,128)(2,1)} %shard_map.140.rest_0_.refs_1_), channel_id=1, source_target_pairs={{0,8},{4,20},{8,24},{12,4},{24,16},{28,12},{16,0},{20,28},{1,9},{5... | collective-permute-start | bytes 1179656 | tf_op jit(solution)/shard_map/ppermute | solution.py:436
  31.0 51.7 %collective-permute-start.6 = (bf16[4,128,1536]{2,1,0:T(8,128)(2,1)}, bf16[4,128,1536]{2,1,0:T(8,128)(2,1)S(1)}, u32[]{:S(2)}, u32[]{:S(2)}) collective-permute-start(bf16[4,128,1536]{2,1,0:T(8,128)(2,1)} %get-tuple-element.79), channel_id=1, source_target_pairs={{0,4},{4,0},{8,12},{12,8},{16,20},{20,16},{24,28},{28,24},{1,5},{5... | collective-permute-start | bytes 4718600 | tf_op jit(solution)/shard_map/ppermute | solution.py:367
  37.0 14.6 %collective-permute-start.7 = (bf16[128,1536]{1,0:T(8,128)(2,1)}, bf16[128,1536]{1,0:T(8,128)(2,1)S(1)}, u32[]{:S(2)}, u32[]{:S(2)}) collective-permute-start(bf16[128,1536]{1,0:T(8,128)(2,1)} %shard_map.142.rest_0_.refs_0_), channel_id=1, source_target_pairs={{0,8},{4,20},{8,24},{12,4},{24,16},{28,12},{16,0},{20,28},{1,9},{5... | collective-permute-start | bytes 1179656 | tf_op jit(solution)/shard_map/ppermute | solution.py:436
  44.7 15.5 %collective-permute-start.10 = (bf16[128,1536]{1,0:T(8,128)(2,1)}, bf16[128,1536]{1,0:T(8,128)(2,1)S(1)}, u32[]{:S(2)}, u32[]{:S(2)}) collective-permute-start(bf16[128,1536]{1,0:T(8,128)(2,1)} %shard_map.144.rest_0_.refs_1_), channel_id=1, source_target_pairs={{0,8},{4,20},{8,24},{12,4},{24,16},{28,12},{16,0},{20,28},{1,9},{5... | collective-permute-start | bytes 1179656 | tf_op jit(solution)/shard_map/ppermute | solution.py:436
  53.1 14.4 %collective-permute-start.9 = (bf16[128,1536]{1,0:T(8,128)(2,1)}, bf16[128,1536]{1,0:T(8,128)(2,1)S(1)}, u32[]{:S(2)}, u32[]{:S(2)}) collective-permute-start(bf16[128,1536]{1,0:T(8,128)(2,1)} %shard_map.146.rest_1_.refs_0_), channel_id=1, source_target_pairs={{0,8},{4,20},{8,24},{12,4},{24,16},{28,12},{16,0},{20,28},{1,9},{5... | collective-permute-start | bytes 1179656 | tf_op jit(solution)/shard_map/ppermute | solution.py:436
  65.2 42.1 %collective-permute-start.15 = (bf16[8,256,1536]{2,1,0:T(8,128)(2,1)}, bf16[8,256,1536]{2,1,0:T(8,128)(2,1)}, u32[]{:S(2)}, u32[]{:S(2)}) collective-permute-start(bf16[8,256,1536]{2,1,0:T(8,128)(2,1)} %get-tuple-element.91.refs_2_), channel_id=1, source_target_pairs={{0,4},{4,0},{8,12},{12,8},{16,20},{20,16},{24,28},{28,24},{1,5},{5... | collective-permute-start | bytes 18874376 | tf_op jit(solution)/shard_map/ppermute | solution.py:383
  88.5 84.3 %collective-permute-start.26 = (bf16[9,256,1536]{2,1,0:T(8,128)(2,1)}, bf16[9,256,1536]{2,1,0:T(8,128)(2,1)}, u32[]{:S(2)}, u32[]{:S(2)}) collective-permute-start(bf16[9,256,1536]{2,1,0:T(8,128)(2,1)} %get-tuple-element.107.refs_4_.refs_2_), channel_id=1, source_target_pairs={{0,4},{4,0},{8,12},{12,8},{16,20},{20,16},{24,28},{28,24},{1,5},{5... | collective-permute-start | bytes 21233672 | tf_op jit(solution)/shard_map/ppermute | solution.py:383
  92.2 61.5 %collective-permute-start.5 = (bf16[4,128,1536]{2,1,0:T(8,128)(2,1)}, bf16[4,128,1536]{2,1,0:T(8,128)(2,1)S(1)}, u32[]{:S(2)}, u32[]{:S(2)}) collective-permute-start(bf16[4,128,1536]{2,1,0:T(8,128)(2,1)} %get-tuple-element.78), channel_id=1, source_target_pairs={{0,4},{4,0},{8,12},{12,8},{16,20},{20,16},{24,28},{28,24},{1,5},{5... | collective-permute-start | bytes 4718600 | tf_op jit(solution)/shard_map/ppermute | solution.py:367
  105.3 15.1 %collective-permute-start.14 = (bf16[128,1536]{1,0:T(8,128)(2,1)}, bf16[128,1536]{1,0:T(8,128)(2,1)S(1)}, u32[]{:S(2)}, u32[]{:S(2)}) collective-permute-start(bf16[128,1536]{1,0:T(8,128)(2,1)} %shard_map.156.refs_5_.refs_0_), channel_id=1, source_target_pairs={{0,8},{4,20},{8,24},{12,4},{24,16},{28,12},{16,0},{20,28},{1,9},{5... | collective-permute-start | bytes 1179656 | tf_op jit(solution)/shard_map/ppermute | solution.py:436
  113.9 14.5 %collective-permute-start.19 = (bf16[128,1536]{1,0:T(8,128)(2,1)}, bf16[128,1536]{1,0:T(8,128)(2,1)S(1)}, u32[]{:S(2)}, u32[]{:S(2)}) collective-permute-start(bf16[128,1536]{1,0:T(8,128)(2,1)} %shard_map.159.refs_5_.refs_1_), channel_id=1, source_target_pairs={{0,8},{4,20},{8,24},{12,4},{24,16},{28,12},{16,0},{20,28},{1,9},{5... | collective-permute-start | bytes 1179656 | tf_op jit(solution)/shard_map/ppermute | solution.py:436
  121.8 15.6 %collective-permute-start.18 = (bf16[128,1536]{1,0:T(8,128)(2,1)}, bf16[128,1536]{1,0:T(8,128)(2,1)S(1)}, u32[]{:S(2)}, u32[]{:S(2)}) collective-permute-start(bf16[128,1536]{1,0:T(8,128)(2,1)} %shard_map.161.refs_5_.refs_0_), channel_id=1, source_target_pairs={{0,8},{4,20},{8,24},{12,4},{24,16},{28,12},{16,0},{20,28},{1,9},{5... | collective-permute-start | bytes 1179656 | tf_op jit(solution)/shard_map/ppermute | solution.py:436
  129.8 15.9 %collective-permute-start.21 = (bf16[128,1536]{1,0:T(8,128)(2,1)}, bf16[128,1536]{1,0:T(8,128)(2,1)S(1)}, u32[]{:S(2)}, u32[]{:S(2)}) collective-permute-start(bf16[128,1536]{1,0:T(8,128)(2,1)} %shard_map.163.refs_5_.refs_1_), channel_id=1, source_target_pairs={{0,8},{4,20},{8,24},{12,4},{24,16},{28,12},{16,0},{20,28},{1,9},{5... | collective-permute-start | bytes 1179656 | tf_op jit(solution)/shard_map/ppermute | solution.py:436
  138.9 14.7 %collective-permute-start.20 = (bf16[128,1536]{1,0:T(8,128)(2,1)}, bf16[128,1536]{1,0:T(8,128)(2,1)S(1)}, u32[]{:S(2)}, u32[]{:S(2)}) collective-permute-start(bf16[128,1536]{1,0:T(8,128)(2,1)} %shard_map.165.refs_5_.refs_0_), channel_id=1, source_target_pairs={{0,8},{4,20},{8,24},{12,4},{24,16},{28,12},{16,0},{20,28},{1,9},{5... | collective-permute-start | bytes 1179656 | tf_op jit(solution)/shard_map/ppermute | solution.py:436
  147.1 15.1 %collective-permute-start.23 = (bf16[128,1536]{1,0:T(8,128)(2,1)}, bf16[128,1536]{1,0:T(8,128)(2,1)}, u32[]{:S(2)}, u32[]{:S(2)}) collective-permute-start(bf16[128,1536]{1,0:T(8,128)(2,1)} %shard_map.167.refs_5_.refs_1_), channel_id=1, source_target_pairs={{0,8},{4,20},{8,24},{12,4},{24,16},{28,12},{16,0},{20,28},{1,9},{5... | collective-permute-start | bytes 1179656 | tf_op jit(solution)/shard_map/ppermute | solution.py:436
  149.0 61.7 %collective-permute-start.4 = (bf16[5,128,1536]{2,1,0:T(8,128)(2,1)}, bf16[5,128,1536]{2,1,0:T(8,128)(2,1)S(1)}, u32[]{:S(2)}, u32[]{:S(2)}) collective-permute-start(bf16[5,128,1536]{2,1,0:T(8,128)(2,1)} %get-tuple-element.77), channel_id=1, source_target_pairs={{0,4},{4,0},{8,12},{12,8},{16,20},{20,16},{24,28},{28,24},{1,5},{5... | collective-permute-start | bytes 5898248 | tf_op jit(solution)/shard_map/ppermute | solution.py:367
  162.9 15.1 %collective-permute-start.25 = (bf16[128,1536]{1,0:T(8,128)(2,1)}, bf16[128,1536]{1,0:T(8,128)(2,1)S(1)}, u32[]{:S(2)}, u32[]{:S(2)}) collective-permute-start(bf16[128,1536]{1,0:T(8,128)(2,1)} %shard_map.171.refs_5_.refs_1_), channel_id=1, source_target_pairs={{0,8},{4,20},{8,24},{12,4},{24,16},{28,12},{16,0},{20,28},{1,9},{5... | collective-permute-start | bytes 1179656 | tf_op jit(solution)/shard_map/ppermute | solution.py:436
  170.9 16.1 %collective-permute-start.24 = (bf16[128,1536]{1,0:T(8,128)(2,1)}, bf16[128,1536]{1,0:T(8,128)(2,1)S(1)}, u32[]{:S(2)}, u32[]{:S(2)}) collective-permute-start(bf16[128,1536]{1,0:T(8,128)(2,1)} %shard_map.173.refs_7_.refs_0_), channel_id=1, source_target_pairs={{0,8},{4,20},{8,24},{12,4},{24,16},{28,12},{16,0},{20,28},{1,9},{5... | collective-permute-start | bytes 1179656 | tf_op jit(solution)/shard_map/ppermute | solution.py:436
  276.7 27.2 %collective-permute-start.45 = (bf16[128,1536]{1,0:T(8,128)(2,1)S(1)}, bf16[128,1536]{1,0:T(8,128)(2,1)S(1)}, u32[]{:S(2)}, u32[]{:S(2)}) collective-permute-start(bf16[128,1536]{1,0:T(8,128)(2,1)S(1)} %collective-permute-done.44.refs_0_), channel_id=1, source_target_pairs={{0,8},{4,20},{8,24},{12,4},{24,16},{28,12},{16,0},{20,28},{1,9},{5... | collective-permute-start | bytes 1179656 | tf_op jit(solution)/shard_map/ppermute | solution.py:436
  280.9 23.0 %collective-permute-start.48 = (bf16[128,1536]{1,0:T(8,128)(2,1)S(1)}, bf16[128,1536]{1,0:T(8,128)(2,1)S(1)}, u32[]{:S(2)}, u32[]{:S(2)}) collective-permute-start(bf16[128,1536]{1,0:T(8,128)(2,1)S(1)} %collective-permute-done.47.refs_1_.refs_5_), channel_id=1, source_target_pairs={{0,8},{4,20},{8,24},{12,4},{24,16},{28,12},{16,0},{20,28},{1,9},{5... | collective-permute-start | bytes 1179656 | tf_op jit(solution)/shard_map/ppermute | solution.py:436
  288.8 23.4 %collective-permute-start.40 = (bf16[2,2,128,128]{3,2,1,0:T(8,128)(2,1)}, bf16[2,2,128,128]{3,2,1,0:T(8,128)(2,1)S(1)}, u32[]{:S(2)}, u32[]{:S(2)}) collective-permute-start(bf16[2,2,128,128]{3,2,1,0:T(8,128)(2,1)} %get-tuple-element.127), channel_id=1, source_target_pairs={{0,1},{1,2},{2,3},{3,0},{4,5},{5,6},{6,7},{7,4},{8,9},{9,10},{10,1... | collective-permute-start | bytes 393224 | tf_op jit(solution)/shard_map/ppermute | solution.py:396
  290.5 25.2 %collective-permute-start.41 = (bf16[2,2,128,128]{3,2,1,0:T(8,128)(2,1)}, bf16[2,2,128,128]{3,2,1,0:T(8,128)(2,1)S(1)}, u32[]{:S(2)}, u32[]{:S(2)}) collective-permute-start(bf16[2,2,128,128]{3,2,1,0:T(8,128)(2,1)} %get-tuple-element.128), channel_id=1, source_target_pairs={{0,2},{1,3},{2,0},{3,1},{4,6},{5,7},{6,4},{7,5},{8,10},{9,11},{10,... | collective-permute-start | bytes 393224 | tf_op jit(solution)/shard_map/ppermute | solution.py:396
  293.1 22.7 %collective-permute-start.42 = (bf16[2,2,128,128]{3,2,1,0:T(8,128)(2,1)}, bf16[2,2,128,128]{3,2,1,0:T(8,128)(2,1)S(1)}, u32[]{:S(2)}, u32[]{:S(2)}) collective-permute-start(bf16[2,2,128,128]{3,2,1,0:T(8,128)(2,1)} %get-tuple-element.129), channel_id=1, source_target_pairs={{0,3},{1,0},{2,1},{3,2},{4,7},{5,4},{6,5},{7,6},{8,11},{9,8},{10,9... | collective-permute-start | bytes 393224 | tf_op jit(solution)/shard_map/ppermute | solution.py:396
  (90 other events, 466.9 us)
where the time goes:
time: 344 us; the launch traced here: 337 us
  Pallas kernels  172 us (50%)
  starting transfers between devices  96.1 us (28%)
  local copies, waits for them, and re-layouts  31.5 us (9%)
  waiting for transfers between devices  19.7 us (6%)
  between operations  11.4 us (3%)
  other arithmetic  6.44 us (2%)
    pallas_call x20, Pallas kernels, use(): pl.pallas_call(functools.partial(use_body, t, groups, width, bounds), gri...  91.7 us
    ppermute x38, starting transfers between devices, local(): got[r] = lax.ppermute(held[r][t], 'dp', along)  77.3 us
    pallas_call x11, Pallas kernels, pack(): pl.pallas_call(functools.partial(pack_body, groups, width, first, transfo...  45.8 us
    unnamed x110, local copies, waits for them, and re-layouts  27.7 us
    pallas_call x34, Pallas kernels, inject(): pl.pallas_call(functools.partial(inject_body, t, at, groups, width, held...  27.4 us
    ppermute x38, waiting for transfers between devices, local(): got[r] = lax.ppermute(held[r][t], 'dp', along)  13 us
    ppermute x6, starting transfers between devices, scatter(): lax.ppermute(pieces[m], 'tensor', [(z, (z + m) % n_tensor) for z in range...  9.62 us
  transfers between devices with their start and end apart: 59, of which 8 were waited for; matrix products, arithmetic and copies ran while one was open for 3% of the time, Pallas kernels for 49%

commit v1 on v0

v1 whole, which is shorter than its diff:
```python
import functools
import math

import jax
import jax.numpy as jnp
from jax import lax
from jax.experimental import pallas as pl
from jax.experimental.pallas import tpu as pltpu
from jax.sharding import PartitionSpec as P

D = 8192
FF = 28672
ROUNDS = 2
FB = 512
W = 3 * FB
VMEM = 64 * 1024 * 1024 - 256 * 1024

START = 11
NT = (((1,), (1,)), ((), ()))


def derive(gate, up, grad_hidden):
    gate_f = gate.astype(jnp.float32)
    up_f = up.astype(jnp.float32)
    grad_f = grad_hidden.astype(jnp.float32)
    sigmoid_gate = jax.nn.sigmoid(gate_f)
    activated = gate_f * sigmoid_gate
    hidden = (activated * up_f).astype(jnp.bfloat16)
    grad_gate = (grad_f * up_f * sigmoid_gate * (1.0 + gate_f * (1.0 - sigmoid_gate))).astype(
        jnp.bfloat16
    )
    grad_up = (grad_f * activated).astype(jnp.bfloat16)
    return (grad_gate, grad_up, hidden)


def segment_of(lengths, total):
    bounds = jnp.cumsum(lengths)
    position = jnp.arange(total, dtype=jnp.int32)
    return jnp.sum((position[:, None] >= bounds[None, :]).astype(jnp.int32), axis=1)


def segments(j, width):
    out = []
    for which in (0, 1):
        lo = max(j * W, which * width)
        hi = min((j + 1) * W, (which + 1) * width)
        if hi > lo:
            out.append((which, lo - which * width, lo - j * W, hi - lo))
    return out


ANYWHERE = pl.BlockSpec(memory_space=pl.ANY)
IN_HBM = pl.BlockSpec(memory_space=pltpu.HBM)
IN_SMEM = pl.BlockSpec(memory_space=pltpu.SMEM)
MARK = jax.ShapeDtypeStruct((8, 128), jnp.float32)


def place_of(chip, chips):
    return jnp.where(chip < chips // 2, chip, chips // 2 + chips - 1 - chip)


def away_of(me, owner, chips):
    behind = place_of(me // 2, chips) - place_of(owner // 2, chips)
    return lax.rem(jnp.where(me % 2 == 0, behind, -behind) + chips, chips)


def pack_body(groups, width, first, half, gate, up, dh, x, dy, *rest):
    out = rest[-2]
    k = pl.program_id(0) + first

    @pl.when(k < groups)
    def _():
        out[0, :, 0:FB] = gate[...]
        out[0, :, FB : 2 * FB] = up[...]
        out[0, :, 2 * FB : 3 * FB] = dh[...]

    for j in range(-(-2 * width // W)):

        @pl.when(k == groups + j)
        def _():
            end = 0
            for which, src, dst, cols in segments(j, width):
                out[0, :, dst : dst + cols] = (x, dy)[which][:, src : src + cols]
                end = dst + cols
            if end < W:
                out[0, :, end:W] = jnp.zeros((out.shape[1], W - end), out.dtype)


def pack(half, rows, first, count, deps, *arrays):
    groups, width = arrays[0].shape[1] // FB, arrays[3].shape[1]
    wide = pl.BlockSpec(
        (rows, FB), lambda k, half: (half[0], jnp.minimum(k + first, groups - 1))
    )
    flat = pl.BlockSpec((rows, width), lambda k, half: (half[0], 0))
    return pl.pallas_call(
        functools.partial(pack_body, groups, width, first),
        grid_spec=pltpu.PrefetchScalarGridSpec(
            num_scalar_prefetch=1,
            grid=(count,),
            in_specs=[wide, wide, wide, flat, flat] + [ANYWHERE] * len(deps),
            out_specs=[pl.BlockSpec((1, rows, W), lambda k, half: (k, 0, 0)), IN_HBM],
        ),
        out_shape=[jax.ShapeDtypeStruct((count, rows, W), jnp.bfloat16), MARK],
        cost_estimate=pl.CostEstimate(
            flops=0, bytes_accessed=4 * count * rows * W, transcendentals=0
        ),
        compiler_params=pltpu.CompilerParams(vmem_limit_bytes=VMEM),
    )(half, *arrays, *deps)


def inject_body(t, at, r, groups, width, n_dp, always, owner, gate, up, dh, x, dy, sib, *rest):
    out, room, sem = rest[-3:]
    rows = out.shape[0]
    me = lax.axis_index("dp")
    start = pl.multiple_of(me % 2 * rows, rows)
    mine = owner[r] % 2 == me % 2
    first = jnp.logical_or(always, owner[r] // 2 == me // 2)

    if t < groups:
        parts = [(ref, t * FB, i * FB, FB) for i, ref in enumerate((gate, up, dh))]
    else:
        parts = [
            ((x, dy)[which], src, dst, cols)
            for which, src, dst, cols in segments(t - groups, width)
        ]

    def through(sources):
        ins, outs = [], []
        for i, (source, dst, cols) in enumerate(sources):
            ins.append(pltpu.make_async_copy(source, room.at[:, pl.ds(dst, cols)], sem.at[0, i]))
            outs.append(
                pltpu.make_async_copy(
                    room.at[:, pl.ds(dst, cols)], out.at[:, pl.ds(dst, cols)], sem.at[1, i]
                )
            )
        for copy in ins:
            copy.start()
        for before, copy in zip(ins, outs):
            before.wait()
            copy.start()
        for copy in outs:
            copy.wait()

    @pl.when(first)
    def _():
        @pl.when(mine)
        def _():
            through(
                [(ref.at[pl.ds(start, rows), pl.ds(src, cols)], dst, cols) for ref, src, dst, cols in parts]
            )

        @pl.when(jnp.logical_not(mine))
        def _():
            through([(sib.at[at, :, pl.ds(i * FB, FB)], i * FB, FB) for i in range(3)])


def inject(t, at, r, rows, n_dp, owner, vals, sib, held, deps):
    groups, width = vals[0].shape[1] // FB, vals[3].shape[1]
    extra = ([] if held is None else [held]) + list(deps)
    return pl.pallas_call(
        functools.partial(inject_body, t, at, r, groups, width, n_dp, held is None),
        in_specs=[IN_SMEM]
        + [IN_HBM] * (6 if held is None else 7)
        + [ANYWHERE] * len(deps),
        out_specs=IN_HBM,
        out_shape=jax.ShapeDtypeStruct((rows, W), jnp.bfloat16),
        scratch_shapes=[pltpu.VMEM((rows, W), jnp.bfloat16), pltpu.SemaphoreType.DMA((2, 3))],
        input_output_aliases={} if held is None else {7: 0},
        cost_estimate=pl.CostEstimate(
            flops=0, bytes_accessed=4 * rows * W, transcendentals=0
        ),
        compiler_params=pltpu.CompilerParams(vmem_limit_bytes=VMEM),
    )(owner, *vals, sib, *extra)


def use_body(k, groups, width, chips, fresh, owner, own, sib, held, accs_in, accs, room, val, sums, sem):
    rows = room.shape[1]
    half = val.shape[0] // ROUNDS
    me = lax.axis_index("dp")
    brought = []
    for r in range(ROUNDS):
        away = away_of(me, owner[r], chips)
        there = val.at[pl.ds(r * half, half)]
        for i in range(chips):

            @pl.when(away == i)
            def _():
                pltpu.make_async_copy(held[r * chips + i], there, sem.at[r]).start()

        brought.append(pltpu.make_async_copy(held[r * chips], there, sem.at[r]))
    if k < groups:
        parts = [(i, k * FB, i * FB, FB) for i in range(3)]
    else:
        parts = [(3 + which, src, dst, cols) for which, src, dst, cols in segments(k - groups, width)]
    loads = []
    for side, arrays in enumerate((own, sib)):
        loads.append([])
        for i, (which, src, dst, cols) in enumerate(parts):
            copy = pltpu.make_async_copy(
                arrays[which].at[:, pl.ds(src, cols)],
                room.at[side, :, pl.ds(dst, cols)],
                sem.at[2 + 3 * side + i],
            )
            copy.start()
            loads[side].append(copy)
    priors, slot = [], 0
    slots = []
    for i, acc in enumerate(accs):
        n = acc.shape[0]
        slots.append((slot, n))
        if not fresh[i]:
            copy = pltpu.make_async_copy(accs_in.pop(0), sums.at[pl.ds(slot, n)], sem.at[8 + i])
            copy.start()
            priors.append(copy)
        slot += n

    for copy in brought:
        copy.wait()
    if k < groups:
        rights = derive(val[:, 0:FB], val[:, FB : 2 * FB], val[:, 2 * FB : 3 * FB])
    for copy in priors:
        copy.wait()
    stores = []
    for side in (0, 1):
        for copy in loads[side]:
            copy.wait()
        at = pl.ds(side * rows, rows)

        def dot(left, right):
            return lax.dot_general(left, right, NT, preferred_element_type=jnp.float32)

        if k < groups:
            lefts = derive(*(room[side, :, i * FB : (i + 1) * FB] for i in range(3)))
            terms = [
                dot(lefts[0], rights[0]) + dot(lefts[1], rights[1]),
                dot(lefts[2], rights[2]),
            ]
        else:
            terms = [
                dot(room[side, :, dst : dst + cols], val[:, dst : dst + cols])
                for _, _, dst, cols in parts
            ]
        for i, term in enumerate(terms):
            if fresh[i if len(accs) > 1 else 0]:
                sums[i, at, :] = term
            else:
                sums[i, at, :] += term
        for i, acc in enumerate(accs):
            first, n = slots[i]
            copy = pltpu.make_async_copy(
                sums.at[pl.ds(first, n), at], acc.at[:, at], sem.at[10 + 2 * side + i]
            )
            copy.start()
            stores.append(copy)
    for copy in stores:
        copy.wait()


def use(k, owner, groups, width, chips, own, sib, held, grams, deps):
    cand_rows, half = own[0].shape[0], held[0].shape[0]
    if k < groups:
        names = [("gu_h", 2)]
    else:
        names = [(("x", "dy")[which], 1) for which, _, _, _ in segments(k - groups, width)]
    fresh = [name not in grams for name, _ in names]
    priors = [grams[name] for name, _ in names if name in grams]
    shapes = [
        jax.ShapeDtypeStruct((n, 2 * cand_rows, ROUNDS * half), jnp.float32) for _, n in names
    ]
    n_cand, n_held = len(own), len(held)

    def body(owner, *refs):
        a, b = n_cand, 2 * n_cand
        c = b + n_held
        d = c + len(priors)
        e = d + len(deps)
        f = e + len(shapes)
        use_body(
            k, groups, width, chips, fresh, owner, refs[:a], refs[a:b], refs[b:c],
            list(refs[c:d]), refs[e:f], *refs[f + 1 :],
        )

    results = pl.pallas_call(
        body,
        in_specs=[IN_SMEM]
        + [IN_HBM] * (2 * n_cand + n_held + len(priors))
        + [ANYWHERE] * len(deps),
        out_specs=[IN_HBM] * (len(shapes) + 1),
        out_shape=shapes + [MARK],
        scratch_shapes=[
            pltpu.VMEM((2, cand_rows, W), jnp.bfloat16),
            pltpu.VMEM((ROUNDS * half, W), jnp.bfloat16),
            pltpu.VMEM((2, 2 * cand_rows, ROUNDS * half), jnp.float32),
            pltpu.SemaphoreType.DMA((14,)),
        ],
        cost_estimate=pl.CostEstimate(
            flops=8 * cand_rows * half * W,
            bytes_accessed=4 * (cand_rows + half) * W + 32 * cand_rows * half,
            transcendentals=2 * (cand_rows + half) * FB,
        ),
        compiler_params=pltpu.CompilerParams(vmem_limit_bytes=VMEM),
    )(owner, *own, *sib, *held, *priors, *deps)
    for (name, _), value in zip(names, results):
        grams[name] = value
    return results[-1]


def cut_body(pieces, at, acc, own, *others):
    block = own.shape[1]
    for m in range(pieces):
        rows = pl.ds(pl.multiple_of(lax.rem(at[0] + m, pieces) * block, block), block)
        tile = acc[:, rows, :]
        if m == 0:
            own[...] = tile
        else:
            others[m - 1][...] = tile.astype(jnp.bfloat16)


def cut(at_z, pieces, acc):
    shape = (acc.shape[0], acc.shape[1] // pieces, acc.shape[2])
    whole = pl.BlockSpec(shape, lambda i, at: (0, 0, 0))
    return pl.pallas_call(
        functools.partial(cut_body, pieces),
        grid_spec=pltpu.PrefetchScalarGridSpec(
            num_scalar_prefetch=1,
            grid=(1,),
            in_specs=[pl.BlockSpec(acc.shape, lambda i, at: (0, 0, 0))],
            out_specs=[whole] * pieces,
        ),
        out_shape=[jax.ShapeDtypeStruct(shape, jnp.float32)]
        + [jax.ShapeDtypeStruct(shape, jnp.bfloat16)] * (pieces - 1),
        cost_estimate=pl.CostEstimate(flops=0, bytes_accessed=8 * acc.size, transcendentals=0),
        compiler_params=pltpu.CompilerParams(vmem_limit_bytes=VMEM),
    )(at_z[None], acc)


def score_body(pieces, cand_hot, val_hot, *refs):
    out = refs[-1]

    def total(i, slot):
        value = refs[i * pieces][slot]
        for ref in refs[i * pieces + 1 : (i + 1) * pieces]:
            value = value + ref[slot].astype(jnp.float32)
        return value

    pair = total(1, 0) * total(0, 0) + total(0, 1) * total(2, 0)
    half = pair.shape[1] // ROUNDS
    summed = jnp.dot(
        cand_hot[...],
        pair,
        precision=lax.Precision.HIGHEST,
        preferred_element_type=jnp.float32,
    )
    for r in range(ROUNDS):
        out[r] = jnp.dot(
            summed[:, r * half : (r + 1) * half],
            val_hot[r],
            precision=lax.Precision.HIGHEST,
            preferred_element_type=jnp.float32,
        )


def score(cand_hot, val_hot, gu_h, x, dy):
    return pl.pallas_call(
        functools.partial(score_body, len(x)),
        out_shape=jax.ShapeDtypeStruct(
            (ROUNDS, cand_hot.shape[0], val_hot.shape[2]), jnp.float32
        ),
        compiler_params=pltpu.CompilerParams(vmem_limit_bytes=VMEM),
    )(cand_hot, val_hot, *gu_h, *x, *dy)


def local(
    n_dp,
    n_tensor,
    cand_gate,
    cand_up,
    cand_dh,
    cand_x,
    cand_dy,
    val_gate,
    val_up,
    val_dh,
    val_x,
    val_dy,
    cand_lengths,
    val_lengths,
    round_owner,
):
    chips = n_dp // 2
    ring = list(range(chips // 2)) + list(range(chips - 1, chips // 2 - 1, -1))
    along = []
    for i, chip in enumerate(ring):
        along.append((2 * chip, 2 * ring[(i + 1) % chips]))
        along.append((2 * chip + 1, 2 * ring[(i - 1) % chips] + 1))
    across = [(i, i ^ 1) for i in range(n_dp)]

    at_z = lax.axis_index("tensor")
    core = lax.axis_index("dp") % 2

    cand_rows, val_rows = cand_x.shape[0], val_x.shape[0]
    half = val_rows // 2
    groups, width = cand_gate.shape[1] // FB, cand_x.shape[1]
    count = groups + -(-2 * width // W)
    vals = (val_gate, val_up, val_dh, val_x, val_dy)
    own = (cand_gate, cand_up, cand_dh, cand_x, cand_dy)
    other = (1 - core)[None]

    sib_parts = [None] * count

    def send_half(lo, hi, deps):
        part, mark = pack(other, half, lo, hi - lo, deps, *vals)
        part = lax.ppermute(part, "dp", across)
        for t in range(lo, hi):
            sib_parts[t] = (part, t - lo)
        return mark

    mark = send_half(0, 1, [])
    mark = send_half(1, min(4, count), [mark])
    sib = [lax.ppermute(array, "dp", across) for array in own]
    sib_lengths = lax.ppermute(cand_lengths, "dp", across)

    grams, parts = {}, {}
    steps = count + chips - 1
    held = [[None] * steps for _ in range(ROUNDS)]
    got = [None] * ROUNDS

    def scatter(name):
        pieces = cut(at_z, n_tensor, grams[name])
        parts[name] = [pieces[0]] + [
            lax.ppermute(pieces[m], "tensor", [(z, (z + m) % n_tensor) for z in range(n_tensor)])
            for m in range(1, n_tensor)
        ]

    last_of = {"gu_h": groups - 1}
    for k in range(groups, count):
        for which, _, _, _ in segments(k - groups, width):
            last_of[("x", "dy")[which]] = k

    def consume(k, deps):
        came = [held[r][k + i] for r in range(ROUNDS) for i in range(chips)]
        mark = use(k, round_owner, groups, width, chips, own, sib, came, grams, deps)
        for name in last_of:
            if last_of[name] == k:
                scatter(name)
        return mark

    work = []
    cuts = [c for c in (4, 8, 12) if c < count] + [count]
    for lo, hi in zip(cuts[:-1], cuts[1:]):
        work.append((0, functools.partial(send_half, lo, hi)))
    for k in range(count):
        work.append((max((k + chips) * ROUNDS - 1, START), functools.partial(consume, k)))

    slot = 0
    for t in range(steps):
        for r in range(ROUNDS):
            if t < count:
                part, at = sib_parts[t]
                held[r][t] = inject(t, at, r, half, n_dp, round_owner, vals, part, got[r], [mark])
            else:
                held[r][t] = got[r]
            if t < steps - 1:
                got[r] = lax.ppermute(held[r][t], "dp", along)
            if work and work[0][0] <= slot:
                mark = work.pop(0)[1]([held[r][t]])
            slot += 1
    while work:
        mark = work.pop(0)[1]([mark])

    block = 2 * cand_rows // n_tensor
    samples = cand_lengths.shape[1]
    segs = jnp.concatenate(
        [
            segment_of(cand_lengths[0], cand_rows),
            segment_of(sib_lengths[0], cand_rows) + samples,
        ]
    )
    segs = lax.dynamic_slice_in_dim(segs, at_z * block, block, 0)
    cand_hot = (jnp.arange(2 * samples, dtype=jnp.int32)[:, None] == segs[None, :]).astype(
        jnp.float32
    )
    hots, weights = [], []
    for r in range(ROUNDS):
        lengths = lax.dynamic_index_in_dim(val_lengths, round_owner[r], 0, keepdims=False)
        seg = lax.dynamic_slice_in_dim(segment_of(lengths, val_rows), core * half, half, 0)
        hots.append((seg[:, None] == jnp.arange(128, dtype=jnp.int32)[None, :]).astype(jnp.float32))
        weights.append(
            1.0
            / math.sqrt(D * FF)
            / jnp.sqrt(
                cand_lengths[0].astype(jnp.float32)[:, None]
                * lengths.astype(jnp.float32)[None, :]
            )
        )
    partial = score(
        cand_hot, jnp.stack(hots, axis=0), parts["gu_h"], parts["x"], parts["dy"]
    )
    total = partial[:, :samples] + lax.ppermute(partial[:, samples:], "dp", across)
    turned = [
        lax.ppermute(total, "tensor", [(z, (z + m) % n_tensor) for z in range(n_tensor)])
        for m in range(1, n_tensor)
    ]
    for piece in turned:
        total = total + piece
    return total[:, :, : val_lengths.shape[1]] * jnp.stack(weights, axis=0)


def solution(mesh):
    n_dp, n_tensor = mesh.shape["dp"], mesh.shape["tensor"]
    in_specs = (P("dp", "tensor"),) * 10 + (P("dp", None), P(), P())
    return jax.shard_map(
        functools.partial(local, n_dp, n_tensor),
        mesh=mesh,
        in_specs=in_specs,
        out_specs=P(None, "dp", None),
        check_vma=False,
    )
```

time: 344 us -> 303 us (0.88)
  waiting for transfers between devices: 19.7 us -> 67.1 us
  starting transfers between devices: 96.1 us -> 56.8 us
  local copies, waits for them, and re-layouts: 31.5 us -> 2.87 us
  Pallas kernels: 172 us -> 159 us
  between operations: 11.4 us -> 4.6 us
    ppermute x38, waiting for transfers between devices: 13 us -> 59.4 us  [local(): got[r] = lax.ppermute(held[r][t], 'dp', along)]
    ppermute x38, starting transfers between devices: 77.3 us -> 36.6 us  [local(): got[r] = lax.ppermute(held[r][t], 'dp', along)]
    unnamed x110 -> x10, local copies, waits for them, and re-layouts: 27.7 us -> 0.78 us
    pallas_call x66 -> x57, Pallas kernels: 168 us -> 153 us  [the longest x17 76.6 us: use(): pl.pallas_call(body, in_specs=[IN_SMEM] + [IN_HBM] * (2 * n_cand + n_held...]
    ppermute x6 -> x9, starting transfers between devices: 9.62 us -> 14.3 us  [scatter(): lax.ppermute(pieces[m], 'tensor', [(z, (z + m) % n_tensor) for z in range...]
    ppermute x6 -> x9, waiting for transfers between devices: 5.07 us -> 1.37 us  [scatter(): lax.ppermute(pieces[m], 'tensor', [(z, (z + m) % n_tensor) for z in range...]
  transfers between devices with their start and end apart: 59 -> 62, of which waited for: 8 -> 30; matrix products, arithmetic and copies ran while one was open for 3% -> 3% of each run, Pallas kernels for 49% -> 50%
where the time goes in v1:
time: 303 us; the launch traced here: 299 us
  Pallas kernels  159 us (52%)
  waiting for transfers between devices  67.1 us (22%)
  starting transfers between devices  56.8 us (19%)
  other arithmetic  8.93 us (3%)
  between operations  4.6 us (2%)
    pallas_call x17, Pallas kernels, use(): pl.pallas_call(body, in_specs=[IN_SMEM] + [IN_HBM] * (2 * n_cand + n_held...  76.6 us
    ppermute x38, waiting for transfers between devices, local(): got[r] = lax.ppermute(held[r][t], 'dp', along)  59.4 us
    pallas_call x34, Pallas kernels, inject(): pl.pallas_call(functools.partial(inject_body, t, at, r, groups, width, n_...  56.1 us
    ppermute x38, starting transfers between devices, local(): got[r] = lax.ppermute(held[r][t], 'dp', along)  36.6 us
    pallas_call x5, Pallas kernels, pack(): pl.pallas_call(functools.partial(pack_body, groups, width, first), grid_s...  17.9 us
    ppermute x9, starting transfers between devices, scatter(): lax.ppermute(pieces[m], 'tensor', [(z, (z + m) % n_tensor) for z in range...  14.3 us
  transfers between devices with their start and end apart: 62, of which 30 were waited for; matrix products, arithmetic and copies ran while one was open for 3% of the time, Pallas kernels for 50%

profile of v1, /device:TPU:0, one launch (start us, length us, event | category | flops | bytes accessed | tf_op | source)
XLA Modules:
  0.0 299.1 jit_solution(7977800379630138882)
XLA Ops:
  15.0 4.1 %shard_map.130 = (bf16[4,128,1536]{2,1,0:T(8,128)(2,1)}, f32[8,128]{1,0:T(8,128)}) custom-call(s32[1]{0:T(128)} %bitcast.11.half, bf16[256,7168]{1,0:T(8,128)(2,1)} %gate.77, bf16[256,7168]{1,0:T(8,128)(2,1)} %up.77, bf16[256,7168]{1,0:T(8,128)(2,1)} %dh.77, bf16[256,2048]{1,0:T(8,128)(2,1)} %x.77, bf16[256,2048]{1,0:T(8,128)(2,1)} %dy.77, ...), custom_call_target="tpu_custom_call" | custom-call | bytes 3145728 | tf_op jit(solution)/shard_map/pallas_call | solution.py:95
  23.6 4.1 %shard_map.132 = (bf16[4,128,1536]{2,1,0:T(8,128)(2,1)}, f32[8,128]{1,0:T(8,128)}) custom-call(s32[1]{0:T(128)} %bitcast.11.half, bf16[256,7168]{1,0:T(8,128)(2,1)} %gate.77, bf16[256,7168]{1,0:T(8,128)(2,1)} %up.77, bf16[256,7168]{1,0:T(8,128)(2,1)} %dh.77, bf16[256,2048]{1,0:T(8,128)(2,1)} %x.77, bf16[256,2048]{1,0:T(8,128)(2,1)} %dy.77, ...), custom_call_target="tpu_custom_call" | custom-call | bytes 3145728 | tf_op jit(solution)/shard_map/pallas_call | solution.py:95
  40.0 5.8 %collective-permute-done.18.rest_0_ = bf16[128,1536]{1,0:T(8,128)(2,1)} collective-permute-done((bf16[128,1536]{1,0:T(8,128)(2,1)}, bf16[128,1536]{1,0:T(8,128)(2,1)}, u32[]{:S(2)}, u32[]{:S(2)}) %collective-permute-start.18) | collective-permute-done | bytes 393248 | tf_op jit(solution)/shard_map/ppermute | solution.py:464
  49.9 4.1 %collective-permute-done.13.rest_0_ = bf16[128,1536]{1,0:T(8,128)(2,1)} collective-permute-done((bf16[128,1536]{1,0:T(8,128)(2,1)}, bf16[128,1536]{1,0:T(8,128)(2,1)}, u32[]{:S(2)}, u32[]{:S(2)}) %collective-permute-start.13) | collective-permute-done | bytes 393248 | tf_op jit(solution)/shard_map/ppermute | solution.py:464
  56.2 5.8 %collective-permute-done.19.rest_0_ = bf16[128,1536]{1,0:T(8,128)(2,1)} collective-permute-done((bf16[128,1536]{1,0:T(8,128)(2,1)}, bf16[128,1536]{1,0:T(8,128)(2,1)}, u32[]{:S(2)}, u32[]{:S(2)}) %collective-permute-start.19) | collective-permute-done | bytes 393248 | tf_op jit(solution)/shard_map/ppermute | solution.py:464
  66.0 4.1 %collective-permute-done.14.rest_0_ = bf16[128,1536]{1,0:T(8,128)(2,1)} collective-permute-done((bf16[128,1536]{1,0:T(8,128)(2,1)}, bf16[128,1536]{1,0:T(8,128)(2,1)}, u32[]{:S(2)}, u32[]{:S(2)}) %collective-permute-start.14) | collective-permute-done | bytes 393248 | tf_op jit(solution)/shard_map/ppermute | solution.py:464
  72.4 5.8 %collective-permute-done.20.rest_0_ = bf16[128,1536]{1,0:T(8,128)(2,1)} collective-permute-done((bf16[128,1536]{1,0:T(8,128)(2,1)}, bf16[128,1536]{1,0:T(8,128)(2,1)}, u32[]{:S(2)}, u32[]{:S(2)}) %collective-permute-start.20) | collective-permute-done | bytes 393248 | tf_op jit(solution)/shard_map/ppermute | solution.py:464
  94.6 4.3 %shard_map.144 = (f32[2,512,256]{2,1,0:T(8,128)}, f32[8,128]{1,0:T(8,128)}) custom-call(s32[2]{0:T(128)} %owner.101, bf16[256,7168]{1,0:T(8,128)(2,1)} %refs_0_.33, bf16[256,7168]{1,0:T(8,128)(2,1)} %refs_1_.33, bf16[256,7168]{1,0:T(8,128)(2,1)} %refs_2_.33, bf16[256,2048]{1,0:T(8,128)(2,1)} %refs_3_.33, bf16[256,2048]{1,0:T(8,128)(2,1)} %refs_4_.33, ...), custom_call_target="tpu_custom_call" | custom-call | flops 402653184 | bytes 3407872 | tf_op jit(solution)/shard_map/pallas_call | solution.py:283
  102.6 4.6 %shard_map.146 = (f32[2,512,256]{2,1,0:T(8,128)}, f32[8,128]{1,0:T(8,128)}) custom-call(s32[2]{0:T(128)} %owner.101, bf16[256,7168]{1,0:T(8,128)(2,1)} %refs_0_.33, bf16[256,7168]{1,0:T(8,128)(2,1)} %refs_1_.33, bf16[256,7168]{1,0:T(8,128)(2,1)} %refs_2_.33, bf16[256,2048]{1,0:T(8,128)(2,1)} %refs_3_.33, bf16[256,2048]{1,0:T(8,128)(2,1)} %refs_4_.33, ...), custom_call_target="tpu_custom_call" | custom-call | flops 402653184 | bytes 3407872 | tf_op jit(solution)/shard_map/pallas_call | solution.py:283
  109.8 4.6 %shard_map.148 = (f32[2,512,256]{2,1,0:T(8,128)}, f32[8,128]{1,0:T(8,128)}) custom-call(s32[2]{0:T(128)} %owner.101, bf16[256,7168]{1,0:T(8,128)(2,1)} %refs_0_.33, bf16[256,7168]{1,0:T(8,128)(2,1)} %refs_1_.33, bf16[256,7168]{1,0:T(8,128)(2,1)} %refs_2_.33, bf16[256,2048]{1,0:T(8,128)(2,1)} %refs_3_.33, bf16[256,2048]{1,0:T(8,128)(2,1)} %refs_4_.33, ...), custom_call_target="tpu_custom_call" | custom-call | flops 402653184 | bytes 3407872 | tf_op jit(solution)/shard_map/pallas_call | solution.py:283
  115.1 4.6 %shard_map.150 = (f32[2,512,256]{2,1,0:T(8,128)}, f32[8,128]{1,0:T(8,128)}) custom-call(s32[2]{0:T(128)} %owner.101, bf16[256,7168]{1,0:T(8,128)(2,1)} %refs_0_.33, bf16[256,7168]{1,0:T(8,128)(2,1)} %refs_1_.33, bf16[256,7168]{1,0:T(8,128)(2,1)} %refs_2_.33, bf16[256,2048]{1,0:T(8,128)(2,1)} %refs_3_.33, bf16[256,2048]{1,0:T(8,128)(2,1)} %refs_4_.33, ...), custom_call_target="tpu_custom_call" | custom-call | flops 402653184 | bytes 3407872 | tf_op jit(solution)/shard_map/pallas_call | solution.py:283
  122.6 4.6 %shard_map.152 = (f32[2,512,256]{2,1,0:T(8,128)}, f32[8,128]{1,0:T(8,128)}) custom-call(s32[2]{0:T(128)} %owner.101, bf16[256,7168]{1,0:T(8,128)(2,1)} %refs_0_.33, bf16[256,7168]{1,0:T(8,128)(2,1)} %refs_1_.33, bf16[256,7168]{1,0:T(8,128)(2,1)} %refs_2_.33, bf16[256,2048]{1,0:T(8,128)(2,1)} %refs_3_.33, bf16[256,2048]{1,0:T(8,128)(2,1)} %refs_4_.33, ...), custom_call_target="tpu_custom_call" | custom-call | flops 402653184 | bytes 3407872 | tf_op jit(solution)/shard_map/pallas_call | solution.py:283
  137.1 4.6 %shard_map.155 = (f32[2,512,256]{2,1,0:T(8,128)}, f32[8,128]{1,0:T(8,128)}) custom-call(s32[2]{0:T(128)} %owner.101, bf16[256,7168]{1,0:T(8,128)(2,1)} %refs_0_.33, bf16[256,7168]{1,0:T(8,128)(2,1)} %refs_1_.33, bf16[256,7168]{1,0:T(8,128)(2,1)} %refs_2_.33, bf16[256,2048]{1,0:T(8,128)(2,1)} %refs_3_.33, bf16[256,2048]{1,0:T(8,128)(2,1)} %refs_4_.33, ...), custom_call_target="tpu_custom_call" | custom-call | flops 402653184 | bytes 3407872 | tf_op jit(solution)/shard_map/pallas_call | solution.py:283
  147.7 4.6 %shard_map.158 = (f32[2,512,256]{2,1,0:T(8,128)}, f32[8,128]{1,0:T(8,128)}) custom-call(s32[2]{0:T(128)} %owner.101, bf16[256,7168]{1,0:T(8,128)(2,1)} %refs_0_.33, bf16[256,7168]{1,0:T(8,128)(2,1)} %refs_1_.33, bf16[256,7168]{1,0:T(8,128)(2,1)} %refs_2_.33, bf16[256,2048]{1,0:T(8,128)(2,1)} %refs_3_.33, bf16[256,2048]{1,0:T(8,128)(2,1)} %refs_4_.33, ...), custom_call_target="tpu_custom_call" | custom-call | flops 402653184 | bytes 3407872 | tf_op jit(solution)/shard_map/pallas_call | solution.py:283
  159.1 4.6 %shard_map.161 = (f32[2,512,256]{2,1,0:T(8,128)}, f32[8,128]{1,0:T(8,128)}) custom-call(s32[2]{0:T(128)} %owner.101, bf16[256,7168]{1,0:T(8,128)(2,1)} %refs_0_.33, bf16[256,7168]{1,0:T(8,128)(2,1)} %refs_1_.33, bf16[256,7168]{1,0:T(8,128)(2,1)} %refs_2_.33, bf16[256,2048]{1,0:T(8,128)(2,1)} %refs_3_.33, bf16[256,2048]{1,0:T(8,128)(2,1)} %refs_4_.33, ...), custom_call_target="tpu_custom_call" | custom-call | flops 402653184 | bytes 3407872 | tf_op jit(solution)/shard_map/pallas_call | solution.py:283
  169.7 4.6 %shard_map.164 = (f32[2,512,256]{2,1,0:T(8,128)}, f32[8,128]{1,0:T(8,128)}) custom-call(s32[2]{0:T(128)} %owner.101, bf16[256,7168]{1,0:T(8,128)(2,1)} %refs_0_.33, bf16[256,7168]{1,0:T(8,128)(2,1)} %refs_1_.33, bf16[256,7168]{1,0:T(8,128)(2,1)} %refs_2_.33, bf16[256,2048]{1,0:T(8,128)(2,1)} %refs_3_.33, bf16[256,2048]{1,0:T(8,128)(2,1)} %refs_4_.33, ...), custom_call_target="tpu_custom_call" | custom-call | flops 402653184 | bytes 3407872 | tf_op jit(solution)/shard_map/pallas_call | solution.py:283
  181.0 4.5 %shard_map.167 = (f32[2,512,256]{2,1,0:T(8,128)}, f32[8,128]{1,0:T(8,128)}) custom-call(s32[2]{0:T(128)} %owner.101, bf16[256,7168]{1,0:T(8,128)(2,1)} %refs_0_.33, bf16[256,7168]{1,0:T(8,128)(2,1)} %refs_1_.33, bf16[256,7168]{1,0:T(8,128)(2,1)} %refs_2_.33, bf16[256,2048]{1,0:T(8,128)(2,1)} %refs_3_.33, bf16[256,2048]{1,0:T(8,128)(2,1)} %refs_4_.33, ...), custom_call_target="tpu_custom_call" | custom-call | flops 402653184 | bytes 3407872 | tf_op jit(solution)/shard_map/pallas_call | solution.py:283
  191.9 4.6 %shard_map.170 = (f32[2,512,256]{2,1,0:T(8,128)}, f32[8,128]{1,0:T(8,128)}) custom-call(s32[2]{0:T(128)} %owner.101, bf16[256,7168]{1,0:T(8,128)(2,1)} %refs_0_.33, bf16[256,7168]{1,0:T(8,128)(2,1)} %refs_1_.33, bf16[256,7168]{1,0:T(8,128)(2,1)} %refs_2_.33, bf16[256,2048]{1,0:T(8,128)(2,1)} %refs_3_.33, bf16[256,2048]{1,0:T(8,128)(2,1)} %refs_4_.33, ...), custom_call_target="tpu_custom_call" | custom-call | flops 402653184 | bytes 3407872 | tf_op jit(solution)/shard_map/pallas_call | solution.py:283
  202.9 4.6 %shard_map.173 = (f32[2,512,256]{2,1,0:T(8,128)}, f32[8,128]{1,0:T(8,128)}) custom-call(s32[2]{0:T(128)} %owner.101, bf16[256,7168]{1,0:T(8,128)(2,1)} %refs_0_.33, bf16[256,7168]{1,0:T(8,128)(2,1)} %refs_1_.33, bf16[256,7168]{1,0:T(8,128)(2,1)} %refs_2_.33, bf16[256,2048]{1,0:T(8,128)(2,1)} %refs_3_.33, bf16[256,2048]{1,0:T(8,128)(2,1)} %refs_4_.33, ...), custom_call_target="tpu_custom_call" | custom-call | flops 402653184 | bytes 3407872 | tf_op jit(solution)/shard_map/pallas_call | solution.py:283
  213.8 4.6 %shard_map.176 = (f32[2,512,256]{2,1,0:T(8,128)}, f32[8,128]{1,0:T(8,128)}) custom-call(s32[2]{0:T(128)} %owner.101, bf16[256,7168]{1,0:T(8,128)(2,1)} %refs_0_.33, bf16[256,7168]{1,0:T(8,128)(2,1)} %refs_1_.33, bf16[256,7168]{1,0:T(8,128)(2,1)} %refs_2_.33, bf16[256,2048]{1,0:T(8,128)(2,1)} %refs_3_.33, bf16[256,2048]{1,0:T(8,128)(2,1)} %refs_4_.33, ...), custom_call_target="tpu_custom_call" | custom-call | flops 402653184 | bytes 3407872 | tf_op jit(solution)/shard_map/pallas_call | solution.py:283
  239.5 4.1 %collective-permute-done.47.refs_13_.refs_12_ = bf16[128,1536]{1,0:T(8,128)(2,1)} collective-permute-done((bf16[128,1536]{1,0:T(8,128)(2,1)S(1)}, bf16[128,1536]{1,0:T(8,128)(2,1)}, u32[]{:S(2)}, u32[]{:S(2)}) %collective-permute-start.47) | collective-permute-done | bytes 393248 | tf_op jit(solution)/shard_map/ppermute | solution.py:464
  244.2 4.6 %shard_map.179 = (f32[2,512,256]{2,1,0:T(8,128)}, f32[8,128]{1,0:T(8,128)}) custom-call(s32[2]{0:T(128)} %owner.101, bf16[256,7168]{1,0:T(8,128)(2,1)} %refs_0_.33, bf16[256,7168]{1,0:T(8,128)(2,1)} %refs_1_.33, bf16[256,7168]{1,0:T(8,128)(2,1)} %refs_2_.33, bf16[256,2048]{1,0:T(8,128)(2,1)} %refs_3_.33, bf16[256,2048]{1,0:T(8,128)(2,1)} %refs_4_.33, ...), custom_call_target="tpu_custom_call" | custom-call | flops 402653184 | bytes 3407872 | tf_op jit(solution)/shard_map/pallas_call | solution.py:283
  256.5 4.1 %shard_map.181 = (f32[1,512,256]{2,1,0:T(8,128)}, f32[8,128]{1,0:T(8,128)}) custom-call(s32[2]{0:T(128)} %owner.101, bf16[256,7168]{1,0:T(8,128)(2,1)} %refs_0_.33, bf16[256,7168]{1,0:T(8,128)(2,1)} %refs_1_.33, bf16[256,7168]{1,0:T(8,128)(2,1)} %refs_2_.33, bf16[256,2048]{1,0:T(8,128)(2,1)} %refs_3_.33, bf16[256,2048]{1,0:T(8,128)(2,1)} %refs_4_.33, ...), custom_call_target="tpu_custom_call" | custom-call | flops 402653184 | bytes 3407872 | tf_op jit(solution)/shard_map/pallas_call | solution.py:283
  260.6 4.6 %shard_map.182 = (f32[1,512,256]{2,1,0:T(8,128)}, f32[1,512,256]{2,1,0:T(8,128)}, f32[8,128]{1,0:T(8,128)}) custom-call(s32[2]{0:T(128)} %owner.101, bf16[256,7168]{1,0:T(8,128)(2,1)} %refs_0_.33, bf16[256,7168]{1,0:T(8,128)(2,1)} %refs_1_.33, bf16[256,7168]{1,0:T(8,128)(2,1)} %refs_2_.33, bf16[256,2048]{1,0:T(8,128)(2,1)} %refs_3_.33, ...), custom_call_target="tpu_custom_call" | custom-call | flops 402653184 | bytes 3407872 | tf_op jit(solution)/shard_map/pallas_call | solution.py:283
  (193 shorter events, 184.0 us)
Async XLA Ops:
  5.8 17.3 %collective-permute-start.6 = (bf16[3,128,1536]{2,1,0:T(8,128)(2,1)}, bf16[3,128,1536]{2,1,0:T(8,128)(2,1)}, u32[]{:S(2)}, u32[]{:S(2)}) collective-permute-start(bf16[3,128,1536]{2,1,0:T(8,128)(2,1)} %get-tuple-element.59), channel_id=1, source_target_pairs={{0,4},{4,0},{8,12},{12,8},{16,20},{20,16},{24,28},{28,24},{1,5},{5... | collective-permute-start | bytes 3538952 | tf_op jit(solution)/shard_map/ppermute | solution.py:413
  6.3 24.9 %collective-permute-start.4 = (bf16[256,2048]{1,0:T(8,128)(2,1)}, bf16[256,2048]{1,0:T(8,128)(2,1)}, u32[]{:S(2)}, u32[]{:S(2)}) collective-permute-start(bf16[256,2048]{1,0:T(8,128)(2,1)} %refs_3_.33), channel_id=1, source_target_pairs={{0,4},{4,0},{8,12},{12,8},{16,20},{20,16},{24,28},{28,24},{1,5},{5... | collective-permute-start | bytes 3145736 | tf_op jit(solution)/shard_map/ppermute | solution.py:420
  12.0 11.1 %collective-permute-start.8 = (bf16[128,1536]{1,0:T(8,128)(2,1)}, bf16[128,1536]{1,0:T(8,128)(2,1)}, u32[]{:S(2)}, u32[]{:S(2)}) collective-permute-start(bf16[128,1536]{1,0:T(8,128)(2,1)} %shard_map.129.rest_0_.refs_10_), channel_id=1, source_target_pairs={{0,8},{4,20},{8,24},{12,4},{24,16},{28,12},{16,0},{20,28},{1,9},{5... | collective-permute-start | bytes 1179656 | tf_op jit(solution)/shard_map/ppermute | solution.py:464
  15.0 79.5 %collective-permute-start.1 = (bf16[256,7168]{1,0:T(8,128)(2,1)}, bf16[256,7168]{1,0:T(8,128)(2,1)}, u32[]{:S(2)}, u32[]{:S(2)}) collective-permute-start(bf16[256,7168]{1,0:T(8,128)(2,1)} %refs_0_.33), channel_id=1, source_target_pairs={{0,4},{4,0},{8,12},{12,8},{16,20},{20,16},{24,28},{28,24},{1,5},{5... | collective-permute-start | bytes 11010056 | tf_op jit(solution)/shard_map/ppermute | solution.py:420
  23.1 71.5 %collective-permute-start.2 = (bf16[256,7168]{1,0:T(8,128)(2,1)}, bf16[256,7168]{1,0:T(8,128)(2,1)}, u32[]{:S(2)}, u32[]{:S(2)}) collective-permute-start(bf16[256,7168]{1,0:T(8,128)(2,1)} %refs_1_.33), channel_id=1, source_target_pairs={{0,4},{4,0},{8,12},{12,8},{16,20},{20,16},{24,28},{28,24},{1,5},{5... | collective-permute-start | bytes 11010056 | tf_op jit(solution)/shard_map/ppermute | solution.py:420
  23.1 71.5 %collective-permute-start.3 = (bf16[256,7168]{1,0:T(8,128)(2,1)}, bf16[256,7168]{1,0:T(8,128)(2,1)}, u32[]{:S(2)}, u32[]{:S(2)}) collective-permute-start(bf16[256,7168]{1,0:T(8,128)(2,1)} %refs_2_.33), channel_id=1, source_target_pairs={{0,4},{4,0},{8,12},{12,8},{16,20},{20,16},{24,28},{28,24},{1,5},{5... | collective-permute-start | bytes 11010056 | tf_op jit(solution)/shard_map/ppermute | solution.py:420
  31.2 32.4 %collective-permute-start.11 = (bf16[4,128,1536]{2,1,0:T(8,128)(2,1)}, bf16[4,128,1536]{2,1,0:T(8,128)(2,1)}, u32[]{:S(2)}, u32[]{:S(2)}) collective-permute-start(bf16[4,128,1536]{2,1,0:T(8,128)(2,1)} %get-tuple-element.66), channel_id=1, source_target_pairs={{0,4},{4,0},{8,12},{12,8},{16,20},{20,16},{24,28},{28,24},{1,5},{5... | collective-permute-start | bytes 4718600 | tf_op jit(solution)/shard_map/ppermute | solution.py:413
  63.6 18.7 %collective-permute-start.5 = (bf16[256,2048]{1,0:T(8,128)(2,1)}, bf16[256,2048]{1,0:T(8,128)(2,1)}, u32[]{:S(2)}, u32[]{:S(2)}) collective-permute-start(bf16[256,2048]{1,0:T(8,128)(2,1)} %refs_4_.33), channel_id=1, source_target_pairs={{0,4},{4,0},{8,12},{12,8},{16,20},{20,16},{24,28},{28,24},{1,5},{5... | collective-permute-start | bytes 3145736 | tf_op jit(solution)/shard_map/ppermute | solution.py:420
  86.3 40.9 %collective-permute-start.10 = (bf16[4,128,1536]{2,1,0:T(8,128)(2,1)}, bf16[4,128,1536]{2,1,0:T(8,128)(2,1)}, u32[]{:S(2)}, u32[]{:S(2)}) collective-permute-start(bf16[4,128,1536]{2,1,0:T(8,128)(2,1)} %get-tuple-element.65), channel_id=1, source_target_pairs={{0,4},{4,0},{8,12},{12,8},{16,20},{20,16},{24,28},{28,24},{1,5},{5... | collective-permute-start | bytes 4718600 | tf_op jit(solution)/shard_map/ppermute | solution.py:413
  94.5 12.7 %collective-permute-start.23 = (bf16[128,1536]{1,0:T(8,128)(2,1)}, bf16[128,1536]{1,0:T(8,128)(2,1)}, u32[]{:S(2)}, u32[]{:S(2)}) collective-permute-start(bf16[128,1536]{1,0:T(8,128)(2,1)} %shard_map.143.refs_18_.refs_17_.refs_16_.refs_15_.refs_14_), channel_id=1, source_target_pairs={{0,8},{4,20},{8,24},{12,4},{24,16},{28,12},{16,0},{20,28},{1,9},{5... | collective-permute-start | bytes 1179656 | tf_op jit(solution)/shard_map/ppermute | solution.py:464
  99.7 14.7 %collective-permute-start.22 = (bf16[128,1536]{1,0:T(8,128)(2,1)}, bf16[128,1536]{1,0:T(8,128)(2,1)}, u32[]{:S(2)}, u32[]{:S(2)}) collective-permute-start(bf16[128,1536]{1,0:T(8,128)(2,1)} %shard_map.145.refs_19_.refs_13_.refs_12_.refs_11_.refs_10_), channel_id=1, source_target_pairs={{0,8},{4,20},{8,24},{12,4},{24,16},{28,12},{16,0},{20,28},{1,9},{5... | collective-permute-start | bytes 1179656 | tf_op jit(solution)/shard_map/ppermute | solution.py:464
  122.3 52.0 %collective-permute-start.9 = (bf16[5,128,1536]{2,1,0:T(8,128)(2,1)}, bf16[5,128,1536]{2,1,0:T(8,128)(2,1)}, u32[]{:S(2)}, u32[]{:S(2)}) collective-permute-start(bf16[5,128,1536]{2,1,0:T(8,128)(2,1)} %get-tuple-element.64), channel_id=1, source_target_pairs={{0,4},{4,0},{8,12},{12,8},{16,20},{20,16},{24,28},{28,24},{1,5},{5... | collective-permute-start | bytes 5898248 | tf_op jit(solution)/shard_map/ppermute | solution.py:413
  122.4 12.2 %collective-permute-start.24 = (bf16[128,1536]{1,0:T(8,128)(2,1)}, bf16[128,1536]{1,0:T(8,128)(2,1)}, u32[]{:S(2)}, u32[]{:S(2)}) collective-permute-start(bf16[128,1536]{1,0:T(8,128)(2,1)} %shard_map.149.refs_19_.refs_13_.refs_12_.refs_11_.refs_10_), channel_id=1, source_target_pairs={{0,8},{4,20},{8,24},{12,4},{24,16},{28,12},{16,0},{20,28},{1,9},{5... | collective-permute-start | bytes 1179656 | tf_op jit(solution)/shard_map/ppermute | solution.py:464
  145.9 10.6 %collective-permute-start.28 = (bf16[128,1536]{1,0:T(8,128)(2,1)}, bf16[128,1536]{1,0:T(8,128)(2,1)}, u32[]{:S(2)}, u32[]{:S(2)}) collective-permute-start(bf16[128,1536]{1,0:T(8,128)(2,1)} %shard_map.156.refs_13_.refs_12_.refs_11_.refs_10_), channel_id=1, source_target_pairs={{0,8},{4,20},{8,24},{12,4},{24,16},{28,12},{16,0},{20,28},{1,9},{5... | collective-permute-start | bytes 1179656 | tf_op jit(solution)/shard_map/ppermute | solution.py:464
  167.9 10.6 %collective-permute-start.32 = (bf16[128,1536]{1,0:T(8,128)(2,1)}, bf16[128,1536]{1,0:T(8,128)(2,1)}, u32[]{:S(2)}, u32[]{:S(2)}) collective-permute-start(bf16[128,1536]{1,0:T(8,128)(2,1)} %shard_map.162.refs_13_.refs_12_.refs_11_.refs_10_), channel_id=1, source_target_pairs={{0,8},{4,20},{8,24},{12,4},{24,16},{28,12},{16,0},{20,28},{1,9},{5... | collective-permute-start | bytes 1179656 | tf_op jit(solution)/shard_map/ppermute | solution.py:464
  213.8 21.7 %collective-permute-start = (s32[1,8]{1,0:T(1,128)S(1)}, s32[1,8]{1,0:T(1,128)S(1)}, u32[]{:S(2)}, u32[]{:S(2)}) collective-permute-start(s32[1,8]{1,0:T(1,128)S(1)} %copy-done.4), channel_id=1, source_target_pairs={{0,4},{4,0},{8,12},{12,8},{16,20},{20,16},{24,28},{28,24},{1,5},{5... | collective-permute-start | bytes 104 | tf_op jit(solution)/shard_map/ppermute | solution.py:421
  220.8 10.5 %collective-permute-start.48 = (bf16[128,1536]{1,0:T(8,128)(2,1)}, bf16[128,1536]{1,0:T(8,128)(2,1)}, u32[]{:S(2)}, u32[]{:S(2)}) collective-permute-start(bf16[128,1536]{1,0:T(8,128)(2,1)} %shard_map.178.refs_17_.refs_19_.refs_16_.refs_15_.refs_14_), channel_id=1, source_target_pairs={{0,8},{4,20},{8,24},{12,4},{24,16},{28,12},{16,0},{20,28},{1,9},{5... | collective-permute-start | bytes 1179656 | tf_op jit(solution)/shard_map/ppermute | solution.py:464
  239.4 27.5 %collective-permute-start.54 = (bf16[128,1536]{1,0:T(8,128)(2,1)}, bf16[128,1536]{1,0:T(8,128)(2,1)}, u32[]{:S(2)}, u32[]{:S(2)}) collective-permute-start(bf16[128,1536]{1,0:T(8,128)(2,1)} %collective-permute-done.49.refs_17_.refs_19_.refs_16_), channel_id=1, source_target_pairs={{0,8},{4,20},{8,24},{12,4},{24,16},{28,12},{16,0},{20,28},{1,9},{5... | collective-permute-start | bytes 1179656 | tf_op jit(solution)/shard_map/ppermute | solution.py:464
  243.6 25.2 %collective-permute-start.53 = (bf16[128,1536]{1,0:T(8,128)(2,1)}, bf16[128,1536]{1,0:T(8,128)(2,1)}, u32[]{:S(2)}, u32[]{:S(2)}) collective-permute-start(bf16[128,1536]{1,0:T(8,128)(2,1)} %collective-permute-done.47.refs_13_.refs_12_), channel_id=1, source_target_pairs={{0,8},{4,20},{8,24},{12,4},{24,16},{28,12},{16,0},{20,28},{1,9},{5... | collective-permute-start | bytes 1179656 | tf_op jit(solution)/shard_map/ppermute | solution.py:464
  251.0 24.1 %collective-permute-start.43 = (bf16[2,128,256]{2,1,0:T(8,128)(2,1)}, bf16[2,128,256]{2,1,0:T(8,128)(2,1)S(1)}, u32[]{:S(2)}, u32[]{:S(2)}) collective-permute-start(bf16[2,128,256]{2,1,0:T(8,128)(2,1)} %get-tuple-element.96), channel_id=1, source_target_pairs={{0,1},{1,2},{2,3},{3,0},{4,5},{5,6},{6,7},{7,4},{8,9},{9,10},{10,1... | collective-permute-start | bytes 393224 | tf_op jit(solution)/shard_map/ppermute | solution.py:431
  252.5 25.4 %collective-permute-start.44 = (bf16[2,128,256]{2,1,0:T(8,128)(2,1)}, bf16[2,128,256]{2,1,0:T(8,128)(2,1)}, u32[]{:S(2)}, u32[]{:S(2)}) collective-permute-start(bf16[2,128,256]{2,1,0:T(8,128)(2,1)} %get-tuple-element.97), channel_id=1, source_target_pairs={{0,2},{1,3},{2,0},{3,1},{4,6},{5,7},{6,4},{7,5},{8,10},{9,11},{10,... | collective-permute-start | bytes 393224 | tf_op jit(solution)/shard_map/ppermute | solution.py:431
  255.1 23.4 %collective-permute-start.45 = (bf16[2,128,256]{2,1,0:T(8,128)(2,1)}, bf16[2,128,256]{2,1,0:T(8,128)(2,1)}, u32[]{:S(2)}, u32[]{:S(2)}) collective-permute-start(bf16[2,128,256]{2,1,0:T(8,128)(2,1)} %get-tuple-element.98), channel_id=1, source_target_pairs={{0,3},{1,0},{2,1},{3,2},{4,7},{5,4},{6,5},{7,6},{8,11},{9,8},{10,9... | collective-permute-start | bytes 393224 | tf_op jit(solution)/shard_map/ppermute | solution.py:431
  266.9 13.1 %collective-permute-start.50 = (bf16[1,128,256]{2,1,0:T(8,128)(2,1)}, bf16[1,128,256]{2,1,0:T(8,128)(2,1)S(1)}, u32[]{:S(2)}, u32[]{:S(2)}) collective-permute-start(bf16[1,128,256]{2,1,0:T(8,128)(2,1)} %get-tuple-element.102), channel_id=1, source_target_pairs={{0,1},{1,2},{2,3},{3,0},{4,5},{5,6},{6,7},{7,4},{8,9},{9,10},{10,1... | collective-permute-start | bytes 196616 | tf_op jit(solution)/shard_map/ppermute | solution.py:431
  268.9 15.2 %collective-permute-start.51 = (bf16[1,128,256]{2,1,0:T(8,128)(2,1)}, bf16[1,128,256]{2,1,0:T(8,128)(2,1)}, u32[]{:S(2)}, u32[]{:S(2)}) collective-permute-start(bf16[1,128,256]{2,1,0:T(8,128)(2,1)} %get-tuple-element.103), channel_id=1, source_target_pairs={{0,2},{1,3},{2,0},{3,1},{4,6},{5,7},{6,4},{7,5},{8,10},{9,11},{10,... | collective-permute-start | bytes 196616 | tf_op jit(solution)/shard_map/ppermute | solution.py:431
  (43 other events, 326.8 us)

commit v2 on v1

--- a/solution.py
+++ b/solution.py
@@ -11,11 +11,10 @@
 D = 8192
 FF = 28672
 ROUNDS = 2
-FB = 512
+FB = 896
 W = 3 * FB
 VMEM = 64 * 1024 * 1024 - 256 * 1024
 
-START = 11
 NT = (((1,), (1,)), ((), ()))
 
 
@@ -111,6 +110,8 @@
 def inject_body(t, at, r, groups, width, n_dp, always, owner, gate, up, dh, x, dy, sib, *rest):
     out, room, sem = rest[-3:]
     rows = out.shape[0]
+    if t >= groups + -(-2 * width // W):
+        return
     me = lax.axis_index("dp")
     start = pl.multiple_of(me % 2 * rows, rows)
     mine = owner[r] % 2 == me % 2
@@ -126,13 +127,17 @@
 
     def through(sources):
         ins, outs = [], []
-        for i, (source, dst, cols) in enumerate(sources):
-            ins.append(pltpu.make_async_copy(source, room.at[:, pl.ds(dst, cols)], sem.at[0, i]))
-            outs.append(
-                pltpu.make_async_copy(
-                    room.at[:, pl.ds(dst, cols)], out.at[:, pl.ds(dst, cols)], sem.at[1, i]
+        half = rows // 2
+        for n in (0, 1):
+            some = pl.ds(n * half, half)
+            for source, first, src, dst, cols in sources:
+                there = room.at[some, pl.ds(dst, cols)]
+                i = len(ins)
+                here = source.at[pl.ds(first + n * half, half), pl.ds(src, cols)]
+                ins.append(pltpu.make_async_copy(here, there, sem.at[0, i]))
+                outs.append(
+                    pltpu.make_async_copy(there, out.at[some, pl.ds(dst, cols)], sem.at[1, i])
                 )
-            )
         for copy in ins:
             copy.start()
         for before, copy in zip(ins, outs):
@@ -145,13 +150,11 @@
     def _():
         @pl.when(mine)
         def _():
-            through(
-                [(ref.at[pl.ds(start, rows), pl.ds(src, cols)], dst, cols) for ref, src, dst, cols in parts]
-            )
+            through([(ref, start, src, dst, cols) for ref, src, dst, cols in parts])
 
         @pl.when(jnp.logical_not(mine))
         def _():
-            through([(sib.at[at, :, pl.ds(i * FB, FB)], i * FB, FB) for i in range(3)])
+            through([(sib.at[at], 0, dst, dst, cols) for _, _, dst, cols in parts])
 
 
 def inject(t, at, r, rows, n_dp, owner, vals, sib, held, deps):
@@ -164,7 +167,7 @@
         + [ANYWHERE] * len(deps),
         out_specs=IN_HBM,
         out_shape=jax.ShapeDtypeStruct((rows, W), jnp.bfloat16),
-        scratch_shapes=[pltpu.VMEM((rows, W), jnp.bfloat16), pltpu.SemaphoreType.DMA((2, 3))],
+        scratch_shapes=[pltpu.VMEM((rows, W), jnp.bfloat16), pltpu.SemaphoreType.DMA((2, 6))],
         input_output_aliases={} if held is None else {7: 0},
         cost_estimate=pl.CostEstimate(
             flops=0, bytes_accessed=4 * rows * W, transcendentals=0
@@ -214,10 +217,20 @@
             priors.append(copy)
         slot += n
 
+    def derive_in(ref):
+        def some(i, carry):
+            at = [pl.ds(pl.multiple_of(m * FB + i * 128, 128), 128) for m in range(3)]
+            new = derive(ref[:, at[0]], ref[:, at[1]], ref[:, at[2]])
+            for m in range(3):
+                ref[:, at[m]] = new[m]
+            return carry
+
+        lax.fori_loop(0, FB // 128, some, 0)
+
     for copy in brought:
         copy.wait()
     if k < groups:
-        rights = derive(val[:, 0:FB], val[:, FB : 2 * FB], val[:, 2 * FB : 3 * FB])
+        derive_in(val)
     for copy in priors:
         copy.wait()
     stores = []
@@ -230,10 +243,9 @@
             return lax.dot_general(left, right, NT, preferred_element_type=jnp.float32)
 
         if k < groups:
-            lefts = derive(*(room[side, :, i * FB : (i + 1) * FB] for i in range(3)))
+            derive_in(room.at[side])
             terms = [
-                dot(lefts[0], rights[0]) + dot(lefts[1], rights[1]),
-                dot(lefts[2], rights[2]),
+                dot(room[side, :, a:b], val[:, a:b]) for a, b in ((0, 2 * FB), (2 * FB, 3 * FB))
             ]
         else:
             terms = [
@@ -416,7 +428,6 @@
         return mark
 
     mark = send_half(0, 1, [])
-    mark = send_half(1, min(4, count), [mark])
     sib = [lax.ppermute(array, "dp", across) for array in own]
     sib_lengths = lax.ppermute(cand_lengths, "dp", across)
 
@@ -446,17 +457,17 @@
         return mark
 
     work = []
-    cuts = [c for c in (4, 8, 12) if c < count] + [count]
+    cuts = [c for c in (1, 2, 3, 4, 6, 8, 9) if c < count] + [count]
     for lo, hi in zip(cuts[:-1], cuts[1:]):
         work.append((0, functools.partial(send_half, lo, hi)))
     for k in range(count):
-        work.append((max((k + chips) * ROUNDS - 1, START), functools.partial(consume, k)))
+        work.append(((k + chips) * ROUNDS - 1, functools.partial(consume, k)))
 
     slot = 0
     for t in range(steps):
         for r in range(ROUNDS):
-            if t < count:
-                part, at = sib_parts[t]
+            if t < steps - 1:
+                part, at = sib_parts[min(t, count - 1)]
                 held[r][t] = inject(t, at, r, half, n_dp, round_owner, vals, part, got[r], [mark])
             else:
                 held[r][t] = got[r]

time: 303 us -> 255 us (0.84); the launches traced: 299 us -> 256 us
  Pallas kernels: 159 us -> 115 us
  starting transfers between devices: 56.8 us -> 80.5 us
  waiting for transfers between devices: 67.1 us -> 46.8 us
    pallas_call x34 -> x24, Pallas kernels: 56.1 us -> 23.3 us  [inject(): pl.pallas_call(functools.partial(inject_body, t, at, r, groups, width, n_...]
    ppermute x38 -> x24, starting transfers between devices: 36.6 us -> 60.2 us  [local(): got[r] = lax.ppermute(held[r][t], 'dp', along)]
    ppermute x38 -> x24, waiting for transfers between devices: 59.4 us -> 39.5 us  [local(): got[r] = lax.ppermute(held[r][t], 'dp', along)]
    pallas_call x17 -> x10, Pallas kernels: 76.6 us -> 63.3 us  [use(): pl.pallas_call(body, in_specs=[IN_SMEM] + [IN_HBM] * (2 * n_cand + n_held...]
    pallas_call x5 -> x8, Pallas kernels: 17.9 us -> 19.9 us  [pack(): pl.pallas_call(functools.partial(pack_body, groups, width, first), grid_s...]
  transfers between devices with their start and end apart: 62 -> 51, of which waited for: 30 -> 21; matrix products, arithmetic and copies ran while one was open for 3% -> 3% of each run, Pallas kernels for 50% -> 43%
where the time goes in v2:
time: 255 us; the launch traced here: 256 us
  Pallas kernels  115 us (45%)
  starting transfers between devices  80.5 us (32%)
  waiting for transfers between devices  46.8 us (18%)
  other arithmetic  7.1 us (3%)
  between operations  4.3 us (2%)
    pallas_call x10, Pallas kernels, use(): pl.pallas_call(body, in_specs=[IN_SMEM] + [IN_HBM] * (2 * n_cand + n_held...  63.3 us
    ppermute x24, starting transfers between devices, local(): got[r] = lax.ppermute(held[r][t], 'dp', along)  60.2 us
    ppermute x24, waiting for transfers between devices, local(): got[r] = lax.ppermute(held[r][t], 'dp', along)  39.5 us
    pallas_call x24, Pallas kernels, inject(): pl.pallas_call(functools.partial(inject_body, t, at, r, groups, width, n_...  23.3 us
    pallas_call x8, Pallas kernels, pack(): pl.pallas_call(functools.partial(pack_body, groups, width, first), grid_s...  19.9 us
    ppermute x9, starting transfers between devices, scatter(): lax.ppermute(pieces[m], 'tensor', [(z, (z + m) % n_tensor) for z in range...  14.8 us
    pallas_call x3, Pallas kernels, cut(): pl.pallas_call(functools.partial(cut_body, pieces), grid_spec=pltpu.Prefe...  5.74 us
  transfers between devices with their start and end apart: 51, of which 21 were waited for; matrix products, arithmetic and copies ran while one was open for 3% of the time, Pallas kernels for 43%

profile of v2, /device:TPU:0, one launch (start us, length us, event | category | flops | bytes accessed | tf_op | source)
XLA Modules:
  0.0 255.6 jit_solution(17014136371111046080)
XLA Ops:
  23.1 6.5 %collective-permute-done.11.rest_0_ = bf16[128,2688]{1,0:T(8,128)(2,1)} collective-permute-done((bf16[128,2688]{1,0:T(8,128)(2,1)}, bf16[128,2688]{1,0:T(8,128)(2,1)}, u32[]{:S(2)}, u32[]{:S(2)}) %collective-permute-start.11) | collective-permute-done | bytes 688160 | tf_op jit(solution)/shard_map/ppermute | solution.py:475
  34.9 3.4 %collective-permute-start.16 = (bf16[128,2688]{1,0:T(8,128)(2,1)}, bf16[128,2688]{1,0:T(8,128)(2,1)}, u32[]{:S(2)}, u32[]{:S(2)}) collective-permute-start(bf16[128,2688]{1,0:T(8,128)(2,1)} %shard_map.134.rest_0_.refs_15_.refs_14_), channel_id=1, source_target_pairs={{0,8},{4,20},{8,24},{12,4},{24,16},{28,12},{16,0},{20,28},{1,9},{5... | collective-permute-start | bytes 2064392 | tf_op jit(solution)/shard_map/ppermute | solution.py:475
  44.5 3.7 %collective-permute-done.16.rest_0_ = bf16[128,2688]{1,0:T(8,128)(2,1)} collective-permute-done((bf16[128,2688]{1,0:T(8,128)(2,1)}, bf16[128,2688]{1,0:T(8,128)(2,1)}, u32[]{:S(2)}, u32[]{:S(2)}) %collective-permute-start.16) | collective-permute-done | bytes 688160 | tf_op jit(solution)/shard_map/ppermute | solution.py:475
  53.9 3.4 %collective-permute-start.18 = (bf16[128,2688]{1,0:T(8,128)(2,1)}, bf16[128,2688]{1,0:T(8,128)(2,1)}, u32[]{:S(2)}, u32[]{:S(2)}) collective-permute-start(bf16[128,2688]{1,0:T(8,128)(2,1)} %shard_map.138.rest_0_.refs_16_.refs_15_.refs_14_), channel_id=1, source_target_pairs={{0,8},{4,20},{8,24},{12,4},{24,16},{28,12},{16,0},{20,28},{1,9},{5... | collective-permute-start | bytes 2064392 | tf_op jit(solution)/shard_map/ppermute | solution.py:475
  59.5 7.4 %collective-permute-done.18.rest_0_ = bf16[128,2688]{1,0:T(8,128)(2,1)} collective-permute-done((bf16[128,2688]{1,0:T(8,128)(2,1)}, bf16[128,2688]{1,0:T(8,128)(2,1)}, u32[]{:S(2)}, u32[]{:S(2)}) %collective-permute-start.18) | collective-permute-done | bytes 688160 | tf_op jit(solution)/shard_map/ppermute | solution.py:475
  73.4 5.7 %collective-permute-start.20 = (bf16[128,2688]{1,0:T(8,128)(2,1)}, bf16[128,2688]{1,0:T(8,128)(2,1)}, u32[]{:S(2)}, u32[]{:S(2)}) collective-permute-start(bf16[128,2688]{1,0:T(8,128)(2,1)} %shard_map.142.refs_17_.refs_18_.refs_16_.refs_15_.refs_14_), channel_id=1, source_target_pairs={{0,8},{4,20},{8,24},{12,4},{24,16},{28,12},{16,0},{20,28},{1,9},{5... | collective-permute-start | bytes 2064392 | tf_op jit(solution)/shard_map/ppermute | solution.py:475
  79.1 6.3 %shard_map.143 = (f32[2,512,256]{2,1,0:T(8,128)}, f32[8,128]{1,0:T(8,128)}) custom-call(s32[2]{0:T(128)} %owner.67, bf16[256,7168]{1,0:T(8,128)(2,1)} %refs_0_.19, bf16[256,7168]{1,0:T(8,128)(2,1)} %refs_1_.19, bf16[256,7168]{1,0:T(8,128)(2,1)} %refs_2_.19, bf16[256,2048]{1,0:T(8,128)(2,1)} %refs_3_.19, bf16[256,2048]{1,0:T(8,128)(2,1)} %refs_4_.19, ...), custom_call_target="tpu_custom_call" | custom-call | flops 704643072 | bytes 5177344 | tf_op jit(solution)/shard_map/pallas_call | solution.py:295
  88.6 4.3 %collective-permute-start.22 = (bf16[128,2688]{1,0:T(8,128)(2,1)}, bf16[128,2688]{1,0:T(8,128)(2,1)}, u32[]{:S(2)}, u32[]{:S(2)}) collective-permute-start(bf16[128,2688]{1,0:T(8,128)(2,1)} %shard_map.145.refs_17_.refs_19_.refs_16_.refs_15_.refs_14_), channel_id=1, source_target_pairs={{0,8},{4,20},{8,24},{12,4},{24,16},{28,12},{16,0},{20,28},{1,9},{5... | collective-permute-start | bytes 2064392 | tf_op jit(solution)/shard_map/ppermute | solution.py:475
  96.0 4.4 %collective-permute-start.19 = (bf16[128,2688]{1,0:T(8,128)(2,1)}, bf16[128,2688]{1,0:T(8,128)(2,1)}, u32[]{:S(2)}, u32[]{:S(2)}) collective-permute-start(bf16[128,2688]{1,0:T(8,128)(2,1)} %shard_map.144.refs_13_.refs_12_.refs_11_.refs_10_), channel_id=1, source_target_pairs={{0,8},{4,20},{8,24},{12,4},{24,16},{28,12},{16,0},{20,28},{1,9},{5... | collective-permute-start | bytes 2064392 | tf_op jit(solution)/shard_map/ppermute | solution.py:475
  100.4 6.8 %shard_map.146 = (f32[2,512,256]{2,1,0:T(8,128)}, f32[8,128]{1,0:T(8,128)}) custom-call(s32[2]{0:T(128)} %owner.67, bf16[256,7168]{1,0:T(8,128)(2,1)} %refs_0_.19, bf16[256,7168]{1,0:T(8,128)(2,1)} %refs_1_.19, bf16[256,7168]{1,0:T(8,128)(2,1)} %refs_2_.19, bf16[256,2048]{1,0:T(8,128)(2,1)} %refs_3_.19, bf16[256,2048]{1,0:T(8,128)(2,1)} %refs_4_.19, ...), custom_call_target="tpu_custom_call" | custom-call | flops 704643072 | bytes 5177344 | tf_op jit(solution)/shard_map/pallas_call | solution.py:295
  110.8 4.3 %collective-permute-start.21 = (bf16[128,2688]{1,0:T(8,128)(2,1)}, bf16[128,2688]{1,0:T(8,128)(2,1)}, u32[]{:S(2)}, u32[]{:S(2)}) collective-permute-start(bf16[128,2688]{1,0:T(8,128)(2,1)} %shard_map.147.refs_13_.refs_12_.refs_11_.refs_10_), channel_id=1, source_target_pairs={{0,8},{4,20},{8,24},{12,4},{24,16},{28,12},{16,0},{20,28},{1,9},{5... | collective-permute-start | bytes 2064392 | tf_op jit(solution)/shard_map/ppermute | solution.py:475
  115.1 6.8 %shard_map.149 = (f32[2,512,256]{2,1,0:T(8,128)}, f32[8,128]{1,0:T(8,128)}) custom-call(s32[2]{0:T(128)} %owner.67, bf16[256,7168]{1,0:T(8,128)(2,1)} %refs_0_.19, bf16[256,7168]{1,0:T(8,128)(2,1)} %refs_1_.19, bf16[256,7168]{1,0:T(8,128)(2,1)} %refs_2_.19, bf16[256,2048]{1,0:T(8,128)(2,1)} %refs_3_.19, bf16[256,2048]{1,0:T(8,128)(2,1)} %refs_4_.19, ...), custom_call_target="tpu_custom_call" | custom-call | flops 704643072 | bytes 5177344 | tf_op jit(solution)/shard_map/pallas_call | solution.py:295
  127.5 3.7 %collective-permute-start.23 = (bf16[128,2688]{1,0:T(8,128)(2,1)}, bf16[128,2688]{1,0:T(8,128)(2,1)}, u32[]{:S(2)}, u32[]{:S(2)}) collective-permute-start(bf16[128,2688]{1,0:T(8,128)(2,1)} %shard_map.150.refs_13_.refs_12_.refs_11_.refs_10_), channel_id=1, source_target_pairs={{0,8},{4,20},{8,24},{12,4},{24,16},{28,12},{16,0},{20,28},{1,9},{5... | collective-permute-start | bytes 2064392 | tf_op jit(solution)/shard_map/ppermute | solution.py:475
  131.3 6.8 %shard_map.152 = (f32[2,512,256]{2,1,0:T(8,128)}, f32[8,128]{1,0:T(8,128)}) custom-call(s32[2]{0:T(128)} %owner.67, bf16[256,7168]{1,0:T(8,128)(2,1)} %refs_0_.19, bf16[256,7168]{1,0:T(8,128)(2,1)} %refs_1_.19, bf16[256,7168]{1,0:T(8,128)(2,1)} %refs_2_.19, bf16[256,2048]{1,0:T(8,128)(2,1)} %refs_3_.19, bf16[256,2048]{1,0:T(8,128)(2,1)} %refs_4_.19, ...), custom_call_target="tpu_custom_call" | custom-call | flops 704643072 | bytes 5177344 | tf_op jit(solution)/shard_map/pallas_call | solution.py:295
  142.3 3.7 %collective-permute-start.26 = (bf16[128,2688]{1,0:T(8,128)(2,1)}, bf16[128,2688]{1,0:T(8,128)(2,1)}, u32[]{:S(2)}, u32[]{:S(2)}) collective-permute-start(bf16[128,2688]{1,0:T(8,128)(2,1)} %shard_map.153.refs_13_.refs_12_.refs_11_.refs_10_), channel_id=1, source_target_pairs={{0,8},{4,20},{8,24},{12,4},{24,16},{28,12},{16,0},{20,28},{1,9},{5... | collective-permute-start | bytes 2064392 | tf_op jit(solution)/shard_map/ppermute | solution.py:475
  146.0 6.8 %shard_map.155 = (f32[2,512,256]{2,1,0:T(8,128)}, f32[8,128]{1,0:T(8,128)}) custom-call(s32[2]{0:T(128)} %owner.67, bf16[256,7168]{1,0:T(8,128)(2,1)} %refs_0_.19, bf16[256,7168]{1,0:T(8,128)(2,1)} %refs_1_.19, bf16[256,7168]{1,0:T(8,128)(2,1)} %refs_2_.19, bf16[256,2048]{1,0:T(8,128)(2,1)} %refs_3_.19, bf16[256,2048]{1,0:T(8,128)(2,1)} %refs_4_.19, ...), custom_call_target="tpu_custom_call" | custom-call | flops 704643072 | bytes 5177344 | tf_op jit(solution)/shard_map/pallas_call | solution.py:295
  158.4 4.0 %collective-permute-start.29 = (bf16[128,2688]{1,0:T(8,128)(2,1)}, bf16[128,2688]{1,0:T(8,128)(2,1)}, u32[]{:S(2)}, u32[]{:S(2)}) collective-permute-start(bf16[128,2688]{1,0:T(8,128)(2,1)} %shard_map.156.refs_13_.refs_12_.refs_11_.refs_10_), channel_id=1, source_target_pairs={{0,8},{4,20},{8,24},{12,4},{24,16},{28,12},{16,0},{20,28},{1,9},{5... | collective-permute-start | bytes 2064392 | tf_op jit(solution)/shard_map/ppermute | solution.py:475
  162.4 6.8 %shard_map.158 = (f32[2,512,256]{2,1,0:T(8,128)}, f32[8,128]{1,0:T(8,128)}) custom-call(s32[2]{0:T(128)} %owner.67, bf16[256,7168]{1,0:T(8,128)(2,1)} %refs_0_.19, bf16[256,7168]{1,0:T(8,128)(2,1)} %refs_1_.19, bf16[256,7168]{1,0:T(8,128)(2,1)} %refs_2_.19, bf16[256,2048]{1,0:T(8,128)(2,1)} %refs_3_.19, bf16[256,2048]{1,0:T(8,128)(2,1)} %refs_4_.19, ...), custom_call_target="tpu_custom_call" | custom-call | flops 704643072 | bytes 5177344 | tf_op jit(solution)/shard_map/pallas_call | solution.py:295
  173.2 3.6 %collective-permute-start.31 = (bf16[128,2688]{1,0:T(8,128)(2,1)}, bf16[128,2688]{1,0:T(8,128)(2,1)}, u32[]{:S(2)}, u32[]{:S(2)}) collective-permute-start(bf16[128,2688]{1,0:T(8,128)(2,1)} %shard_map.159.refs_13_.refs_12_.refs_11_.refs_10_), channel_id=1, source_target_pairs={{0,8},{4,20},{8,24},{12,4},{24,16},{28,12},{16,0},{20,28},{1,9},{5... | collective-permute-start | bytes 2064392 | tf_op jit(solution)/shard_map/ppermute | solution.py:475
  176.9 6.8 %shard_map.161 = (f32[2,512,256]{2,1,0:T(8,128)}, f32[8,128]{1,0:T(8,128)}) custom-call(s32[2]{0:T(128)} %owner.67, bf16[256,7168]{1,0:T(8,128)(2,1)} %refs_0_.19, bf16[256,7168]{1,0:T(8,128)(2,1)} %refs_1_.19, bf16[256,7168]{1,0:T(8,128)(2,1)} %refs_2_.19, bf16[256,2048]{1,0:T(8,128)(2,1)} %refs_3_.19, bf16[256,2048]{1,0:T(8,128)(2,1)} %refs_4_.19, ...), custom_call_target="tpu_custom_call" | custom-call | flops 704643072 | bytes 5177344 | tf_op jit(solution)/shard_map/pallas_call | solution.py:295
  184.7 4.1 %collective-permute-done.31.rest_0_ = bf16[128,2688]{1,0:T(8,128)(2,1)} collective-permute-done((bf16[128,2688]{1,0:T(8,128)(2,1)}, bf16[128,2688]{1,0:T(8,128)(2,1)}, u32[]{:S(2)}, u32[]{:S(2)}) %collective-permute-start.31) | collective-permute-done | bytes 688160 | tf_op jit(solution)/shard_map/ppermute | solution.py:475
  198.0 6.8 %shard_map.164 = (f32[2,512,256]{2,1,0:T(8,128)}, f32[8,128]{1,0:T(8,128)}) custom-call(s32[2]{0:T(128)} %owner.67, bf16[256,7168]{1,0:T(8,128)(2,1)} %refs_0_.19, bf16[256,7168]{1,0:T(8,128)(2,1)} %refs_1_.19, bf16[256,7168]{1,0:T(8,128)(2,1)} %refs_2_.19, bf16[256,2048]{1,0:T(8,128)(2,1)} %refs_3_.19, bf16[256,2048]{1,0:T(8,128)(2,1)} %refs_4_.19, ...), custom_call_target="tpu_custom_call" | custom-call | flops 704643072 | bytes 5177344 | tf_op jit(solution)/shard_map/pallas_call | solution.py:295
  215.9 4.8 %shard_map.168 = (f32[1,512,256]{2,1,0:T(8,128)}, f32[1,512,256]{2,1,0:T(8,128)}, f32[8,128]{1,0:T(8,128)}) custom-call(s32[2]{0:T(128)} %owner.67, bf16[256,7168]{1,0:T(8,128)(2,1)} %refs_0_.19, bf16[256,7168]{1,0:T(8,128)(2,1)} %refs_1_.19, bf16[256,7168]{1,0:T(8,128)(2,1)} %refs_2_.19, bf16[256,2048]{1,0:T(8,128)(2,1)} %refs_3_.19, ...), custom_call_target="tpu_custom_call" | custom-call | flops 704643072 | bytes 5177344 | tf_op jit(solution)/shard_map/pallas_call | solution.py:295
  226.9 4.6 %shard_map.170 = (f32[1,512,256]{2,1,0:T(8,128)}, f32[8,128]{1,0:T(8,128)}) custom-call(s32[2]{0:T(128)} %owner.67, bf16[256,7168]{1,0:T(8,128)(2,1)} %refs_0_.19, bf16[256,7168]{1,0:T(8,128)(2,1)} %refs_1_.19, bf16[256,7168]{1,0:T(8,128)(2,1)} %refs_2_.19, bf16[256,2048]{1,0:T(8,128)(2,1)} %refs_3_.19, bf16[256,2048]{1,0:T(8,128)(2,1)} %refs_4_.19, ...), custom_call_target="tpu_custom_call" | custom-call | flops 704643072 | bytes 5177344 | tf_op jit(solution)/shard_map/pallas_call | solution.py:295
  (155 shorter events, 125.7 us)
Async XLA Ops:
  2.9 16.7 %collective-permute-start.4 = (bf16[256,2048]{1,0:T(8,128)(2,1)}, bf16[256,2048]{1,0:T(8,128)(2,1)}, u32[]{:S(2)}, u32[]{:S(2)}) collective-permute-start(bf16[256,2048]{1,0:T(8,128)(2,1)} %refs_3_.19), channel_id=1, source_target_pairs={{0,4},{4,0},{8,12},{12,8},{16,20},{20,16},{24,28},{28,24},{1,5},{5... | collective-permute-start | bytes 3145736 | tf_op jit(solution)/shard_map/ppermute | solution.py:431
  13.0 66.0 %collective-permute-start.1 = (bf16[256,7168]{1,0:T(8,128)(2,1)}, bf16[256,7168]{1,0:T(8,128)(2,1)}, u32[]{:S(2)}, u32[]{:S(2)}) collective-permute-start(bf16[256,7168]{1,0:T(8,128)(2,1)} %refs_0_.19), channel_id=1, source_target_pairs={{0,4},{4,0},{8,12},{12,8},{16,20},{20,16},{24,28},{28,24},{1,5},{5... | collective-permute-start | bytes 11010056 | tf_op jit(solution)/shard_map/ppermute | solution.py:431
  19.6 15.3 %collective-permute-start.7 = (bf16[1,128,2688]{2,1,0:T(8,128)(2,1)}, bf16[1,128,2688]{2,1,0:T(8,128)(2,1)}, u32[]{:S(2)}, u32[]{:S(2)}) collective-permute-start(bf16[1,128,2688]{2,1,0:T(8,128)(2,1)} %get-tuple-element.55), channel_id=1, source_target_pairs={{0,4},{4,0},{8,12},{12,8},{16,20},{20,16},{24,28},{28,24},{1,5},{5... | collective-permute-start | bytes 2064392 | tf_op jit(solution)/shard_map/ppermute | solution.py:425
  19.6 59.5 %collective-permute-start.2 = (bf16[256,7168]{1,0:T(8,128)(2,1)}, bf16[256,7168]{1,0:T(8,128)(2,1)}, u32[]{:S(2)}, u32[]{:S(2)}) collective-permute-start(bf16[256,7168]{1,0:T(8,128)(2,1)} %refs_1_.19), channel_id=1, source_target_pairs={{0,4},{4,0},{8,12},{12,8},{16,20},{20,16},{24,28},{28,24},{1,5},{5... | collective-permute-start | bytes 11010056 | tf_op jit(solution)/shard_map/ppermute | solution.py:431
  22.3 56.8 %collective-permute-start.3 = (bf16[256,7168]{1,0:T(8,128)(2,1)}, bf16[256,7168]{1,0:T(8,128)(2,1)}, u32[]{:S(2)}, u32[]{:S(2)}) collective-permute-start(bf16[256,7168]{1,0:T(8,128)(2,1)} %refs_2_.19), channel_id=1, source_target_pairs={{0,4},{4,0},{8,12},{12,8},{16,20},{20,16},{24,28},{28,24},{1,5},{5... | collective-permute-start | bytes 11010056 | tf_op jit(solution)/shard_map/ppermute | solution.py:431
  66.9 18.5 %collective-permute-start.13 = (bf16[2,128,2688]{2,1,0:T(8,128)(2,1)}, bf16[2,128,2688]{2,1,0:T(8,128)(2,1)}, u32[]{:S(2)}, u32[]{:S(2)}) collective-permute-start(bf16[2,128,2688]{2,1,0:T(8,128)(2,1)} %get-tuple-element.61), channel_id=1, source_target_pairs={{0,4},{4,0},{8,12},{12,8},{16,20},{20,16},{24,28},{28,24},{1,5},{5... | collective-permute-start | bytes 4128776 | tf_op jit(solution)/shard_map/ppermute | solution.py:425
  79.0 16.1 %collective-permute-start.17 = (bf16[128,2688]{1,0:T(8,128)(2,1)}, bf16[128,2688]{1,0:T(8,128)(2,1)}, u32[]{:S(2)}, u32[]{:S(2)}) collective-permute-start(bf16[128,2688]{1,0:T(8,128)(2,1)} %shard_map.140.rest_0_.refs_13_.refs_12_.refs_11_.refs_10_), channel_id=1, source_target_pairs={{0,8},{4,20},{8,24},{12,4},{24,16},{28,12},{16,0},{20,28},{1,9},{5... | collective-permute-start | bytes 2064392 | tf_op jit(solution)/shard_map/ppermute | solution.py:475
  88.6 18.6 %collective-permute-start.22 = (bf16[128,2688]{1,0:T(8,128)(2,1)}, bf16[128,2688]{1,0:T(8,128)(2,1)}, u32[]{:S(2)}, u32[]{:S(2)}) collective-permute-start(bf16[128,2688]{1,0:T(8,128)(2,1)} %shard_map.145.refs_17_.refs_19_.refs_16_.refs_15_.refs_14_), channel_id=1, source_target_pairs={{0,8},{4,20},{8,24},{12,4},{24,16},{28,12},{16,0},{20,28},{1,9},{5... | collective-permute-start | bytes 2064392 | tf_op jit(solution)/shard_map/ppermute | solution.py:475
  93.0 29.0 %collective-permute-start.12 = (bf16[2,128,2688]{2,1,0:T(8,128)(2,1)}, bf16[2,128,2688]{2,1,0:T(8,128)(2,1)}, u32[]{:S(2)}, u32[]{:S(2)}) collective-permute-start(bf16[2,128,2688]{2,1,0:T(8,128)(2,1)} %get-tuple-element.60), channel_id=1, source_target_pairs={{0,4},{4,0},{8,12},{12,8},{16,20},{20,16},{24,28},{28,24},{1,5},{5... | collective-permute-start | bytes 4128776 | tf_op jit(solution)/shard_map/ppermute | solution.py:425
  110.8 15.9 %collective-permute-start.21 = (bf16[128,2688]{1,0:T(8,128)(2,1)}, bf16[128,2688]{1,0:T(8,128)(2,1)}, u32[]{:S(2)}, u32[]{:S(2)}) collective-permute-start(bf16[128,2688]{1,0:T(8,128)(2,1)} %shard_map.147.refs_13_.refs_12_.refs_11_.refs_10_), channel_id=1, source_target_pairs={{0,8},{4,20},{8,24},{12,4},{24,16},{28,12},{16,0},{20,28},{1,9},{5... | collective-permute-start | bytes 2064392 | tf_op jit(solution)/shard_map/ppermute | solution.py:475
  131.3 21.6 %collective-permute-start.25 = (bf16[1,128,2688]{2,1,0:T(8,128)(2,1)}, bf16[1,128,2688]{2,1,0:T(8,128)(2,1)}, u32[]{:S(2)}, u32[]{:S(2)}) collective-permute-start(bf16[1,128,2688]{2,1,0:T(8,128)(2,1)} %get-tuple-element.73), channel_id=1, source_target_pairs={{0,4},{4,0},{8,12},{12,8},{16,20},{20,16},{24,28},{28,24},{1,5},{5... | collective-permute-start | bytes 2064392 | tf_op jit(solution)/shard_map/ppermute | solution.py:425
  142.3 15.3 %collective-permute-start.26 = (bf16[128,2688]{1,0:T(8,128)(2,1)}, bf16[128,2688]{1,0:T(8,128)(2,1)}, u32[]{:S(2)}, u32[]{:S(2)}) collective-permute-start(bf16[128,2688]{1,0:T(8,128)(2,1)} %shard_map.153.refs_13_.refs_12_.refs_11_.refs_10_), channel_id=1, source_target_pairs={{0,8},{4,20},{8,24},{12,4},{24,16},{28,12},{16,0},{20,28},{1,9},{5... | collective-permute-start | bytes 2064392 | tf_op jit(solution)/shard_map/ppermute | solution.py:475
  146.0 23.2 %collective-permute-start.28 = (bf16[1,128,2688]{2,1,0:T(8,128)(2,1)}, bf16[1,128,2688]{2,1,0:T(8,128)(2,1)}, u32[]{:S(2)}, u32[]{:S(2)}) collective-permute-start(bf16[1,128,2688]{2,1,0:T(8,128)(2,1)} %get-tuple-element.76), channel_id=1, source_target_pairs={{0,4},{4,0},{8,12},{12,8},{16,20},{20,16},{24,28},{28,24},{1,5},{5... | collective-permute-start | bytes 2064392 | tf_op jit(solution)/shard_map/ppermute | solution.py:425
  153.7 15.5 %collective-permute-start.32 = (bf16[128,2688]{1,0:T(8,128)(2,1)}, bf16[128,2688]{1,0:T(8,128)(2,1)}, u32[]{:S(2)}, u32[]{:S(2)}) collective-permute-start(bf16[128,2688]{1,0:T(8,128)(2,1)} %shard_map.157.refs_17_.refs_19_.refs_16_.refs_15_.refs_14_), channel_id=1, source_target_pairs={{0,8},{4,20},{8,24},{12,4},{24,16},{28,12},{16,0},{20,28},{1,9},{5... | collective-permute-start | bytes 2064392 | tf_op jit(solution)/shard_map/ppermute | solution.py:475
  173.2 15.5 %collective-permute-start.31 = (bf16[128,2688]{1,0:T(8,128)(2,1)}, bf16[128,2688]{1,0:T(8,128)(2,1)}, u32[]{:S(2)}, u32[]{:S(2)}) collective-permute-start(bf16[128,2688]{1,0:T(8,128)(2,1)} %shard_map.159.refs_13_.refs_12_.refs_11_.refs_10_), channel_id=1, source_target_pairs={{0,8},{4,20},{8,24},{12,4},{24,16},{28,12},{16,0},{20,28},{1,9},{5... | collective-permute-start | bytes 2064392 | tf_op jit(solution)/shard_map/ppermute | solution.py:475
  176.9 30.5 %collective-permute-start = (s32[1,8]{1,0:T(1,128)S(1)}, s32[1,8]{1,0:T(1,128)S(1)}, u32[]{:S(2)}, u32[]{:S(2)}) collective-permute-start(s32[1,8]{1,0:T(1,128)S(1)} %copy-done.3), channel_id=1, source_target_pairs={{0,4},{4,0},{8,12},{12,8},{16,20},{20,16},{24,28},{28,24},{1,5},{5... | collective-permute-start | bytes 104 | tf_op jit(solution)/shard_map/ppermute | solution.py:432
  184.5 20.4 %collective-permute-start.38 = (bf16[128,2688]{1,0:T(8,128)(2,1)}, bf16[128,2688]{1,0:T(8,128)(2,1)}, u32[]{:S(2)}, u32[]{:S(2)}) collective-permute-start(bf16[128,2688]{1,0:T(8,128)(2,1)} %shard_map.163.refs_17_.refs_19_.refs_16_.refs_15_), channel_id=1, source_target_pairs={{0,8},{4,20},{8,24},{12,4},{24,16},{28,12},{16,0},{20,28},{1,9},{5... | collective-permute-start | bytes 2064392 | tf_op jit(solution)/shard_map/ppermute | solution.py:475
  189.5 16.2 %collective-permute-start.37 = (bf16[128,2688]{1,0:T(8,128)(2,1)}, bf16[128,2688]{1,0:T(8,128)(2,1)}, u32[]{:S(2)}, u32[]{:S(2)}) collective-permute-start(bf16[128,2688]{1,0:T(8,128)(2,1)} %shard_map.162.refs_13_.refs_12_.refs_11_), channel_id=1, source_target_pairs={{0,8},{4,20},{8,24},{12,4},{24,16},{28,12},{16,0},{20,28},{1,9},{5... | collective-permute-start | bytes 2064392 | tf_op jit(solution)/shard_map/ppermute | solution.py:475
  205.6 16.8 %collective-permute-start.43 = (bf16[128,2688]{1,0:T(8,128)(2,1)}, bf16[128,2688]{1,0:T(8,128)(2,1)}, u32[]{:S(2)}, u32[]{:S(2)}) collective-permute-start(bf16[128,2688]{1,0:T(8,128)(2,1)} %shard_map.167.refs_17_.refs_18_.refs_16_), channel_id=1, source_target_pairs={{0,8},{4,20},{8,24},{12,4},{24,16},{28,12},{16,0},{20,28},{1,9},{5... | collective-permute-start | bytes 2064392 | tf_op jit(solution)/shard_map/ppermute | solution.py:475
  206.5 17.8 %collective-permute-start.42 = (bf16[128,2688]{1,0:T(8,128)(2,1)}, bf16[128,2688]{1,0:T(8,128)(2,1)}, u32[]{:S(2)}, u32[]{:S(2)}) collective-permute-start(bf16[128,2688]{1,0:T(8,128)(2,1)} %shard_map.166.refs_13_.refs_12_), channel_id=1, source_target_pairs={{0,8},{4,20},{8,24},{12,4},{24,16},{28,12},{16,0},{20,28},{1,9},{5... | collective-permute-start | bytes 2064392 | tf_op jit(solution)/shard_map/ppermute | solution.py:475
  210.3 23.0 %collective-permute-start.34 = (bf16[2,128,256]{2,1,0:T(8,128)(2,1)}, bf16[2,128,256]{2,1,0:T(8,128)(2,1)S(1)}, u32[]{:S(2)}, u32[]{:S(2)}) collective-permute-start(bf16[2,128,256]{2,1,0:T(8,128)(2,1)} %get-tuple-element.84), channel_id=1, source_target_pairs={{0,1},{1,2},{2,3},{3,0},{4,5},{5,6},{6,7},{7,4},{8,9},{9,10},{10,1... | collective-permute-start | bytes 393224 | tf_op jit(solution)/shard_map/ppermute | solution.py:442
  211.9 22.8 %collective-permute-start.35 = (bf16[2,128,256]{2,1,0:T(8,128)(2,1)}, bf16[2,128,256]{2,1,0:T(8,128)(2,1)}, u32[]{:S(2)}, u32[]{:S(2)}) collective-permute-start(bf16[2,128,256]{2,1,0:T(8,128)(2,1)} %get-tuple-element.85), channel_id=1, source_target_pairs={{0,2},{1,3},{2,0},{3,1},{4,6},{5,7},{6,4},{7,5},{8,10},{9,11},{10,... | collective-permute-start | bytes 393224 | tf_op jit(solution)/shard_map/ppermute | solution.py:442
  214.5 20.9 %collective-permute-start.36 = (bf16[2,128,256]{2,1,0:T(8,128)(2,1)}, bf16[2,128,256]{2,1,0:T(8,128)(2,1)}, u32[]{:S(2)}, u32[]{:S(2)}) collective-permute-start(bf16[2,128,256]{2,1,0:T(8,128)(2,1)} %get-tuple-element.86), channel_id=1, source_target_pairs={{0,3},{1,0},{2,1},{3,2},{4,7},{5,4},{6,5},{7,6},{8,11},{9,8},{10,9... | collective-permute-start | bytes 393224 | tf_op jit(solution)/shard_map/ppermute | solution.py:442
  224.3 16.2 %collective-permute-start.40 = (bf16[1,128,256]{2,1,0:T(8,128)(2,1)}, bf16[1,128,256]{2,1,0:T(8,128)(2,1)}, u32[]{:S(2)}, u32[]{:S(2)}) collective-permute-start(bf16[1,128,256]{2,1,0:T(8,128)(2,1)} %get-tuple-element.91), channel_id=1, source_target_pairs={{0,2},{1,3},{2,0},{3,1},{4,6},{5,7},{6,4},{7,5},{8,10},{9,11},{10,... | collective-permute-start | bytes 196616 | tf_op jit(solution)/shard_map/ppermute | solution.py:442
  (31 other events, 310.2 us)

commit v3 on v2

--- a/solution.py
+++ b/solution.py
@@ -32,12 +32,6 @@
     return (grad_gate, grad_up, hidden)
 
 
-def segment_of(lengths, total):
-    bounds = jnp.cumsum(lengths)
-    position = jnp.arange(total, dtype=jnp.int32)
-    return jnp.sum((position[:, None] >= bounds[None, :]).astype(jnp.int32), axis=1)
-
-
 def segments(j, width):
     out = []
     for which in (0, 1):
@@ -61,6 +55,10 @@
 def away_of(me, owner, chips):
     behind = place_of(me // 2, chips) - place_of(owner // 2, chips)
     return lax.rem(jnp.where(me % 2 == 0, behind, -behind) + chips, chips)
+
+
+def valid(j, width):
+    return max(dst + cols for _, _, dst, cols in segments(j, width))
 
 
 def pack_body(groups, width, first, half, gate, up, dh, x, dy, *rest):
@@ -101,7 +99,7 @@
         ),
         out_shape=[jax.ShapeDtypeStruct((count, rows, W), jnp.bfloat16), MARK],
         cost_estimate=pl.CostEstimate(
-            flops=0, bytes_accessed=4 * count * rows * W, transcendentals=0
+            flops=16 * rows * rows * W, bytes_accessed=24 * rows * W, transcendentals=0
         ),
         compiler_params=pltpu.CompilerParams(vmem_limit_bytes=VMEM),
     )(half, *arrays, *deps)
@@ -176,25 +174,63 @@
     )(owner, *vals, sib, *extra)
 
 
-def use_body(k, groups, width, chips, fresh, owner, own, sib, held, accs_in, accs, room, val, sums, sem):
+def trim_body(source, *rest):
+    out, room, sem = rest[-3:]
+    rows, cols = out.shape
+    some = rows // 4
+    ins, outs = [], []
+    for i in range(4):
+        at = pl.ds(i * some, some)
+        ins.append(
+            pltpu.make_async_copy(source.at[at, pl.ds(0, cols)], room.at[at], sem.at[0, i])
+        )
+        outs.append(pltpu.make_async_copy(room.at[at], out.at[at], sem.at[1, i]))
+    for copy in ins:
+        copy.start()
+    for before, copy in zip(ins, outs):
+        before.wait()
+        copy.start()
+    for copy in outs:
+        copy.wait()
+
+
+def trim(source, cols, deps):
+    rows = source.shape[0]
+    return pl.pallas_call(
+        trim_body,
+        in_specs=[IN_HBM] + [ANYWHERE] * len(deps),
+        out_specs=IN_HBM,
+        out_shape=jax.ShapeDtypeStruct((rows, cols), source.dtype),
+        scratch_shapes=[pltpu.VMEM((rows, cols), source.dtype), pltpu.SemaphoreType.DMA((2, 4))],
+        cost_estimate=pl.CostEstimate(flops=0, bytes_accessed=4 * rows * cols, transcendentals=0),
+        compiler_params=pltpu.CompilerParams(vmem_limit_bytes=VMEM),
+    )(source, *deps)
+
+
+def use_body(k, groups, width, chips, names, fresh, owner, own, sib, held, accs_in, accs, room, val, sums, sem):
     rows = room.shape[1]
     half = val.shape[0] // ROUNDS
     me = lax.axis_index("dp")
     brought = []
     for r in range(ROUNDS):
         away = away_of(me, owner[r], chips)
-        there = val.at[pl.ds(r * half, half)]
+        cols = 3 * FB if k < groups else valid(k - groups, width)
+        there = val.at[pl.ds(r * half, half), pl.ds(0, cols)]
         for i in range(chips):
 
             @pl.when(away == i)
             def _():
-                pltpu.make_async_copy(held[r * chips + i], there, sem.at[r]).start()
-
-        brought.append(pltpu.make_async_copy(held[r * chips], there, sem.at[r]))
+                pltpu.make_async_copy(
+                    held[r * chips + i].at[:, pl.ds(0, cols)], there, sem.at[r]
+                ).start()
+
+        brought.append(
+            pltpu.make_async_copy(held[r * chips].at[:, pl.ds(0, cols)], there, sem.at[r])
+        )
     if k < groups:
         parts = [(i, k * FB, i * FB, FB) for i in range(3)]
     else:
-        parts = [(3 + which, src, dst, cols) for which, src, dst, cols in segments(k - groups, width)]
+        parts = segments(k - groups, width)
     loads = []
     for side, arrays in enumerate((own, sib)):
         loads.append([])
@@ -208,8 +244,7 @@
             loads[side].append(copy)
     priors, slot = [], 0
     slots = []
-    for i, acc in enumerate(accs):
-        n = acc.shape[0]
+    for i, (_, n, _) in enumerate(names):
         slots.append((slot, n))
         if not fresh[i]:
             copy = pltpu.make_async_copy(accs_in.pop(0), sums.at[pl.ds(slot, n)], sem.at[8 + i])
@@ -253,32 +288,49 @@
                 for _, _, dst, cols in parts
             ]
         for i, term in enumerate(terms):
-            if fresh[i if len(accs) > 1 else 0]:
+            if fresh[i if len(names) > 1 else 0]:
                 sums[i, at, :] = term
             else:
                 sums[i, at, :] += term
-        for i, acc in enumerate(accs):
-            first, n = slots[i]
-            copy = pltpu.make_async_copy(
-                sums.at[pl.ds(first, n), at], acc.at[:, at], sem.at[10 + 2 * side + i]
-            )
-            copy.start()
-            stores.append(copy)
+        for i, (_, _, pieces) in enumerate(names):
+            if pieces == 0:
+                first, n = slots[i]
+                copy = pltpu.make_async_copy(
+                    sums.at[pl.ds(first, n), at], accs[i][0].at[:, at], sem.at[10 + 2 * side + i]
+                )
+                copy.start()
+                stores.append(copy)
+    for i, (_, _, pieces) in enumerate(names):
+        first, n = slots[i]
+        for m in range(pieces):
+            out = accs[i][m]
+            block = out.shape[1]
+            at = pl.multiple_of(lax.rem(lax.axis_index("tensor") + m, pieces) * block, block)
+            out[...] = sums[first : first + n, pl.ds(at, block), :].astype(out.dtype)
     for copy in stores:
         copy.wait()
 
 
-def use(k, owner, groups, width, chips, own, sib, held, grams, deps):
+def use(k, owner, groups, width, chips, n_tensor, own, sib, held, grams, deps):
     cand_rows, half = own[0].shape[0], held[0].shape[0]
     if k < groups:
-        names = [("gu_h", 2)]
+        names = [("gu_h", 2, n_tensor if k == groups - 1 else 0)]
     else:
-        names = [(("x", "dy")[which], 1) for which, _, _, _ in segments(k - groups, width)]
-    fresh = [name not in grams for name, _ in names]
-    priors = [grams[name] for name, _ in names if name in grams]
-    shapes = [
-        jax.ShapeDtypeStruct((n, 2 * cand_rows, ROUNDS * half), jnp.float32) for _, n in names
-    ]
+        names = [
+            (("x", "dy")[which], 1, n_tensor if src + cols == width else 0)
+            for which, src, _, cols in segments(k - groups, width)
+        ]
+    fresh = [name not in grams for name, _, _ in names]
+    priors = [grams[name] for name, _, _ in names if name in grams]
+    shapes, places, cuts = [], [], []
+    for _, n, pieces in names:
+        rows = 2 * cand_rows // max(pieces, 1)
+        cuts.append(len(shapes))
+        for m in range(max(pieces, 1)):
+            dtype = jnp.bfloat16 if m else jnp.float32
+            shapes.append(jax.ShapeDtypeStruct((n, rows, ROUNDS * half), dtype))
+            places.append(pl.BlockSpec(memory_space=pltpu.VMEM) if pieces else IN_HBM)
+    cuts.append(len(shapes))
     n_cand, n_held = len(own), len(held)
 
     def body(owner, *refs):
@@ -287,9 +339,10 @@
         d = c + len(priors)
         e = d + len(deps)
         f = e + len(shapes)
+        accs = [refs[e + i : e + j] for i, j in zip(cuts[:-1], cuts[1:])]
         use_body(
-            k, groups, width, chips, fresh, owner, refs[:a], refs[a:b], refs[b:c],
-            list(refs[c:d]), refs[e:f], *refs[f + 1 :],
+            k, groups, width, chips, names, fresh, owner, refs[:a], refs[a:b], refs[b:c],
+            list(refs[c:d]), accs, *refs[f + 1 :],
         )
 
     results = pl.pallas_call(
@@ -297,7 +350,7 @@
         in_specs=[IN_SMEM]
         + [IN_HBM] * (2 * n_cand + n_held + len(priors))
         + [ANYWHERE] * len(deps),
-        out_specs=[IN_HBM] * (len(shapes) + 1),
+        out_specs=places + [IN_HBM],
         out_shape=shapes + [MARK],
         scratch_shapes=[
             pltpu.VMEM((2, cand_rows, W), jnp.bfloat16),
@@ -312,42 +365,17 @@
         ),
         compiler_params=pltpu.CompilerParams(vmem_limit_bytes=VMEM),
     )(owner, *own, *sib, *held, *priors, *deps)
-    for (name, _), value in zip(names, results):
-        grams[name] = value
-    return results[-1]
-
-
-def cut_body(pieces, at, acc, own, *others):
-    block = own.shape[1]
-    for m in range(pieces):
-        rows = pl.ds(pl.multiple_of(lax.rem(at[0] + m, pieces) * block, block), block)
-        tile = acc[:, rows, :]
-        if m == 0:
-            own[...] = tile
+    done = {}
+    for (name, _, pieces), i, j in zip(names, cuts[:-1], cuts[1:]):
+        if pieces:
+            done[name] = results[i:j]
         else:
-            others[m - 1][...] = tile.astype(jnp.bfloat16)
-
-
-def cut(at_z, pieces, acc):
-    shape = (acc.shape[0], acc.shape[1] // pieces, acc.shape[2])
-    whole = pl.BlockSpec(shape, lambda i, at: (0, 0, 0))
-    return pl.pallas_call(
-        functools.partial(cut_body, pieces),
-        grid_spec=pltpu.PrefetchScalarGridSpec(
-            num_scalar_prefetch=1,
-            grid=(1,),
-            in_specs=[pl.BlockSpec(acc.shape, lambda i, at: (0, 0, 0))],
-            out_specs=[whole] * pieces,
-        ),
-        out_shape=[jax.ShapeDtypeStruct(shape, jnp.float32)]
-        + [jax.ShapeDtypeStruct(shape, jnp.bfloat16)] * (pieces - 1),
-        cost_estimate=pl.CostEstimate(flops=0, bytes_accessed=8 * acc.size, transcendentals=0),
-        compiler_params=pltpu.CompilerParams(vmem_limit_bytes=VMEM),
-    )(at_z[None], acc)
-
-
-def score_body(pieces, cand_hot, val_hot, *refs):
-    out = refs[-1]
+            grams[name] = results[i]
+    return results[-1], done
+
+
+def score_body(pieces, cand_rows, own_len, sib_len, val_len, owner, *refs):
+    mine, other = refs[-2:]
 
     def total(i, slot):
         value = refs[i * pieces][slot]
@@ -356,30 +384,66 @@
         return value
 
     pair = total(1, 0) * total(0, 0) + total(0, 1) * total(2, 0)
-    half = pair.shape[1] // ROUNDS
+    block, half = pair.shape[0], pair.shape[1] // ROUNDS
+    samples, lanes = own_len.shape[1], mine.shape[2]
+
+    row = lax.broadcasted_iota(jnp.int32, (2 * samples, block), 0)
+    token = lax.axis_index("tensor") * block + lax.broadcasted_iota(
+        jnp.int32, (2 * samples, block), 1
+    )
+    count_row = lax.broadcasted_iota(jnp.int32, (2 * samples, lanes), 0)
+    cand_hot = jnp.zeros((2 * samples, block), jnp.float32)
+    cand_count = jnp.ones((2 * samples, lanes), jnp.float32)
+    for side, lengths in enumerate((own_len, sib_len)):
+        low = jnp.int32(side * cand_rows)
+        for i in range(samples):
+            n = lengths[0, i]
+            at = side * samples + i
+            inside = (row == at) & (token >= low) & (token < low + n)
+            cand_hot = jnp.where(inside, 1.0, cand_hot)
+            cand_count = jnp.where(count_row == at, n.astype(jnp.float32), cand_count)
+            low = low + n
     summed = jnp.dot(
-        cand_hot[...],
+        cand_hot,
         pair,
         precision=lax.Precision.HIGHEST,
         preferred_element_type=jnp.float32,
     )
+    val_token = (lax.axis_index("dp") % 2) * half + lax.broadcasted_iota(
+        jnp.int32, (half, lanes), 0
+    )
+    column = lax.broadcasted_iota(jnp.int32, (half, lanes), 1)
+    count_column = lax.broadcasted_iota(jnp.int32, (2 * samples, lanes), 1)
     for r in range(ROUNDS):
-        out[r] = jnp.dot(
+        val_hot = jnp.zeros((half, lanes), jnp.float32)
+        val_count = jnp.ones((2 * samples, lanes), jnp.float32)
+        low = jnp.int32(0)
+        for j in range(val_len.shape[1]):
+            n = val_len[owner[r], j]
+            inside = (column == j) & (val_token >= low) & (val_token < low + n)
+            val_hot = jnp.where(inside, 1.0, val_hot)
+            val_count = jnp.where(count_column == j, n.astype(jnp.float32), val_count)
+            low = low + n
+        scored = jnp.dot(
             summed[:, r * half : (r + 1) * half],
-            val_hot[r],
+            val_hot,
             precision=lax.Precision.HIGHEST,
             preferred_element_type=jnp.float32,
         )
-
-
-def score(cand_hot, val_hot, gu_h, x, dy):
+        scored = scored * (1.0 / math.sqrt(D * FF)) / jnp.sqrt(cand_count * val_count)
+        mine[r] = scored[:samples]
+        other[r] = scored[samples:]
+
+
+def score(cand_rows, own_len, sib_len, val_len, owner, gu_h, x, dy):
+    shape = jax.ShapeDtypeStruct((ROUNDS, own_len.shape[1], 128), jnp.float32)
+    tiles = list(gu_h) + list(x) + list(dy)
     return pl.pallas_call(
-        functools.partial(score_body, len(x)),
-        out_shape=jax.ShapeDtypeStruct(
-            (ROUNDS, cand_hot.shape[0], val_hot.shape[2]), jnp.float32
-        ),
+        functools.partial(score_body, len(x), cand_rows),
+        in_specs=[IN_SMEM] * 4 + [pl.BlockSpec(memory_space=pltpu.VMEM)] * len(tiles),
+        out_shape=[shape, shape],
         compiler_params=pltpu.CompilerParams(vmem_limit_bytes=VMEM),
-    )(cand_hot, val_hot, *gu_h, *x, *dy)
+    )(own_len, sib_len, val_len, owner, *tiles)
 
 
 def local(
@@ -407,7 +471,6 @@
         along.append((2 * chip + 1, 2 * ring[(i - 1) % chips] + 1))
     across = [(i, i ^ 1) for i in range(n_dp)]
 
-    at_z = lax.axis_index("tensor")
     core = lax.axis_index("dp") % 2
 
     cand_rows, val_rows = cand_x.shape[0], val_x.shape[0]
@@ -428,7 +491,13 @@
         return mark
 
     mark = send_half(0, 1, [])
-    sib = [lax.ppermute(array, "dp", across) for array in own]
+    sib = []
+
+    def send_next(deps):
+        array = own[len(sib)]
+        array = lax.optimization_barrier((array, *deps, *sib[-1:]))[0]
+        sib.append(lax.ppermute(array, "dp", across))
+
     sib_lengths = lax.ppermute(cand_lengths, "dp", across)
 
     grams, parts = {}, {}
@@ -436,85 +505,64 @@
     held = [[None] * steps for _ in range(ROUNDS)]
     got = [None] * ROUNDS
 
-    def scatter(name):
-        pieces = cut(at_z, n_tensor, grams[name])
-        parts[name] = [pieces[0]] + [
-            lax.ppermute(pieces[m], "tensor", [(z, (z + m) % n_tensor) for z in range(n_tensor)])
-            for m in range(1, n_tensor)
-        ]
-
-    last_of = {"gu_h": groups - 1}
-    for k in range(groups, count):
-        for which, _, _, _ in segments(k - groups, width):
-            last_of[("x", "dy")[which]] = k
-
     def consume(k, deps):
         came = [held[r][k + i] for r in range(ROUNDS) for i in range(chips)]
-        mark = use(k, round_owner, groups, width, chips, own, sib, came, grams, deps)
-        for name in last_of:
-            if last_of[name] == k:
-                scatter(name)
+        kind = slice(0, 3) if k < groups else slice(3, 5)
+        mark, done = use(
+            k, round_owner, groups, width, chips, n_tensor, own[kind], sib[kind], came, grams, deps
+        )
+        for name, pieces in done.items():
+            parts[name] = [pieces[0]] + [
+                lax.ppermute(
+                    pieces[m], "tensor", [(z, (z + m) % n_tensor) for z in range(n_tensor)]
+                )
+                for m in range(1, n_tensor)
+            ]
         return mark
 
     work = []
     cuts = [c for c in (1, 2, 3, 4, 6, 8, 9) if c < count] + [count]
     for lo, hi in zip(cuts[:-1], cuts[1:]):
-        work.append((0, functools.partial(send_half, lo, hi)))
+        work.append((1, functools.partial(send_half, lo, hi)))
     for k in range(count):
         work.append(((k + chips) * ROUNDS - 1, functools.partial(consume, k)))
+
+    def latest(t, r):
+        return [held[q][t] if q <= r else held[q][t - 1] for q in range(ROUNDS)]
 
     slot = 0
     for t in range(steps):
         for r in range(ROUNDS):
-            if t < steps - 1:
+            if t < steps - 2:
                 part, at = sib_parts[min(t, count - 1)]
                 held[r][t] = inject(t, at, r, half, n_dp, round_owner, vals, part, got[r], [mark])
             else:
                 held[r][t] = got[r]
-            if t < steps - 1:
+            if t < steps - 2:
                 got[r] = lax.ppermute(held[r][t], "dp", along)
+            elif t == steps - 2:
+                last = trim(held[r][t], valid(count - 1 - groups, width), [mark])
+                got[r] = lax.ppermute(last, "dp", along)
+            if slot in (0, 2, 4, 9, 13):
+                send_next(latest(t, r))
             if work and work[0][0] <= slot:
-                mark = work.pop(0)[1]([held[r][t]])
+                mark = work.pop(0)[1](latest(t, r))
             slot += 1
     while work:
         mark = work.pop(0)[1]([mark])
 
-    block = 2 * cand_rows // n_tensor
-    samples = cand_lengths.shape[1]
-    segs = jnp.concatenate(
-        [
-            segment_of(cand_lengths[0], cand_rows),
-            segment_of(sib_lengths[0], cand_rows) + samples,
-        ]
-    )
-    segs = lax.dynamic_slice_in_dim(segs, at_z * block, block, 0)
-    cand_hot = (jnp.arange(2 * samples, dtype=jnp.int32)[:, None] == segs[None, :]).astype(
-        jnp.float32
-    )
-    hots, weights = [], []
-    for r in range(ROUNDS):
-        lengths = lax.dynamic_index_in_dim(val_lengths, round_owner[r], 0, keepdims=False)
-        seg = lax.dynamic_slice_in_dim(segment_of(lengths, val_rows), core * half, half, 0)
-        hots.append((seg[:, None] == jnp.arange(128, dtype=jnp.int32)[None, :]).astype(jnp.float32))
-        weights.append(
-            1.0
-            / math.sqrt(D * FF)
-            / jnp.sqrt(
-                cand_lengths[0].astype(jnp.float32)[:, None]
-                * lengths.astype(jnp.float32)[None, :]
-            )
-        )
-    partial = score(
-        cand_hot, jnp.stack(hots, axis=0), parts["gu_h"], parts["x"], parts["dy"]
-    )
-    total = partial[:, :samples] + lax.ppermute(partial[:, samples:], "dp", across)
+    mine, theirs = score(
+        cand_rows, cand_lengths, sib_lengths, val_lengths, round_owner,
+        parts["gu_h"], parts["x"], parts["dy"],
+    )
+    total = mine + lax.ppermute(theirs, "dp", across)
     turned = [
         lax.ppermute(total, "tensor", [(z, (z + m) % n_tensor) for z in range(n_tensor)])
         for m in range(1, n_tensor)
     ]
     for piece in turned:
         total = total + piece
-    return total[:, :, : val_lengths.shape[1]] * jnp.stack(weights, axis=0)
+    return total[:, :, : val_lengths.shape[1]]
 
 
 def solution(mesh):

time: 255 us -> 243 us (0.953)
  starting transfers between devices: 80.5 us -> 54.3 us
  Pallas kernels: 115 us -> 128 us
  waiting for transfers between devices: 46.8 us -> 58.5 us
  other arithmetic: 7.1 us -> 1.3 us
  between operations: 4.3 us -> 0.55 us
    ppermute x24 -> x22, starting transfers between devices: 60.2 us -> 31.9 us  [local(): got[r] = lax.ppermute(held[r][t], 'dp', along)]
    pallas_call x24 -> x22, Pallas kernels: 23.3 us -> 38 us  [inject(): pl.pallas_call(functools.partial(inject_body, t, at, r, groups, width, n_...]
    ppermute x24 -> x22, waiting for transfers between devices: 39.5 us -> 47 us  [local(): got[r] = lax.ppermute(held[r][t], 'dp', along)]
    ppermute x15 -> x17, waiting for transfers between devices: 2.29 us -> 6.27 us  [the longest x9 4.87 us: consume(): lax.ppermute(pieces[m], 'tensor', [(z, (z + m) % n_tensor) for z in range...]
    pallas_call x4 -> x3, Pallas kernels: 8.21 us -> 5.98 us  [the longest x2 3.45 us: trim(): pl.pallas_call(trim_body, in_specs=[IN_HBM] + [ANYWHERE] * len(deps), out...]
    ppermute x15 -> x17, starting transfers between devices: 15.5 us -> 17.6 us  [the longest x9 14.4 us: consume(): lax.ppermute(pieces[m], 'tensor', [(z, (z + m) % n_tensor) for z in range...]
  transfers between devices with their start and end apart: 51 -> 51, of which waited for: 21 -> 20; matrix products, arithmetic and copies ran while one was open for 3% -> 0% of each run, Pallas kernels for 43% -> 50%
where the time goes in v3:
time: 243 us; the launch traced here: 242 us
  Pallas kernels  128 us (53%)
  waiting for transfers between devices  58.5 us (24%)
  starting transfers between devices  54.3 us (22%)
    pallas_call x10, Pallas kernels, use(): pl.pallas_call(body, in_specs=[IN_SMEM] + [IN_HBM] * (2 * n_cand + n_held...  64 us
    ppermute x22, waiting for transfers between devices, local(): got[r] = lax.ppermute(held[r][t], 'dp', along)  47 us
    pallas_call x22, Pallas kernels, inject(): pl.pallas_call(functools.partial(inject_body, t, at, r, groups, width, n_...  38 us
    ppermute x22, starting transfers between devices, local(): got[r] = lax.ppermute(held[r][t], 'dp', along)  31.9 us
    pallas_call x8, Pallas kernels, pack(): pl.pallas_call(functools.partial(pack_body, groups, width, first), grid_s...  19.8 us
    ppermute x9, starting transfers between devices, consume(): lax.ppermute(pieces[m], 'tensor', [(z, (z + m) % n_tensor) for z in range...  14.4 us
    ppermute x9, waiting for transfers between devices, consume(): lax.ppermute(pieces[m], 'tensor', [(z, (z + m) % n_tensor) for z in range...  4.87 us
  transfers between devices with their start and end apart: 51, of which 20 were waited for; matrix products, arithmetic and copies ran while one was open for 0% of the time, Pallas kernels for 50%

profile of v3, /device:TPU:0, one launch (start us, length us, event | category | flops | bytes accessed | tf_op | source)
XLA Modules:
  0.0 242.3 jit_solution(6661290084771723225)
XLA Ops:
  13.2 2.9 %collective-permute-start.4 = (bf16[128,2688]{1,0:T(8,128)(2,1)}, bf16[128,2688]{1,0:T(8,128)(2,1)}, u32[]{:S(2)}, u32[]{:S(2)}) collective-permute-start(bf16[128,2688]{1,0:T(8,128)(2,1)} %shard_map.128.rest_0_.refs_6_), channel_id=1, source_target_pairs={{0,8},{4,20},{8,24},{12,4},{24,16},{28,12},{16,0},{20,28},{1,9},{5... | collective-permute-start | bytes 2064392 | tf_op jit(solution)/shard_map/ppermute | solution.py:542
  16.1 9.3 %collective-permute-done.4.rest_0_ = bf16[128,2688]{1,0:T(8,128)(2,1)} collective-permute-done((bf16[128,2688]{1,0:T(8,128)(2,1)}, bf16[128,2688]{1,0:T(8,128)(2,1)}, u32[]{:S(2)}, u32[]{:S(2)}) %collective-permute-start.4) | collective-permute-done | bytes 688160 | tf_op jit(solution)/shard_map/ppermute | solution.py:542
  26.3 3.9 %collective-permute-start.8 = (bf16[128,2688]{1,0:T(8,128)(2,1)}, bf16[128,2688]{1,0:T(8,128)(2,1)}, u32[]{:S(2)}, u32[]{:S(2)}) collective-permute-start(bf16[128,2688]{1,0:T(8,128)(2,1)} %shard_map.129.rest_1_.refs_10_), channel_id=1, source_target_pairs={{0,8},{4,20},{8,24},{12,4},{24,16},{28,12},{16,0},{20,28},{1,9},{5... | collective-permute-start | bytes 2064392 | tf_op jit(solution)/shard_map/ppermute | solution.py:542
  32.9 6.0 %collective-permute-done.8.rest_0_ = bf16[128,2688]{1,0:T(8,128)(2,1)} collective-permute-done((bf16[128,2688]{1,0:T(8,128)(2,1)}, bf16[128,2688]{1,0:T(8,128)(2,1)}, u32[]{:S(2)}, u32[]{:S(2)}) %collective-permute-start.8) | collective-permute-done | bytes 688160 | tf_op jit(solution)/shard_map/ppermute | solution.py:542
  47.2 4.3 %collective-permute-start.10 = (bf16[128,2688]{1,0:T(8,128)(2,1)}, bf16[128,2688]{1,0:T(8,128)(2,1)}, u32[]{:S(2)}, u32[]{:S(2)}) collective-permute-start(bf16[128,2688]{1,0:T(8,128)(2,1)} %shard_map.133.rest_1_.refs_11_.refs_10_), channel_id=1, source_target_pairs={{0,8},{4,20},{8,24},{12,4},{24,16},{28,12},{16,0},{20,28},{1,9},{5... | collective-permute-start | bytes 2064392 | tf_op jit(solution)/shard_map/ppermute | solution.py:542
  54.9 5.5 %collective-permute-done.10.rest_0_ = bf16[128,2688]{1,0:T(8,128)(2,1)} collective-permute-done((bf16[128,2688]{1,0:T(8,128)(2,1)}, bf16[128,2688]{1,0:T(8,128)(2,1)}, u32[]{:S(2)}, u32[]{:S(2)}) %collective-permute-start.10) | collective-permute-done | bytes 688160 | tf_op jit(solution)/shard_map/ppermute | solution.py:542
  68.5 4.4 %collective-permute-start.15 = (bf16[128,2688]{1,0:T(8,128)(2,1)}, bf16[128,2688]{1,0:T(8,128)(2,1)}, u32[]{:S(2)}, u32[]{:S(2)}) collective-permute-start(bf16[128,2688]{1,0:T(8,128)(2,1)} %shard_map.139.rest_0_.refs_9_.refs_8_.refs_7_.refs_6_), channel_id=1, source_target_pairs={{0,8},{4,20},{8,24},{12,4},{24,16},{28,12},{16,0},{20,28},{1,9},{5... | collective-permute-start | bytes 2064392 | tf_op jit(solution)/shard_map/ppermute | solution.py:542
  83.3 4.3 %collective-permute-start.17 = (bf16[128,2688]{1,0:T(8,128)(2,1)}, bf16[128,2688]{1,0:T(8,128)(2,1)}, u32[]{:S(2)}, u32[]{:S(2)}) collective-permute-start(bf16[128,2688]{1,0:T(8,128)(2,1)} %shard_map.143.refs_14_.refs_9_.refs_15_.refs_8_.refs_7_.refs_6_), channel_id=1, source_target_pairs={{0,8},{4,20},{8,24},{12,4},{24,16},{28,12},{16,0},{20,28},{1,9},{5... | collective-permute-start | bytes 2064392 | tf_op jit(solution)/shard_map/ppermute | solution.py:542
  87.6 6.3 %shard_map.144 = (f32[2,512,256]{2,1,0:T(8,128)}, f32[8,128]{1,0:T(8,128)}) custom-call(s32[2]{0:T(128)} %owner.65, bf16[256,7168]{1,0:T(8,128)(2,1)} %refs_0_.17, bf16[256,7168]{1,0:T(8,128)(2,1)} %refs_1_.17, bf16[256,7168]{1,0:T(8,128)(2,1)} %refs_2_.15, bf16[256,7168]{1,0:T(8,128)(2,1)} %collective-permute-done.2.refs_3_, ...), custom_call_target="tpu_custom_call" | custom-call | flops 704643072 | bytes 5177344 | tf_op jit(solution)/shard_map/pallas_call | solution.py:348
  96.7 6.8 %shard_map.146 = (f32[2,512,256]{2,1,0:T(8,128)}, f32[8,128]{1,0:T(8,128)}) custom-call(s32[2]{0:T(128)} %owner.65, bf16[256,7168]{1,0:T(8,128)(2,1)} %refs_0_.17, bf16[256,7168]{1,0:T(8,128)(2,1)} %refs_1_.17, bf16[256,7168]{1,0:T(8,128)(2,1)} %refs_2_.15, bf16[256,7168]{1,0:T(8,128)(2,1)} %collective-permute-done.2.refs_3_, ...), custom_call_target="tpu_custom_call" | custom-call | flops 704643072 | bytes 5177344 | tf_op jit(solution)/shard_map/pallas_call | solution.py:348
  104.5 3.5 %collective-permute-done.20.rest_0_ = bf16[128,2688]{1,0:T(8,128)(2,1)} collective-permute-done((bf16[128,2688]{1,0:T(8,128)(2,1)}, bf16[128,2688]{1,0:T(8,128)(2,1)}, u32[]{:S(2)}, u32[]{:S(2)}) %collective-permute-start.20) | collective-permute-done | bytes 688160 | tf_op jit(solution)/shard_map/ppermute | solution.py:542
  110.7 6.8 %shard_map.149 = (f32[2,512,256]{2,1,0:T(8,128)}, f32[8,128]{1,0:T(8,128)}) custom-call(s32[2]{0:T(128)} %owner.65, bf16[256,7168]{1,0:T(8,128)(2,1)} %refs_0_.17, bf16[256,7168]{1,0:T(8,128)(2,1)} %refs_1_.17, bf16[256,7168]{1,0:T(8,128)(2,1)} %refs_2_.15, bf16[256,7168]{1,0:T(8,128)(2,1)} %collective-permute-done.2.refs_3_, ...), custom_call_target="tpu_custom_call" | custom-call | flops 704643072 | bytes 5177344 | tf_op jit(solution)/shard_map/pallas_call | solution.py:348
  118.9 4.2 %collective-permute-done.22.rest_0_ = bf16[128,2688]{1,0:T(8,128)(2,1)} collective-permute-done((bf16[128,2688]{1,0:T(8,128)(2,1)}, bf16[128,2688]{1,0:T(8,128)(2,1)}, u32[]{:S(2)}, u32[]{:S(2)}) %collective-permute-start.22) | collective-permute-done | bytes 688160 | tf_op jit(solution)/shard_map/ppermute | solution.py:542
  125.9 6.8 %shard_map.152 = (f32[2,512,256]{2,1,0:T(8,128)}, f32[8,128]{1,0:T(8,128)}) custom-call(s32[2]{0:T(128)} %owner.65, bf16[256,7168]{1,0:T(8,128)(2,1)} %refs_0_.17, bf16[256,7168]{1,0:T(8,128)(2,1)} %refs_1_.17, bf16[256,7168]{1,0:T(8,128)(2,1)} %refs_2_.15, bf16[256,7168]{1,0:T(8,128)(2,1)} %collective-permute-done.2.refs_3_, ...), custom_call_target="tpu_custom_call" | custom-call | flops 704643072 | bytes 5177344 | tf_op jit(solution)/shard_map/pallas_call | solution.py:348
  140.6 6.8 %shard_map.155 = (f32[2,512,256]{2,1,0:T(8,128)}, f32[8,128]{1,0:T(8,128)}) custom-call(s32[2]{0:T(128)} %owner.65, bf16[256,7168]{1,0:T(8,128)(2,1)} %refs_0_.17, bf16[256,7168]{1,0:T(8,128)(2,1)} %refs_1_.17, bf16[256,7168]{1,0:T(8,128)(2,1)} %refs_2_.15, bf16[256,7168]{1,0:T(8,128)(2,1)} %collective-permute-done.2.refs_3_, ...), custom_call_target="tpu_custom_call" | custom-call | flops 704643072 | bytes 5177344 | tf_op jit(solution)/shard_map/pallas_call | solution.py:348
  149.7 2.8 %collective-permute-done.28.rest_0_ = bf16[128,2688]{1,0:T(8,128)(2,1)} collective-permute-done((bf16[128,2688]{1,0:T(8,128)(2,1)}, bf16[128,2688]{1,0:T(8,128)(2,1)}, u32[]{:S(2)}, u32[]{:S(2)}) %collective-permute-start.28) | collective-permute-done | bytes 688160 | tf_op jit(solution)/shard_map/ppermute | solution.py:542
  155.5 6.8 %shard_map.158 = (f32[2,512,256]{2,1,0:T(8,128)}, f32[8,128]{1,0:T(8,128)}) custom-call(s32[2]{0:T(128)} %owner.65, bf16[256,7168]{1,0:T(8,128)(2,1)} %refs_0_.17, bf16[256,7168]{1,0:T(8,128)(2,1)} %refs_1_.17, bf16[256,7168]{1,0:T(8,128)(2,1)} %refs_2_.15, bf16[256,7168]{1,0:T(8,128)(2,1)} %collective-permute-done.2.refs_3_, ...), custom_call_target="tpu_custom_call" | custom-call | flops 704643072 | bytes 5177344 | tf_op jit(solution)/shard_map/pallas_call | solution.py:348
  169.9 6.8 %shard_map.161 = (f32[2,512,256]{2,1,0:T(8,128)}, f32[8,128]{1,0:T(8,128)}) custom-call(s32[2]{0:T(128)} %owner.65, bf16[256,7168]{1,0:T(8,128)(2,1)} %refs_0_.17, bf16[256,7168]{1,0:T(8,128)(2,1)} %refs_1_.17, bf16[256,7168]{1,0:T(8,128)(2,1)} %refs_2_.15, bf16[256,7168]{1,0:T(8,128)(2,1)} %collective-permute-done.2.refs_3_, ...), custom_call_target="tpu_custom_call" | custom-call | flops 704643072 | bytes 5177344 | tf_op jit(solution)/shard_map/pallas_call | solution.py:348
  178.5 3.5 %collective-permute-done.31.rest_0_ = bf16[128,2688]{1,0:T(8,128)(2,1)} collective-permute-done((bf16[128,2688]{1,0:T(8,128)(2,1)}, bf16[128,2688]{1,0:T(8,128)(2,1)}, u32[]{:S(2)}, u32[]{:S(2)}) %collective-permute-start.31) | collective-permute-done | bytes 688160 | tf_op jit(solution)/shard_map/ppermute | solution.py:542
  185.2 6.9 %shard_map.164 = (f32[2,128,256]{2,1,0:T(8,128)}, bf16[2,128,256]{2,1,0:T(8,128)(2,1)}, bf16[2,128,256]{2,1,0:T(8,128)(2,1)}, bf16[2,128,256]{2,1,0:T(8,128)(2,1)}, f32[8,128]{1,0:T(8,128)}) custom-call(s32[2]{0:T(128)} %owner.65, bf16[256,7168]{1,0:T(8,128)(2,1)} %refs_0_.17, bf16[256,7168]{1,0:T(8,128)(2,1)} %refs_1_.17, bf16[256,7168]{1,0:T(8,128)(2,1)} %refs_2_.15, ...), custom_call_target="tpu_custom_call" | custom-call | flops 704643072 | bytes 5177344 | tf_op jit(solution)/shard_map/pallas_call | solution.py:348
  206.4 5.4 %shard_map.165 = (f32[1,128,256]{2,1,0:T(8,128)}, bf16[1,128,256]{2,1,0:T(8,128)(2,1)}, bf16[1,128,256]{2,1,0:T(8,128)(2,1)}, bf16[1,128,256]{2,1,0:T(8,128)(2,1...) custom-call(s32[2]{0:T(128)} %owner.65, bf16[256,2048]{1,0:T(8,128)(2,1)} %refs_0_.19, bf16[256,2048]{1,0:T(8,128)(2,1)} %refs_1_.19, ...), custom_call_target="tpu_custom_call" | custom-call | flops 704643072 | bytes 5177344 | tf_op jit(solution)/shard_map/pallas_call | solution.py:348
  212.7 4.5 %shard_map.168 = (f32[1,128,256]{2,1,0:T(8,128)}, bf16[1,128,256]{2,1,0:T(8,128)(2,1)}, bf16[1,128,256]{2,1,0:T(8,128)(2,1)}, bf16[1,128,256]{2,1,0:T(8,128)(2,1)}, f32[8,128]{1,0:T(8,128)}) custom-call(s32[2]{0:T(128)} %owner.65, bf16[256,2048]{1,0:T(8,128)(2,1)} %refs_0_.19, bf16[256,2048]{1,0:T(8,128)(2,1)} %refs_1_.19, ...), custom_call_target="tpu_custom_call" | custom-call | flops 704643072 | bytes 5177344 | tf_op jit(solution)/shard_map/pallas_call | solution.py:348
  217.6 2.9 %collective-permute-start.41 = (bf16[1,128,256]{2,1,0:T(8,128)(2,1)}, bf16[1,128,256]{2,1,0:T(8,128)(2,1)}, u32[]{:S(2)}, u32[]{:S(2)}) collective-permute-start(bf16[1,128,256]{2,1,0:T(8,128)(2,1)} %get-tuple-element.98), channel_id=1, source_target_pairs={{0,3},{1,0},{2,1},{3,2},{4,7},{5,4},{6,5},{7,6},{8,11},{9,8},{10,9... | collective-permute-start | bytes 196616 | tf_op jit(solution)/shard_map/ppermute | solution.py:516
  222.5 2.9 %collective-permute-start.46 = (bf16[1,128,256]{2,1,0:T(8,128)(2,1)}, bf16[1,128,256]{2,1,0:T(8,128)(2,1)}, u32[]{:S(2)}, u32[]{:S(2)}) collective-permute-start(bf16[1,128,256]{2,1,0:T(8,128)(2,1)} %get-tuple-element.104), channel_id=1, source_target_pairs={{0,3},{1,0},{2,1},{3,2},{4,7},{5,4},{6,5},{7,6},{8,11},{9,8},{10,9... | collective-permute-start | bytes 196616 | tf_op jit(solution)/shard_map/ppermute | solution.py:516
  (127 shorter events, 117.6 us)
Async XLA Ops:
  7.6 18.5 %collective-permute-start.2 = (bf16[256,7168]{1,0:T(8,128)(2,1)}, bf16[256,7168]{1,0:T(8,128)(2,1)}, u32[]{:S(2)}, u32[]{:S(2)}) collective-permute-start(bf16[256,7168]{1,0:T(8,128)(2,1)} %refs_0_.17), channel_id=1, source_target_pairs={{0,4},{4,0},{8,12},{12,8},{16,20},{20,16},{24,28},{28,24},{1,5},{5... | collective-permute-start | bytes 11010056 | tf_op jit(solution)/shard_map/ppermute | solution.py:499
  26.2 20.9 %collective-permute-start.5 = (bf16[256,7168]{1,0:T(8,128)(2,1)}, bf16[256,7168]{1,0:T(8,128)(2,1)}, u32[]{:S(2)}, u32[]{:S(2)}) collective-permute-start(bf16[256,7168]{1,0:T(8,128)(2,1)} %refs_1_.17), channel_id=1, source_target_pairs={{0,4},{4,0},{8,12},{12,8},{16,20},{20,16},{24,28},{28,24},{1,5},{5... | collective-permute-start | bytes 11010056 | tf_op jit(solution)/shard_map/ppermute | solution.py:499
  32.5 13.8 %collective-permute-start.7 = (bf16[128,2688]{1,0:T(8,128)(2,1)}, bf16[128,2688]{1,0:T(8,128)(2,1)}, u32[]{:S(2)}, u32[]{:S(2)}) collective-permute-start(bf16[128,2688]{1,0:T(8,128)(2,1)} %shard_map.131.rest_0_.refs_7_.refs_6_), channel_id=1, source_target_pairs={{0,8},{4,20},{8,24},{12,4},{24,16},{28,12},{16,0},{20,28},{1,9},{5... | collective-permute-start | bytes 2064392 | tf_op jit(solution)/shard_map/ppermute | solution.py:542
  47.1 40.5 %collective-permute-start.9 = (bf16[256,7168]{1,0:T(8,128)(2,1)}, bf16[256,7168]{1,0:T(8,128)(2,1)}, u32[]{:S(2)}, u32[]{:S(2)}) collective-permute-start(bf16[256,7168]{1,0:T(8,128)(2,1)} %refs_2_.15), channel_id=1, source_target_pairs={{0,4},{4,0},{8,12},{12,8},{16,20},{20,16},{24,28},{28,24},{1,5},{5... | collective-permute-start | bytes 11010056 | tf_op jit(solution)/shard_map/ppermute | solution.py:499
  51.6 14.9 %collective-permute-start.13 = (bf16[1,128,2688]{2,1,0:T(8,128)(2,1)}, bf16[1,128,2688]{2,1,0:T(8,128)(2,1)}, u32[]{:S(2)}, u32[]{:S(2)}) collective-permute-start(bf16[1,128,2688]{2,1,0:T(8,128)(2,1)} %get-tuple-element.69), channel_id=1, source_target_pairs={{0,4},{4,0},{8,12},{12,8},{16,20},{20,16},{24,28},{28,24},{1,5},{5... | collective-permute-start | bytes 2064392 | tf_op jit(solution)/shard_map/ppermute | solution.py:488
  51.6 16.1 %collective-permute-start.14 = (bf16[128,2688]{1,0:T(8,128)(2,1)}, bf16[128,2688]{1,0:T(8,128)(2,1)}, u32[]{:S(2)}, u32[]{:S(2)}) collective-permute-start(bf16[128,2688]{1,0:T(8,128)(2,1)} %shard_map.135.rest_0_.refs_8_.refs_7_.refs_6_), channel_id=1, source_target_pairs={{0,8},{4,20},{8,24},{12,4},{24,16},{28,12},{16,0},{20,28},{1,9},{5... | collective-permute-start | bytes 2064392 | tf_op jit(solution)/shard_map/ppermute | solution.py:542
  54.8 27.7 %collective-permute-start.12 = (bf16[2,128,2688]{2,1,0:T(8,128)(2,1)}, bf16[2,128,2688]{2,1,0:T(8,128)(2,1)}, u32[]{:S(2)}, u32[]{:S(2)}) collective-permute-start(bf16[2,128,2688]{2,1,0:T(8,128)(2,1)} %get-tuple-element.68), channel_id=1, source_target_pairs={{0,4},{4,0},{8,12},{12,8},{16,20},{20,16},{24,28},{28,24},{1,5},{5... | collective-permute-start | bytes 4128776 | tf_op jit(solution)/shard_map/ppermute | solution.py:488
  68.5 13.9 %collective-permute-start.15 = (bf16[128,2688]{1,0:T(8,128)(2,1)}, bf16[128,2688]{1,0:T(8,128)(2,1)}, u32[]{:S(2)}, u32[]{:S(2)}) collective-permute-start(bf16[128,2688]{1,0:T(8,128)(2,1)} %shard_map.139.rest_0_.refs_9_.refs_8_.refs_7_.refs_6_), channel_id=1, source_target_pairs={{0,8},{4,20},{8,24},{12,4},{24,16},{28,12},{16,0},{20,28},{1,9},{5... | collective-permute-start | bytes 2064392 | tf_op jit(solution)/shard_map/ppermute | solution.py:542
  77.9 16.0 %collective-permute-start.18 = (bf16[128,2688]{1,0:T(8,128)(2,1)}, bf16[128,2688]{1,0:T(8,128)(2,1)}, u32[]{:S(2)}, u32[]{:S(2)}) collective-permute-start(bf16[128,2688]{1,0:T(8,128)(2,1)} %shard_map.141.rest_1_.refs_13_.refs_15_.refs_12_.refs_11_.refs_10_), channel_id=1, source_target_pairs={{0,8},{4,20},{8,24},{12,4},{24,16},{28,12},{16,0},{20,28},{1,9},{5... | collective-permute-start | bytes 2064392 | tf_op jit(solution)/shard_map/ppermute | solution.py:542
  78.5 39.1 %collective-permute-start.11 = (bf16[2,128,2688]{2,1,0:T(8,128)(2,1)}, bf16[2,128,2688]{2,1,0:T(8,128)(2,1)}, u32[]{:S(2)}, u32[]{:S(2)}) collective-permute-start(bf16[2,128,2688]{2,1,0:T(8,128)(2,1)} %get-tuple-element.67), channel_id=1, source_target_pairs={{0,4},{4,0},{8,12},{12,8},{16,20},{20,16},{24,28},{28,24},{1,5},{5... | collective-permute-start | bytes 4128776 | tf_op jit(solution)/shard_map/ppermute | solution.py:488
  83.3 20.2 %collective-permute-start.17 = (bf16[128,2688]{1,0:T(8,128)(2,1)}, bf16[128,2688]{1,0:T(8,128)(2,1)}, u32[]{:S(2)}, u32[]{:S(2)}) collective-permute-start(bf16[128,2688]{1,0:T(8,128)(2,1)} %shard_map.143.refs_14_.refs_9_.refs_15_.refs_8_.refs_7_.refs_6_), channel_id=1, source_target_pairs={{0,8},{4,20},{8,24},{12,4},{24,16},{28,12},{16,0},{20,28},{1,9},{5... | collective-permute-start | bytes 2064392 | tf_op jit(solution)/shard_map/ppermute | solution.py:542
  118.4 14.3 %collective-permute-start.21 = (bf16[128,2688]{1,0:T(8,128)(2,1)}, bf16[128,2688]{1,0:T(8,128)(2,1)}, u32[]{:S(2)}, u32[]{:S(2)}) collective-permute-start(bf16[128,2688]{1,0:T(8,128)(2,1)} %shard_map.150.refs_9_.refs_15_.refs_8_.refs_7_.refs_6_), channel_id=1, source_target_pairs={{0,8},{4,20},{8,24},{12,4},{24,16},{28,12},{16,0},{20,28},{1,9},{5... | collective-permute-start | bytes 2064392 | tf_op jit(solution)/shard_map/ppermute | solution.py:542
  125.8 21.6 %collective-permute-start.23 = (bf16[1,128,2688]{2,1,0:T(8,128)(2,1)}, bf16[1,128,2688]{2,1,0:T(8,128)(2,1)}, u32[]{:S(2)}, u32[]{:S(2)}) collective-permute-start(bf16[1,128,2688]{2,1,0:T(8,128)(2,1)} %get-tuple-element.80), channel_id=1, source_target_pairs={{0,4},{4,0},{8,12},{12,8},{16,20},{20,16},{24,28},{28,24},{1,5},{5... | collective-permute-start | bytes 2064392 | tf_op jit(solution)/shard_map/ppermute | solution.py:488
  133.5 13.9 %collective-permute-start.24 = (bf16[128,2688]{1,0:T(8,128)(2,1)}, bf16[128,2688]{1,0:T(8,128)(2,1)}, u32[]{:S(2)}, u32[]{:S(2)}) collective-permute-start(bf16[128,2688]{1,0:T(8,128)(2,1)} %shard_map.153.refs_9_.refs_15_.refs_8_.refs_7_.refs_6_), channel_id=1, source_target_pairs={{0,8},{4,20},{8,24},{12,4},{24,16},{28,12},{16,0},{20,28},{1,9},{5... | collective-permute-start | bytes 2064392 | tf_op jit(solution)/shard_map/ppermute | solution.py:542
  140.5 21.8 %collective-permute-start.26 = (bf16[1,128,2688]{2,1,0:T(8,128)(2,1)}, bf16[1,128,2688]{2,1,0:T(8,128)(2,1)}, u32[]{:S(2)}, u32[]{:S(2)}) collective-permute-start(bf16[1,128,2688]{2,1,0:T(8,128)(2,1)} %get-tuple-element.83), channel_id=1, source_target_pairs={{0,4},{4,0},{8,12},{12,8},{16,20},{20,16},{24,28},{28,24},{1,5},{5... | collective-permute-start | bytes 2064392 | tf_op jit(solution)/shard_map/ppermute | solution.py:488
  148.3 14.0 %collective-permute-start.27 = (bf16[128,2688]{1,0:T(8,128)(2,1)}, bf16[128,2688]{1,0:T(8,128)(2,1)}, u32[]{:S(2)}, u32[]{:S(2)}) collective-permute-start(bf16[128,2688]{1,0:T(8,128)(2,1)} %shard_map.156.refs_9_.refs_15_.refs_8_.refs_7_.refs_4_), channel_id=1, source_target_pairs={{0,8},{4,20},{8,24},{12,4},{24,16},{28,12},{16,0},{20,28},{1,9},{5... | collective-permute-start | bytes 2064392 | tf_op jit(solution)/shard_map/ppermute | solution.py:542
  155.4 14.4 %collective-permute-start.35 = (bf16[256,2048]{1,0:T(8,128)(2,1)}, bf16[256,2048]{1,0:T(8,128)(2,1)}, u32[]{:S(2)}, u32[]{:S(2)}) collective-permute-start(bf16[256,2048]{1,0:T(8,128)(2,1)} %refs_0_.19), channel_id=1, source_target_pairs={{0,4},{4,0},{8,12},{12,8},{16,20},{20,16},{24,28},{28,24},{1,5},{5... | collective-permute-start | bytes 3145736 | tf_op jit(solution)/shard_map/ppermute | solution.py:499
  169.9 35.2 %collective-permute-start.36 = (bf16[256,2048]{1,0:T(8,128)(2,1)}, bf16[256,2048]{1,0:T(8,128)(2,1)}, u32[]{:S(2)}, u32[]{:S(2)}) collective-permute-start(bf16[256,2048]{1,0:T(8,128)(2,1)} %refs_1_.19), channel_id=1, source_target_pairs={{0,4},{4,0},{8,12},{12,8},{16,20},{20,16},{24,28},{28,24},{1,5},{5... | collective-permute-start | bytes 3145736 | tf_op jit(solution)/shard_map/ppermute | solution.py:499
  177.5 14.6 %collective-permute-start.37 = (bf16[128,2688]{1,0:T(8,128)(2,1)}, bf16[128,2688]{1,0:T(8,128)(2,1)}, u32[]{:S(2)}, u32[]{:S(2)}) collective-permute-start(bf16[128,2688]{1,0:T(8,128)(2,1)} %shard_map.162.refs_9_.refs_15_.refs_6_.refs_5_), channel_id=1, source_target_pairs={{0,8},{4,20},{8,24},{12,4},{24,16},{28,12},{16,0},{20,28},{1,9},{5... | collective-permute-start | bytes 2064392 | tf_op jit(solution)/shard_map/ppermute | solution.py:542
  182.8 14.0 %collective-permute-start.38 = (bf16[128,2688]{1,0:T(8,128)(2,1)}, bf16[128,2688]{1,0:T(8,128)(2,1)}, u32[]{:S(2)}, u32[]{:S(2)}) collective-permute-start(bf16[128,2688]{1,0:T(8,128)(2,1)} %shard_map.163.refs_13_.refs_16_.refs_10_.refs_9_), channel_id=1, source_target_pairs={{0,8},{4,20},{8,24},{12,4},{24,16},{28,12},{16,0},{20,28},{1,9},{5... | collective-permute-start | bytes 2064392 | tf_op jit(solution)/shard_map/ppermute | solution.py:542
  193.9 17.9 %collective-permute-start.42 = (bf16[128,1408]{1,0:T(8,128)(2,1)}, bf16[128,1408]{1,0:T(8,128)(2,1)}, u32[]{:S(2)}, u32[]{:S(2)}) collective-permute-start(bf16[128,1408]{1,0:T(8,128)(2,1)} %shard_map.166), channel_id=1, source_target_pairs={{0,8},{4,20},{8,24},{12,4},{24,16},{28,12},{16,0},{20,28},{1,9},{5... | collective-permute-start | bytes 1081352 | tf_op jit(solution)/shard_map/ppermute | solution.py:545
  200.9 16.7 %collective-permute-start.32 = (bf16[2,128,256]{2,1,0:T(8,128)(2,1)}, bf16[2,128,256]{2,1,0:T(8,128)(2,1)S(1)}, u32[]{:S(2)}, u32[]{:S(2)}) collective-permute-start(bf16[2,128,256]{2,1,0:T(8,128)(2,1)} %get-tuple-element.90), channel_id=1, source_target_pairs={{0,1},{1,2},{2,3},{3,0},{4,5},{5,6},{6,7},{7,4},{8,9},{9,10},{10,1... | collective-permute-start | bytes 393224 | tf_op jit(solution)/shard_map/ppermute | solution.py:516
  202.5 18.0 %collective-permute-start.33 = (bf16[2,128,256]{2,1,0:T(8,128)(2,1)}, bf16[2,128,256]{2,1,0:T(8,128)(2,1)}, u32[]{:S(2)}, u32[]{:S(2)}) collective-permute-start(bf16[2,128,256]{2,1,0:T(8,128)(2,1)} %get-tuple-element.91), channel_id=1, source_target_pairs={{0,2},{1,3},{2,0},{3,1},{4,6},{5,7},{6,4},{7,5},{8,10},{9,11},{10,... | collective-permute-start | bytes 393224 | tf_op jit(solution)/shard_map/ppermute | solution.py:516
  205.1 16.0 %collective-permute-start.34 = (bf16[2,128,256]{2,1,0:T(8,128)(2,1)}, bf16[2,128,256]{2,1,0:T(8,128)(2,1)}, u32[]{:S(2)}, u32[]{:S(2)}) collective-permute-start(bf16[2,128,256]{2,1,0:T(8,128)(2,1)} %get-tuple-element.92), channel_id=1, source_target_pairs={{0,3},{1,0},{2,1},{3,2},{4,7},{5,4},{6,5},{7,6},{8,11},{9,8},{10,9... | collective-permute-start | bytes 393224 | tf_op jit(solution)/shard_map/ppermute | solution.py:516
  (29 other events, 270.8 us)

commit v4 on v3

--- a/solution.py
+++ b/solution.py
@@ -490,12 +490,12 @@
             sib_parts[t] = (part, t - lo)
         return mark
 
-    mark = send_half(0, 1, [])
+    mark = send_half(0, min(2, count), [])
     sib = []
 
     def send_next(deps):
         array = own[len(sib)]
-        array = lax.optimization_barrier((array, *deps, *sib[-1:]))[0]
+        array = lax.optimization_barrier((array, *deps))[0]
         sib.append(lax.ppermute(array, "dp", across))
 
     sib_lengths = lax.ppermute(cand_lengths, "dp", across)
@@ -521,7 +521,7 @@
         return mark
 
     work = []
-    cuts = [c for c in (1, 2, 3, 4, 6, 8, 9) if c < count] + [count]
+    cuts = [c for c in (2, 4, 6, 8, 9) if c < count] + [count]
     for lo, hi in zip(cuts[:-1], cuts[1:]):
         work.append((1, functools.partial(send_half, lo, hi)))
     for k in range(count):
@@ -543,10 +543,10 @@
             elif t == steps - 2:
                 last = trim(held[r][t], valid(count - 1 - groups, width), [mark])
                 got[r] = lax.ppermute(last, "dp", along)
-            if slot in (0, 2, 4, 9, 13):
-                send_next(latest(t, r))
             if work and work[0][0] <= slot:
                 mark = work.pop(0)[1](latest(t, r))
+            if slot in (1, 3, 5, 9, 13):
+                send_next([mark])
             slot += 1
     while work:
         mark = work.pop(0)[1]([mark])

time: 243 us -> 239 us (0.984)
  Pallas kernels: 128 us -> 108 us
  starting transfers between devices: 54.3 us -> 64.1 us
  waiting for transfers between devices: 58.5 us -> 64 us
    pallas_call x22, Pallas kernels: 38 us -> 21.8 us  [inject(): pl.pallas_call(functools.partial(inject_body, t, at, r, groups, width, n_...]
    ppermute x22, starting transfers between devices: 31.9 us -> 41.2 us  [local(): got[r] = lax.ppermute(held[r][t], 'dp', along)]
    ppermute x22, waiting for transfers between devices: 47 us -> 51.6 us  [local(): got[r] = lax.ppermute(held[r][t], 'dp', along)]
    pallas_call x8 -> x6, Pallas kernels: 19.8 us -> 16 us  [pack(): pl.pallas_call(functools.partial(pack_body, groups, width, first), grid_s...]
  transfers between devices with their start and end apart: 51 -> 49, of which waited for: 20 -> 20; matrix products, arithmetic and copies ran while one was open for 0% -> 0% of each run, Pallas kernels for 50% -> 42%
where the time goes in v4:
time: 239 us; the launch traced here: 238 us
  Pallas kernels  108 us (45%)
  starting transfers between devices  64.1 us (27%)
  waiting for transfers between devices  64 us (27%)
    pallas_call x10, Pallas kernels, use(): pl.pallas_call(body, in_specs=[IN_SMEM] + [IN_HBM] * (2 * n_cand + n_held...  63.9 us
    ppermute x22, waiting for transfers between devices, local(): got[r] = lax.ppermute(held[r][t], 'dp', along)  51.6 us
    ppermute x22, starting transfers between devices, local(): got[r] = lax.ppermute(held[r][t], 'dp', along)  41.2 us
    pallas_call x22, Pallas kernels, inject(): pl.pallas_call(functools.partial(inject_body, t, at, r, groups, width, n_...  21.8 us
    pallas_call x6, Pallas kernels, pack(): pl.pallas_call(functools.partial(pack_body, groups, width, first), grid_s...  16 us
    ppermute x9, starting transfers between devices, consume(): lax.ppermute(pieces[m], 'tensor', [(z, (z + m) % n_tensor) for z in range...  14.4 us
    ppermute x9, waiting for transfers between devices, consume(): lax.ppermute(pieces[m], 'tensor', [(z, (z + m) % n_tensor) for z in range...  4.87 us
  transfers between devices with their start and end apart: 49, of which 20 were waited for; matrix products, arithmetic and copies ran while one was open for 0% of the time, Pallas kernels for 42%

profile of v4, /device:TPU:0, one launch (start us, length us, event | category | flops | bytes accessed | tf_op | source)
XLA Modules:
  0.0 237.6 jit_solution(6320987620424554266)
XLA Ops:
  3.3 3.1 %collective-permute-done.1.sib = bf16[2,128,2688]{2,1,0:T(8,128)(2,1)} collective-permute-done((bf16[2,128,2688]{2,1,0:T(8,128)(2,1)}, bf16[2,128,2688]{2,1,0:T(8,128)(2,1)}, u32[]{:S(2)}, u32[]{:S(2)}) %collective-permute-start.1) | collective-permute-done | bytes 1376288 | tf_op jit(solution)/shard_map/ppermute | solution.py:488
  22.0 3.9 %collective-permute-start.7 = (bf16[128,2688]{1,0:T(8,128)(2,1)}, bf16[128,2688]{1,0:T(8,128)(2,1)}, u32[]{:S(2)}, u32[]{:S(2)}) collective-permute-start(bf16[128,2688]{1,0:T(8,128)(2,1)} %shard_map.131.rest_0_.refs_7_.refs_6_), channel_id=1, source_target_pairs={{0,8},{4,20},{8,24},{12,4},{24,16},{28,12},{16,0},{20,28},{1,9},{5... | collective-permute-start | bytes 2064392 | tf_op jit(solution)/shard_map/ppermute | solution.py:542
  39.3 4.1 %collective-permute-done.8.rest_0_ = bf16[128,2688]{1,0:T(8,128)(2,1)} collective-permute-done((bf16[128,2688]{1,0:T(8,128)(2,1)}, bf16[128,2688]{1,0:T(8,128)(2,1)}, u32[]{:S(2)}, u32[]{:S(2)}) %collective-permute-start.8) | collective-permute-done | bytes 688160 | tf_op jit(solution)/shard_map/ppermute | solution.py:542
  48.8 9.1 %collective-permute-done.14.rest_0_ = bf16[128,2688]{1,0:T(8,128)(2,1)} collective-permute-done((bf16[128,2688]{1,0:T(8,128)(2,1)}, bf16[128,2688]{1,0:T(8,128)(2,1)}, u32[]{:S(2)}, u32[]{:S(2)}) %collective-permute-start.14) | collective-permute-done | bytes 688160 | tf_op jit(solution)/shard_map/ppermute | solution.py:542
  61.4 8.8 %collective-permute-done.12.rest_0_ = bf16[128,2688]{1,0:T(8,128)(2,1)} collective-permute-done((bf16[128,2688]{1,0:T(8,128)(2,1)}, bf16[128,2688]{1,0:T(8,128)(2,1)}, u32[]{:S(2)}, u32[]{:S(2)}) %collective-permute-start.12) | collective-permute-done | bytes 688160 | tf_op jit(solution)/shard_map/ppermute | solution.py:542
  72.7 4.3 %collective-permute-start.13 = (bf16[128,2688]{1,0:T(8,128)(2,1)}, bf16[128,2688]{1,0:T(8,128)(2,1)}, u32[]{:S(2)}, u32[]{:S(2)}) collective-permute-start(bf16[128,2688]{1,0:T(8,128)(2,1)} %shard_map.139.refs_9_.refs_14_.refs_8_.refs_7_.refs_6_), channel_id=1, source_target_pairs={{0,8},{4,20},{8,24},{12,4},{24,16},{28,12},{16,0},{20,28},{1,9},{5... | collective-permute-start | bytes 2064392 | tf_op jit(solution)/shard_map/ppermute | solution.py:542
  77.0 6.3 %shard_map.141 = (f32[2,512,256]{2,1,0:T(8,128)}, f32[8,128]{1,0:T(8,128)}) custom-call(s32[2]{0:T(128)} %owner.65, bf16[256,7168]{1,0:T(8,128)(2,1)} %refs_0_.17, bf16[256,7168]{1,0:T(8,128)(2,1)} %refs_1_.17, bf16[256,7168]{1,0:T(8,128)(2,1)} %refs_2_.15, bf16[256,7168]{1,0:T(8,128)(2,1)} %collective-permute-done.2.refs_3_, ...), custom_call_target="tpu_custom_call" | custom-call | flops 704643072 | bytes 5177344 | tf_op jit(solution)/shard_map/pallas_call | solution.py:348
  84.4 4.5 %collective-permute-done.13.rest_0_ = bf16[128,2688]{1,0:T(8,128)(2,1)} collective-permute-done((bf16[128,2688]{1,0:T(8,128)(2,1)}, bf16[128,2688]{1,0:T(8,128)(2,1)}, u32[]{:S(2)}, u32[]{:S(2)}) %collective-permute-start.13) | collective-permute-done | bytes 688160 | tf_op jit(solution)/shard_map/ppermute | solution.py:542
  89.8 3.5 %collective-permute-start.15 = (bf16[128,2688]{1,0:T(8,128)(2,1)}, bf16[128,2688]{1,0:T(8,128)(2,1)}, u32[]{:S(2)}, u32[]{:S(2)}) collective-permute-start(bf16[128,2688]{1,0:T(8,128)(2,1)} %shard_map.142.refs_9_.refs_15_.refs_8_.refs_7_.refs_6_), channel_id=1, source_target_pairs={{0,8},{4,20},{8,24},{12,4},{24,16},{28,12},{16,0},{20,28},{1,9},{5... | collective-permute-start | bytes 2064392 | tf_op jit(solution)/shard_map/ppermute | solution.py:542
  93.2 6.8 %shard_map.144 = (f32[2,512,256]{2,1,0:T(8,128)}, f32[8,128]{1,0:T(8,128)}) custom-call(s32[2]{0:T(128)} %owner.65, bf16[256,7168]{1,0:T(8,128)(2,1)} %refs_0_.17, bf16[256,7168]{1,0:T(8,128)(2,1)} %refs_1_.17, bf16[256,7168]{1,0:T(8,128)(2,1)} %refs_2_.15, bf16[256,7168]{1,0:T(8,128)(2,1)} %collective-permute-done.2.refs_3_, ...), custom_call_target="tpu_custom_call" | custom-call | flops 704643072 | bytes 5177344 | tf_op jit(solution)/shard_map/pallas_call | solution.py:348
  104.5 3.4 %collective-permute-start.17 = (bf16[128,2688]{1,0:T(8,128)(2,1)}, bf16[128,2688]{1,0:T(8,128)(2,1)}, u32[]{:S(2)}, u32[]{:S(2)}) collective-permute-start(bf16[128,2688]{1,0:T(8,128)(2,1)} %shard_map.145.refs_9_.refs_15_.refs_8_.refs_7_.refs_6_), channel_id=1, source_target_pairs={{0,8},{4,20},{8,24},{12,4},{24,16},{28,12},{16,0},{20,28},{1,9},{5... | collective-permute-start | bytes 2064392 | tf_op jit(solution)/shard_map/ppermute | solution.py:542
  107.9 6.8 %shard_map.147 = (f32[2,512,256]{2,1,0:T(8,128)}, f32[8,128]{1,0:T(8,128)}) custom-call(s32[2]{0:T(128)} %owner.65, bf16[256,7168]{1,0:T(8,128)(2,1)} %refs_0_.17, bf16[256,7168]{1,0:T(8,128)(2,1)} %refs_1_.17, bf16[256,7168]{1,0:T(8,128)(2,1)} %refs_2_.15, bf16[256,7168]{1,0:T(8,128)(2,1)} %collective-permute-done.2.refs_3_, ...), custom_call_target="tpu_custom_call" | custom-call | flops 704643072 | bytes 5177344 | tf_op jit(solution)/shard_map/pallas_call | solution.py:348
  116.3 3.3 %collective-permute-done.17.rest_0_ = bf16[128,2688]{1,0:T(8,128)(2,1)} collective-permute-done((bf16[128,2688]{1,0:T(8,128)(2,1)}, bf16[128,2688]{1,0:T(8,128)(2,1)}, u32[]{:S(2)}, u32[]{:S(2)}) %collective-permute-start.17) | collective-permute-done | bytes 688160 | tf_op jit(solution)/shard_map/ppermute | solution.py:542
  122.9 6.8 %shard_map.150 = (f32[2,512,256]{2,1,0:T(8,128)}, f32[8,128]{1,0:T(8,128)}) custom-call(s32[2]{0:T(128)} %owner.65, bf16[256,7168]{1,0:T(8,128)(2,1)} %refs_0_.17, bf16[256,7168]{1,0:T(8,128)(2,1)} %refs_1_.17, bf16[256,7168]{1,0:T(8,128)(2,1)} %refs_2_.15, bf16[256,7168]{1,0:T(8,128)(2,1)} %collective-permute-done.2.refs_3_, ...), custom_call_target="tpu_custom_call" | custom-call | flops 704643072 | bytes 5177344 | tf_op jit(solution)/shard_map/pallas_call | solution.py:348
  131.1 3.2 %collective-permute-done.19.rest_0_ = bf16[128,2688]{1,0:T(8,128)(2,1)} collective-permute-done((bf16[128,2688]{1,0:T(8,128)(2,1)}, bf16[128,2688]{1,0:T(8,128)(2,1)}, u32[]{:S(2)}, u32[]{:S(2)}) %collective-permute-start.19) | collective-permute-done | bytes 688160 | tf_op jit(solution)/shard_map/ppermute | solution.py:542
  137.7 6.8 %shard_map.153 = (f32[2,512,256]{2,1,0:T(8,128)}, f32[8,128]{1,0:T(8,128)}) custom-call(s32[2]{0:T(128)} %owner.65, bf16[256,7168]{1,0:T(8,128)(2,1)} %refs_0_.17, bf16[256,7168]{1,0:T(8,128)(2,1)} %refs_1_.17, bf16[256,7168]{1,0:T(8,128)(2,1)} %refs_2_.15, bf16[256,7168]{1,0:T(8,128)(2,1)} %collective-permute-done.2.refs_3_, ...), custom_call_target="tpu_custom_call" | custom-call | flops 704643072 | bytes 5177344 | tf_op jit(solution)/shard_map/pallas_call | solution.py:348
  145.8 3.5 %collective-permute-done.22.rest_0_ = bf16[128,2688]{1,0:T(8,128)(2,1)} collective-permute-done((bf16[128,2688]{1,0:T(8,128)(2,1)}, bf16[128,2688]{1,0:T(8,128)(2,1)}, u32[]{:S(2)}, u32[]{:S(2)}) %collective-permute-start.22) | collective-permute-done | bytes 688160 | tf_op jit(solution)/shard_map/ppermute | solution.py:542
  152.6 6.8 %shard_map.156 = (f32[2,512,256]{2,1,0:T(8,128)}, f32[8,128]{1,0:T(8,128)}) custom-call(s32[2]{0:T(128)} %owner.65, bf16[256,7168]{1,0:T(8,128)(2,1)} %refs_0_.17, bf16[256,7168]{1,0:T(8,128)(2,1)} %refs_1_.17, bf16[256,7168]{1,0:T(8,128)(2,1)} %refs_2_.15, bf16[256,7168]{1,0:T(8,128)(2,1)} %collective-permute-done.2.refs_3_, ...), custom_call_target="tpu_custom_call" | custom-call | flops 704643072 | bytes 5177344 | tf_op jit(solution)/shard_map/pallas_call | solution.py:348
  160.7 3.4 %collective-permute-done.25.rest_0_ = bf16[128,2688]{1,0:T(8,128)(2,1)} collective-permute-done((bf16[128,2688]{1,0:T(8,128)(2,1)}, bf16[128,2688]{1,0:T(8,128)(2,1)}, u32[]{:S(2)}, u32[]{:S(2)}) %collective-permute-start.25) | collective-permute-done | bytes 688160 | tf_op jit(solution)/shard_map/ppermute | solution.py:542
  167.5 6.8 %shard_map.159 = (f32[2,512,256]{2,1,0:T(8,128)}, f32[8,128]{1,0:T(8,128)}) custom-call(s32[2]{0:T(128)} %owner.65, bf16[256,7168]{1,0:T(8,128)(2,1)} %refs_0_.17, bf16[256,7168]{1,0:T(8,128)(2,1)} %refs_1_.17, bf16[256,7168]{1,0:T(8,128)(2,1)} %refs_2_.15, bf16[256,7168]{1,0:T(8,128)(2,1)} %collective-permute-done.2.refs_3_, ...), custom_call_target="tpu_custom_call" | custom-call | flops 704643072 | bytes 5177344 | tf_op jit(solution)/shard_map/pallas_call | solution.py:348
  175.7 3.2 %collective-permute-done.27.rest_0_ = bf16[128,2688]{1,0:T(8,128)(2,1)} collective-permute-done((bf16[128,2688]{1,0:T(8,128)(2,1)}, bf16[128,2688]{1,0:T(8,128)(2,1)}, u32[]{:S(2)}, u32[]{:S(2)}) %collective-permute-start.27) | collective-permute-done | bytes 688160 | tf_op jit(solution)/shard_map/ppermute | solution.py:542
  180.1 6.9 %shard_map.162 = (f32[2,128,256]{2,1,0:T(8,128)}, bf16[2,128,256]{2,1,0:T(8,128)(2,1)}, bf16[2,128,256]{2,1,0:T(8,128)(2,1)}, bf16[2,128,256]{2,1,0:T(8,128)(2,1)}, f32[8,128]{1,0:T(8,128)}) custom-call(s32[2]{0:T(128)} %owner.65, bf16[256,7168]{1,0:T(8,128)(2,1)} %refs_0_.17, bf16[256,7168]{1,0:T(8,128)(2,1)} %refs_1_.17, bf16[256,7168]{1,0:T(8,128)(2,1)} %refs_2_.15, ...), custom_call_target="tpu_custom_call" | custom-call | flops 704643072 | bytes 5177344 | tf_op jit(solution)/shard_map/pallas_call | solution.py:348
  201.6 5.4 %shard_map.163 = (f32[1,128,256]{2,1,0:T(8,128)}, bf16[1,128,256]{2,1,0:T(8,128)(2,1)}, bf16[1,128,256]{2,1,0:T(8,128)(2,1)}, bf16[1,128,256]{2,1,0:T(8,128)(2,1...) custom-call(s32[2]{0:T(128)} %owner.65, bf16[256,2048]{1,0:T(8,128)(2,1)} %refs_0_.19, bf16[256,2048]{1,0:T(8,128)(2,1)} %refs_1_.19, ...), custom_call_target="tpu_custom_call" | custom-call | flops 704643072 | bytes 5177344 | tf_op jit(solution)/shard_map/pallas_call | solution.py:348
  207.9 4.5 %shard_map.166 = (f32[1,128,256]{2,1,0:T(8,128)}, bf16[1,128,256]{2,1,0:T(8,128)(2,1)}, bf16[1,128,256]{2,1,0:T(8,128)(2,1)}, bf16[1,128,256]{2,1,0:T(8,128)(2,1)}, f32[8,128]{1,0:T(8,128)}) custom-call(s32[2]{0:T(128)} %owner.65, bf16[256,2048]{1,0:T(8,128)(2,1)} %refs_0_.19, bf16[256,2048]{1,0:T(8,128)(2,1)} %refs_1_.19, ...), custom_call_target="tpu_custom_call" | custom-call | flops 704643072 | bytes 5177344 | tf_op jit(solution)/shard_map/pallas_call | solution.py:348
  (121 shorter events, 111.9 us)
Async XLA Ops:
  17.4 18.6 %collective-permute-start.6 = (bf16[2,128,2688]{2,1,0:T(8,128)(2,1)}, bf16[2,128,2688]{2,1,0:T(8,128)(2,1)}, u32[]{:S(2)}, u32[]{:S(2)}) collective-permute-start(bf16[2,128,2688]{2,1,0:T(8,128)(2,1)} %get-tuple-element.59), channel_id=1, source_target_pairs={{0,4},{4,0},{8,12},{12,8},{16,20},{20,16},{24,28},{28,24},{1,5},{5... | collective-permute-start | bytes 4128776 | tf_op jit(solution)/shard_map/ppermute | solution.py:488
  22.0 14.0 %collective-permute-start.7 = (bf16[128,2688]{1,0:T(8,128)(2,1)}, bf16[128,2688]{1,0:T(8,128)(2,1)}, u32[]{:S(2)}, u32[]{:S(2)}) collective-permute-start(bf16[128,2688]{1,0:T(8,128)(2,1)} %shard_map.131.rest_0_.refs_7_.refs_6_), channel_id=1, source_target_pairs={{0,8},{4,20},{8,24},{12,4},{24,16},{28,12},{16,0},{20,28},{1,9},{5... | collective-permute-start | bytes 2064392 | tf_op jit(solution)/shard_map/ppermute | solution.py:542
  31.4 41.3 %collective-permute-start.2 = (bf16[256,7168]{1,0:T(8,128)(2,1)}, bf16[256,7168]{1,0:T(8,128)(2,1)}, u32[]{:S(2)}, u32[]{:S(2)}) collective-permute-start(bf16[256,7168]{1,0:T(8,128)(2,1)} %refs_0_.17), channel_id=1, source_target_pairs={{0,4},{4,0},{8,12},{12,8},{16,20},{20,16},{24,28},{28,24},{1,5},{5... | collective-permute-start | bytes 11010056 | tf_op jit(solution)/shard_map/ppermute | solution.py:499
  34.2 42.8 %collective-permute-start.5 = (bf16[256,7168]{1,0:T(8,128)(2,1)}, bf16[256,7168]{1,0:T(8,128)(2,1)}, u32[]{:S(2)}, u32[]{:S(2)}) collective-permute-start(bf16[256,7168]{1,0:T(8,128)(2,1)} %refs_1_.17), channel_id=1, source_target_pairs={{0,4},{4,0},{8,12},{12,8},{16,20},{20,16},{24,28},{28,24},{1,5},{5... | collective-permute-start | bytes 11010056 | tf_op jit(solution)/shard_map/ppermute | solution.py:499
  46.6 30.5 %collective-permute-start.9 = (bf16[256,7168]{1,0:T(8,128)(2,1)}, bf16[256,7168]{1,0:T(8,128)(2,1)}, u32[]{:S(2)}, u32[]{:S(2)}) collective-permute-start(bf16[256,7168]{1,0:T(8,128)(2,1)} %refs_2_.15), channel_id=1, source_target_pairs={{0,4},{4,0},{8,12},{12,8},{16,20},{20,16},{24,28},{28,24},{1,5},{5... | collective-permute-start | bytes 11010056 | tf_op jit(solution)/shard_map/ppermute | solution.py:499
  48.5 34.8 %collective-permute-start.11 = (bf16[2,128,2688]{2,1,0:T(8,128)(2,1)}, bf16[2,128,2688]{2,1,0:T(8,128)(2,1)}, u32[]{:S(2)}, u32[]{:S(2)}) collective-permute-start(bf16[2,128,2688]{2,1,0:T(8,128)(2,1)} %get-tuple-element.64), channel_id=1, source_target_pairs={{0,4},{4,0},{8,12},{12,8},{16,20},{20,16},{24,28},{28,24},{1,5},{5... | collective-permute-start | bytes 4128776 | tf_op jit(solution)/shard_map/ppermute | solution.py:488
  72.7 16.2 %collective-permute-start.13 = (bf16[128,2688]{1,0:T(8,128)(2,1)}, bf16[128,2688]{1,0:T(8,128)(2,1)}, u32[]{:S(2)}, u32[]{:S(2)}) collective-permute-start(bf16[128,2688]{1,0:T(8,128)(2,1)} %shard_map.139.refs_9_.refs_14_.refs_8_.refs_7_.refs_6_), channel_id=1, source_target_pairs={{0,8},{4,20},{8,24},{12,4},{24,16},{28,12},{16,0},{20,28},{1,9},{5... | collective-permute-start | bytes 2064392 | tf_op jit(solution)/shard_map/ppermute | solution.py:542
  84.2 15.8 %collective-permute-start.18 = (bf16[128,2688]{1,0:T(8,128)(2,1)}, bf16[128,2688]{1,0:T(8,128)(2,1)}, u32[]{:S(2)}, u32[]{:S(2)}) collective-permute-start(bf16[128,2688]{1,0:T(8,128)(2,1)} %shard_map.143.refs_13_.refs_16_.refs_12_.refs_11_.refs_10_), channel_id=1, source_target_pairs={{0,8},{4,20},{8,24},{12,4},{24,16},{28,12},{16,0},{20,28},{1,9},{5... | collective-permute-start | bytes 2064392 | tf_op jit(solution)/shard_map/ppermute | solution.py:542
  84.3 30.4 %collective-permute-start.10 = (bf16[2,128,2688]{2,1,0:T(8,128)(2,1)}, bf16[2,128,2688]{2,1,0:T(8,128)(2,1)}, u32[]{:S(2)}, u32[]{:S(2)}) collective-permute-start(bf16[2,128,2688]{2,1,0:T(8,128)(2,1)} %get-tuple-element.63), channel_id=1, source_target_pairs={{0,4},{4,0},{8,12},{12,8},{16,20},{20,16},{24,28},{28,24},{1,5},{5... | collective-permute-start | bytes 4128776 | tf_op jit(solution)/shard_map/ppermute | solution.py:488
  104.5 15.1 %collective-permute-start.17 = (bf16[128,2688]{1,0:T(8,128)(2,1)}, bf16[128,2688]{1,0:T(8,128)(2,1)}, u32[]{:S(2)}, u32[]{:S(2)}) collective-permute-start(bf16[128,2688]{1,0:T(8,128)(2,1)} %shard_map.145.refs_9_.refs_15_.refs_8_.refs_7_.refs_6_), channel_id=1, source_target_pairs={{0,8},{4,20},{8,24},{12,4},{24,16},{28,12},{16,0},{20,28},{1,9},{5... | collective-permute-start | bytes 2064392 | tf_op jit(solution)/shard_map/ppermute | solution.py:542
  115.6 14.2 %collective-permute-start.23 = (bf16[128,2688]{1,0:T(8,128)(2,1)}, bf16[128,2688]{1,0:T(8,128)(2,1)}, u32[]{:S(2)}, u32[]{:S(2)}) collective-permute-start(bf16[128,2688]{1,0:T(8,128)(2,1)} %shard_map.149.refs_13_.refs_16_.refs_12_.refs_11_.refs_10_), channel_id=1, source_target_pairs={{0,8},{4,20},{8,24},{12,4},{24,16},{28,12},{16,0},{20,28},{1,9},{5... | collective-permute-start | bytes 2064392 | tf_op jit(solution)/shard_map/ppermute | solution.py:542
  122.9 21.6 %collective-permute-start.21 = (bf16[1,128,2688]{2,1,0:T(8,128)(2,1)}, bf16[1,128,2688]{2,1,0:T(8,128)(2,1)}, u32[]{:S(2)}, u32[]{:S(2)}) collective-permute-start(bf16[1,128,2688]{2,1,0:T(8,128)(2,1)} %get-tuple-element.72), channel_id=1, source_target_pairs={{0,4},{4,0},{8,12},{12,8},{16,20},{20,16},{24,28},{28,24},{1,5},{5... | collective-permute-start | bytes 2064392 | tf_op jit(solution)/shard_map/ppermute | solution.py:488
  135.2 14.1 %collective-permute-start.22 = (bf16[128,2688]{1,0:T(8,128)(2,1)}, bf16[128,2688]{1,0:T(8,128)(2,1)}, u32[]{:S(2)}, u32[]{:S(2)}) collective-permute-start(bf16[128,2688]{1,0:T(8,128)(2,1)} %shard_map.151.refs_9_.refs_15_.refs_8_.refs_7_.refs_6_), channel_id=1, source_target_pairs={{0,8},{4,20},{8,24},{12,4},{24,16},{28,12},{16,0},{20,28},{1,9},{5... | collective-permute-start | bytes 2064392 | tf_op jit(solution)/shard_map/ppermute | solution.py:542
  137.7 21.7 %collective-permute-start.24 = (bf16[1,128,2688]{2,1,0:T(8,128)(2,1)}, bf16[1,128,2688]{2,1,0:T(8,128)(2,1)}, u32[]{:S(2)}, u32[]{:S(2)}) collective-permute-start(bf16[1,128,2688]{2,1,0:T(8,128)(2,1)} %get-tuple-element.75), channel_id=1, source_target_pairs={{0,4},{4,0},{8,12},{12,8},{16,20},{20,16},{24,28},{28,24},{1,5},{5... | collective-permute-start | bytes 2064392 | tf_op jit(solution)/shard_map/ppermute | solution.py:488
  145.3 14.1 %collective-permute-start.28 = (bf16[128,2688]{1,0:T(8,128)(2,1)}, bf16[128,2688]{1,0:T(8,128)(2,1)}, u32[]{:S(2)}, u32[]{:S(2)}) collective-permute-start(bf16[128,2688]{1,0:T(8,128)(2,1)} %shard_map.155.refs_13_.refs_16_.refs_12_.refs_11_.refs_8_), channel_id=1, source_target_pairs={{0,8},{4,20},{8,24},{12,4},{24,16},{28,12},{16,0},{20,28},{1,9},{5... | collective-permute-start | bytes 2064392 | tf_op jit(solution)/shard_map/ppermute | solution.py:542
  160.2 14.1 %collective-permute-start.29 = (bf16[128,2688]{1,0:T(8,128)(2,1)}, bf16[128,2688]{1,0:T(8,128)(2,1)}, u32[]{:S(2)}, u32[]{:S(2)}) collective-permute-start(bf16[128,2688]{1,0:T(8,128)(2,1)} %shard_map.158.refs_13_.refs_16_.refs_12_.refs_9_.refs_8_), channel_id=1, source_target_pairs={{0,8},{4,20},{8,24},{12,4},{24,16},{28,12},{16,0},{20,28},{1,9},{5... | collective-permute-start | bytes 2064392 | tf_op jit(solution)/shard_map/ppermute | solution.py:542
  164.9 14.1 %collective-permute-start.27 = (bf16[128,2688]{1,0:T(8,128)(2,1)}, bf16[128,2688]{1,0:T(8,128)(2,1)}, u32[]{:S(2)}, u32[]{:S(2)}) collective-permute-start(bf16[128,2688]{1,0:T(8,128)(2,1)} %shard_map.157.refs_9_.refs_15_.refs_8_.refs_5_.refs_4_), channel_id=1, source_target_pairs={{0,8},{4,20},{8,24},{12,4},{24,16},{28,12},{16,0},{20,28},{1,9},{5... | collective-permute-start | bytes 2064392 | tf_op jit(solution)/shard_map/ppermute | solution.py:542
  167.0 30.7 %collective-permute-start.33 = (bf16[256,2048]{1,0:T(8,128)(2,1)}, bf16[256,2048]{1,0:T(8,128)(2,1)}, u32[]{:S(2)}, u32[]{:S(2)}) collective-permute-start(bf16[256,2048]{1,0:T(8,128)(2,1)} %refs_0_.19), channel_id=1, source_target_pairs={{0,4},{4,0},{8,12},{12,8},{16,20},{20,16},{24,28},{28,24},{1,5},{5... | collective-permute-start | bytes 3145736 | tf_op jit(solution)/shard_map/ppermute | solution.py:499
  167.0 33.2 %collective-permute-start.34 = (bf16[256,2048]{1,0:T(8,128)(2,1)}, bf16[256,2048]{1,0:T(8,128)(2,1)}, u32[]{:S(2)}, u32[]{:S(2)}) collective-permute-start(bf16[256,2048]{1,0:T(8,128)(2,1)} %refs_1_.19), channel_id=1, source_target_pairs={{0,4},{4,0},{8,12},{12,8},{16,20},{20,16},{24,28},{28,24},{1,5},{5... | collective-permute-start | bytes 3145736 | tf_op jit(solution)/shard_map/ppermute | solution.py:499
  179.7 14.1 %collective-permute-start.35 = (bf16[128,2688]{1,0:T(8,128)(2,1)}, bf16[128,2688]{1,0:T(8,128)(2,1)}, u32[]{:S(2)}, u32[]{:S(2)}) collective-permute-start(bf16[128,2688]{1,0:T(8,128)(2,1)} %shard_map.160.refs_9_.refs_15_.refs_6_.refs_5_), channel_id=1, source_target_pairs={{0,8},{4,20},{8,24},{12,4},{24,16},{28,12},{16,0},{20,28},{1,9},{5... | collective-permute-start | bytes 2064392 | tf_op jit(solution)/shard_map/ppermute | solution.py:542
  188.8 18.3 %collective-permute-start.41 = (bf16[128,1408]{1,0:T(8,128)(2,1)}, bf16[128,1408]{1,0:T(8,128)(2,1)}, u32[]{:S(2)}, u32[]{:S(2)}) collective-permute-start(bf16[128,1408]{1,0:T(8,128)(2,1)} %shard_map.165), channel_id=1, source_target_pairs={{0,8},{4,20},{8,24},{12,4},{24,16},{28,12},{16,0},{20,28},{1,9},{5... | collective-permute-start | bytes 1081352 | tf_op jit(solution)/shard_map/ppermute | solution.py:545
  196.1 16.7 %collective-permute-start.30 = (bf16[2,128,256]{2,1,0:T(8,128)(2,1)}, bf16[2,128,256]{2,1,0:T(8,128)(2,1)S(1)}, u32[]{:S(2)}, u32[]{:S(2)}) collective-permute-start(bf16[2,128,256]{2,1,0:T(8,128)(2,1)} %get-tuple-element.82), channel_id=1, source_target_pairs={{0,1},{1,2},{2,3},{3,0},{4,5},{5,6},{6,7},{7,4},{8,9},{9,10},{10,1... | collective-permute-start | bytes 393224 | tf_op jit(solution)/shard_map/ppermute | solution.py:516
  197.7 18.0 %collective-permute-start.31 = (bf16[2,128,256]{2,1,0:T(8,128)(2,1)}, bf16[2,128,256]{2,1,0:T(8,128)(2,1)}, u32[]{:S(2)}, u32[]{:S(2)}) collective-permute-start(bf16[2,128,256]{2,1,0:T(8,128)(2,1)} %get-tuple-element.83), channel_id=1, source_target_pairs={{0,2},{1,3},{2,0},{3,1},{4,6},{5,7},{6,4},{7,5},{8,10},{9,11},{10,... | collective-permute-start | bytes 393224 | tf_op jit(solution)/shard_map/ppermute | solution.py:516
  200.3 16.0 %collective-permute-start.32 = (bf16[2,128,256]{2,1,0:T(8,128)(2,1)}, bf16[2,128,256]{2,1,0:T(8,128)(2,1)}, u32[]{:S(2)}, u32[]{:S(2)}) collective-permute-start(bf16[2,128,256]{2,1,0:T(8,128)(2,1)} %get-tuple-element.84), channel_id=1, source_target_pairs={{0,3},{1,0},{2,1},{3,2},{4,7},{5,4},{6,5},{7,6},{8,11},{9,8},{10,9... | collective-permute-start | bytes 393224 | tf_op jit(solution)/shard_map/ppermute | solution.py:516
  (27 other events, 261.9 us)

commit v5 on v4

--- a/solution.py
+++ b/solution.py
@@ -235,8 +235,11 @@
     for side, arrays in enumerate((own, sib)):
         loads.append([])
         for i, (which, src, dst, cols) in enumerate(parts):
+            first = 0
+            if side == 1 and k < groups:
+                first, which = (which % 2) * rows, which // 2
             copy = pltpu.make_async_copy(
-                arrays[which].at[:, pl.ds(src, cols)],
+                arrays[which].at[pl.ds(first, rows), pl.ds(src, cols)],
                 room.at[side, :, pl.ds(dst, cols)],
                 sem.at[2 + 3 * side + i],
             )
@@ -334,7 +337,7 @@
     n_cand, n_held = len(own), len(held)
 
     def body(owner, *refs):
-        a, b = n_cand, 2 * n_cand
+        a, b = n_cand, n_cand + len(sib)
         c = b + n_held
         d = c + len(priors)
         e = d + len(deps)
@@ -348,7 +351,7 @@
     results = pl.pallas_call(
         body,
         in_specs=[IN_SMEM]
-        + [IN_HBM] * (2 * n_cand + n_held + len(priors))
+        + [IN_HBM] * (n_cand + len(sib) + n_held + len(priors))
         + [ANYWHERE] * len(deps),
         out_specs=places + [IN_HBM],
         out_shape=shapes + [MARK],
@@ -494,8 +497,9 @@
     sib = []
 
     def send_next(deps):
-        array = own[len(sib)]
-        array = lax.optimization_barrier((array, *deps))[0]
+        arrays = (own[:2], own[2:3], own[3:4], own[4:])[len(sib)]
+        arrays = lax.optimization_barrier((*arrays, *deps))[: len(arrays)]
+        array = jnp.concatenate(arrays, axis=0) if len(arrays) > 1 else arrays[0]
         sib.append(lax.ppermute(array, "dp", across))
 
     sib_lengths = lax.ppermute(cand_lengths, "dp", across)
@@ -509,7 +513,8 @@
         came = [held[r][k + i] for r in range(ROUNDS) for i in range(chips)]
         kind = slice(0, 3) if k < groups else slice(3, 5)
         mark, done = use(
-            k, round_owner, groups, width, chips, n_tensor, own[kind], sib[kind], came, grams, deps
+            k, round_owner, groups, width, chips, n_tensor, own[kind],
+            sib[:2] if k < groups else sib[2:4], came, grams, deps
         )
         for name, pieces in done.items():
             parts[name] = [pieces[0]] + [
@@ -545,7 +550,7 @@
                 got[r] = lax.ppermute(last, "dp", along)
             if work and work[0][0] <= slot:
                 mark = work.pop(0)[1](latest(t, r))
-            if slot in (1, 3, 5, 9, 13):
+            if slot in (1, 4, 9, 13):
                 send_next([mark])
             slot += 1
     while work:

time: 239 us -> 244 us (1.021)
  starting transfers between devices: 64.1 us -> 34.5 us
  Pallas kernels: 108 us -> 124 us
  waiting for transfers between devices: 64 us -> 76.6 us
  other arithmetic: 1.3 us -> 7.99 us
    ppermute x22, starting transfers between devices: 41.2 us -> 8.42 us  [local(): got[r] = lax.ppermute(held[r][t], 'dp', along)]
    pallas_call x22, Pallas kernels: 21.8 us -> 38.1 us  [inject(): pl.pallas_call(functools.partial(inject_body, t, at, r, groups, width, n_...]
    ppermute x22, waiting for transfers between devices: 51.6 us -> 62.2 us  [local(): got[r] = lax.ppermute(held[r][t], 'dp', along)]
    concatenate x0 -> x1, other arithmetic: none -> 6.68 us  [send_next(): array = jnp.concatenate(arrays, axis=0) if len(arrays) > 1 else arrays[0]]
    ppermute x6, starting transfers between devices: 0.75 us -> 5.54 us  [send_half(): part = lax.ppermute(part, 'dp', across)]
  transfers between devices with their start and end apart: 49 -> 48, of which waited for: 20 -> 21; matrix products, arithmetic and copies ran while one was open for 0% -> 0% of each run, Pallas kernels for 42% -> 45%
where the time goes in v5:
time: 244 us
  Pallas kernels  124 us (51%)
  waiting for transfers between devices  76.6 us (31%)
  starting transfers between devices  34.5 us (14%)
  other arithmetic  7.99 us (3%)
    pallas_call x10, Pallas kernels, use(): pl.pallas_call(body, in_specs=[IN_SMEM] + [IN_HBM] * (n_cand + len(sib) +...  64 us
    ppermute x22, waiting for transfers between devices, local(): got[r] = lax.ppermute(held[r][t], 'dp', along)  62.2 us
    pallas_call x22, Pallas kernels, inject(): pl.pallas_call(functools.partial(inject_body, t, at, r, groups, width, n_...  38.1 us
    pallas_call x6, Pallas kernels, pack(): pl.pallas_call(functools.partial(pack_body, groups, width, first), grid_s...  16.1 us
    ppermute x9, starting transfers between devices, consume(): lax.ppermute(pieces[m], 'tensor', [(z, (z + m) % n_tensor) for z in range...  14.9 us
    ppermute x22, starting transfers between devices, local(): got[r] = lax.ppermute(held[r][t], 'dp', along)  8.42 us
    concatenate x1, other arithmetic, send_next(): array = jnp.concatenate(arrays, axis=0) if len(arrays) > 1 else arrays[0]  6.68 us
    ppermute x6, starting transfers between devices, send_half(): part = lax.ppermute(part, 'dp', across)  5.54 us
  transfers between devices with their start and end apart: 48, of which 21 were waited for; matrix products, arithmetic and copies ran while one was open for 0% of the time, Pallas kernels for 45%

profile of v5, /device:TPU:0, one launch (start us, length us, event | category | flops | bytes accessed | tf_op | source)
XLA Modules:
  0.0 243.7 jit_solution(17908687540308275795)
XLA Ops:
  14.5 6.7 %pad_maximum_fusion = bf16[512,7168]{1,0:T(8,128)(2,1)} fusion(bf16[256,7168]{1,0:T(8,128)(2,1)} %refs_1_.17, bf16[256,7168]{1,0:T(8,128)(2,1)} %refs_0_.17), kind=kLoop, calls=%fused_computation | loop fusion | flops 14680064 | bytes 14680064 | tf_op jit(solution)/shard_map/concatenate | solution.py:502
  25.7 7.5 %collective-permute-done.4.rest_0_ = bf16[128,2688]{1,0:T(8,128)(2,1)} collective-permute-done((bf16[128,2688]{1,0:T(8,128)(2,1)S(1)}, bf16[128,2688]{1,0:T(8,128)(2,1)}, u32[]{:S(2)}, u32[]{:S(2)}) %collective-permute-start.4) | collective-permute-done | bytes 688160 | tf_op jit(solution)/shard_map/ppermute | solution.py:547
  44.2 3.7 %collective-permute-done.5.rest_0_ = bf16[128,2688]{1,0:T(8,128)(2,1)} collective-permute-done((bf16[128,2688]{1,0:T(8,128)(2,1)}, bf16[128,2688]{1,0:T(8,128)(2,1)}, u32[]{:S(2)}, u32[]{:S(2)}) %collective-permute-start.5) | collective-permute-done | bytes 688160 | tf_op jit(solution)/shard_map/ppermute | solution.py:547
  54.7 9.5 %collective-permute-done.11.rest_0_ = bf16[128,2688]{1,0:T(8,128)(2,1)} collective-permute-done((bf16[128,2688]{1,0:T(8,128)(2,1)}, bf16[128,2688]{1,0:T(8,128)(2,1)}, u32[]{:S(2)}, u32[]{:S(2)}) %collective-permute-start.11) | collective-permute-done | bytes 688160 | tf_op jit(solution)/shard_map/ppermute | solution.py:547
  67.8 3.9 %collective-permute-done.10.rest_0_ = bf16[128,2688]{1,0:T(8,128)(2,1)} collective-permute-done((bf16[128,2688]{1,0:T(8,128)(2,1)}, bf16[128,2688]{1,0:T(8,128)(2,1)}, u32[]{:S(2)}, u32[]{:S(2)}) %collective-permute-start.10) | collective-permute-done | bytes 688160 | tf_op jit(solution)/shard_map/ppermute | solution.py:547
  74.4 4.7 %collective-permute-done.13.rest_0_ = bf16[128,2688]{1,0:T(8,128)(2,1)} collective-permute-done((bf16[128,2688]{1,0:T(8,128)(2,1)}, bf16[128,2688]{1,0:T(8,128)(2,1)}, u32[]{:S(2)}, u32[]{:S(2)}) %collective-permute-start.13) | collective-permute-done | bytes 688160 | tf_op jit(solution)/shard_map/ppermute | solution.py:547
  80.1 6.3 %shard_map.141 = (f32[2,512,256]{2,1,0:T(8,128)}, f32[8,128]{1,0:T(8,128)}) custom-call(s32[2]{0:T(128)} %owner.65, bf16[256,7168]{1,0:T(8,128)(2,1)} %refs_0_.17, bf16[256,7168]{1,0:T(8,128)(2,1)} %refs_1_.17, bf16[256,7168]{1,0:T(8,128)(2,1)} %refs_2_.15, bf16[512,7168]{1,0:T(8,128)(2,1)} %collective-permute-done.2.refs_3_, ...), custom_call_target="tpu_custom_call" | custom-call | flops 704643072 | bytes 5177344 | tf_op jit(solution)/shard_map/pallas_call | solution.py:351
  90.5 3.3 %collective-permute-done.15.rest_0_ = bf16[128,2688]{1,0:T(8,128)(2,1)} collective-permute-done((bf16[128,2688]{1,0:T(8,128)(2,1)}, bf16[128,2688]{1,0:T(8,128)(2,1)}, u32[]{:S(2)}, u32[]{:S(2)}) %collective-permute-start.15) | collective-permute-done | bytes 688160 | tf_op jit(solution)/shard_map/ppermute | solution.py:547
  94.9 6.8 %shard_map.144 = (f32[2,512,256]{2,1,0:T(8,128)}, f32[8,128]{1,0:T(8,128)}) custom-call(s32[2]{0:T(128)} %owner.65, bf16[256,7168]{1,0:T(8,128)(2,1)} %refs_0_.17, bf16[256,7168]{1,0:T(8,128)(2,1)} %refs_1_.17, bf16[256,7168]{1,0:T(8,128)(2,1)} %refs_2_.15, bf16[512,7168]{1,0:T(8,128)(2,1)} %collective-permute-done.2.refs_3_, ...), custom_call_target="tpu_custom_call" | custom-call | flops 704643072 | bytes 5177344 | tf_op jit(solution)/shard_map/pallas_call | solution.py:351
  104.4 4.1 %collective-permute-done.17.rest_0_ = bf16[128,2688]{1,0:T(8,128)(2,1)} collective-permute-done((bf16[128,2688]{1,0:T(8,128)(2,1)}, bf16[128,2688]{1,0:T(8,128)(2,1)}, u32[]{:S(2)}, u32[]{:S(2)}) %collective-permute-start.17) | collective-permute-done | bytes 688160 | tf_op jit(solution)/shard_map/ppermute | solution.py:547
  109.6 6.8 %shard_map.147 = (f32[2,512,256]{2,1,0:T(8,128)}, f32[8,128]{1,0:T(8,128)}) custom-call(s32[2]{0:T(128)} %owner.65, bf16[256,7168]{1,0:T(8,128)(2,1)} %refs_0_.17, bf16[256,7168]{1,0:T(8,128)(2,1)} %refs_1_.17, bf16[256,7168]{1,0:T(8,128)(2,1)} %refs_2_.15, bf16[512,7168]{1,0:T(8,128)(2,1)} %collective-permute-done.2.refs_3_, ...), custom_call_target="tpu_custom_call" | custom-call | flops 704643072 | bytes 5177344 | tf_op jit(solution)/shard_map/pallas_call | solution.py:351
  119.2 4.1 %collective-permute-done.19.rest_0_ = bf16[128,2688]{1,0:T(8,128)(2,1)} collective-permute-done((bf16[128,2688]{1,0:T(8,128)(2,1)}, bf16[128,2688]{1,0:T(8,128)(2,1)}, u32[]{:S(2)}, u32[]{:S(2)}) %collective-permute-start.19) | collective-permute-done | bytes 688160 | tf_op jit(solution)/shard_map/ppermute | solution.py:547
  126.1 6.8 %shard_map.150 = (f32[2,512,256]{2,1,0:T(8,128)}, f32[8,128]{1,0:T(8,128)}) custom-call(s32[2]{0:T(128)} %owner.65, bf16[256,7168]{1,0:T(8,128)(2,1)} %refs_0_.17, bf16[256,7168]{1,0:T(8,128)(2,1)} %refs_1_.17, bf16[256,7168]{1,0:T(8,128)(2,1)} %refs_2_.15, bf16[512,7168]{1,0:T(8,128)(2,1)} %collective-permute-done.2.refs_3_, ...), custom_call_target="tpu_custom_call" | custom-call | flops 704643072 | bytes 5177344 | tf_op jit(solution)/shard_map/pallas_call | solution.py:351
  140.9 6.8 %shard_map.153 = (f32[2,512,256]{2,1,0:T(8,128)}, f32[8,128]{1,0:T(8,128)}) custom-call(s32[2]{0:T(128)} %owner.65, bf16[256,7168]{1,0:T(8,128)(2,1)} %refs_0_.17, bf16[256,7168]{1,0:T(8,128)(2,1)} %refs_1_.17, bf16[256,7168]{1,0:T(8,128)(2,1)} %refs_2_.15, bf16[512,7168]{1,0:T(8,128)(2,1)} %collective-permute-done.2.refs_3_, ...), custom_call_target="tpu_custom_call" | custom-call | flops 704643072 | bytes 5177344 | tf_op jit(solution)/shard_map/pallas_call | solution.py:351
  150.4 3.9 %collective-permute-done.25.rest_0_ = bf16[128,2688]{1,0:T(8,128)(2,1)} collective-permute-done((bf16[128,2688]{1,0:T(8,128)(2,1)}, bf16[128,2688]{1,0:T(8,128)(2,1)}, u32[]{:S(2)}, u32[]{:S(2)}) %collective-permute-start.25) | collective-permute-done | bytes 688160 | tf_op jit(solution)/shard_map/ppermute | solution.py:547
  155.4 6.8 %shard_map.156 = (f32[2,512,256]{2,1,0:T(8,128)}, f32[8,128]{1,0:T(8,128)}) custom-call(s32[2]{0:T(128)} %owner.65, bf16[256,7168]{1,0:T(8,128)(2,1)} %refs_0_.17, bf16[256,7168]{1,0:T(8,128)(2,1)} %refs_1_.17, bf16[256,7168]{1,0:T(8,128)(2,1)} %refs_2_.15, bf16[512,7168]{1,0:T(8,128)(2,1)} %collective-permute-done.2.refs_3_, ...), custom_call_target="tpu_custom_call" | custom-call | flops 704643072 | bytes 5177344 | tf_op jit(solution)/shard_map/pallas_call | solution.py:351
  164.8 4.2 %collective-permute-done.27.rest_0_ = bf16[128,2688]{1,0:T(8,128)(2,1)} collective-permute-done((bf16[128,2688]{1,0:T(8,128)(2,1)}, bf16[128,2688]{1,0:T(8,128)(2,1)}, u32[]{:S(2)}, u32[]{:S(2)}) %collective-permute-start.27) | collective-permute-done | bytes 688160 | tf_op jit(solution)/shard_map/ppermute | solution.py:547
  170.5 6.8 %shard_map.159 = (f32[2,512,256]{2,1,0:T(8,128)}, f32[8,128]{1,0:T(8,128)}) custom-call(s32[2]{0:T(128)} %owner.65, bf16[256,7168]{1,0:T(8,128)(2,1)} %refs_0_.17, bf16[256,7168]{1,0:T(8,128)(2,1)} %refs_1_.17, bf16[256,7168]{1,0:T(8,128)(2,1)} %refs_2_.15, bf16[512,7168]{1,0:T(8,128)(2,1)} %collective-permute-done.2.refs_3_, ...), custom_call_target="tpu_custom_call" | custom-call | flops 704643072 | bytes 5177344 | tf_op jit(solution)/shard_map/pallas_call | solution.py:351
  178.4 5.3 %collective-permute-done.28.rest_0_ = bf16[128,2688]{1,0:T(8,128)(2,1)} collective-permute-done((bf16[128,2688]{1,0:T(8,128)(2,1)}, bf16[128,2688]{1,0:T(8,128)(2,1)}, u32[]{:S(2)}, u32[]{:S(2)}) %collective-permute-start.28) | collective-permute-done | bytes 688160 | tf_op jit(solution)/shard_map/ppermute | solution.py:547
  184.6 7.0 %shard_map.162 = (f32[2,128,256]{2,1,0:T(8,128)}, bf16[2,128,256]{2,1,0:T(8,128)(2,1)}, bf16[2,128,256]{2,1,0:T(8,128)(2,1)}, bf16[2,128,256]{2,1,0:T(8,128)(2,1)}, f32[8,128]{1,0:T(8,128)}) custom-call(s32[2]{0:T(128)} %owner.65, bf16[256,7168]{1,0:T(8,128)(2,1)} %refs_0_.17, bf16[256,7168]{1,0:T(8,128)(2,1)} %refs_1_.17, bf16[256,7168]{1,0:T(8,128)(2,1)} %refs_2_.15, ...), custom_call_target="tpu_custom_call" | custom-call | flops 704643072 | bytes 5177344 | tf_op jit(solution)/shard_map/pallas_call | solution.py:351
  194.6 3.9 %collective-permute-done.35.refs_11_.refs_13_.source.refs_10_ = bf16[128,2688]{1,0:T(8,128)(2,1)} collective-permute-done((bf16[128,2688]{1,0:T(8,128)(2,1)}, bf16[128,2688]{1,0:T(8,128)(2,1)}, u32[]{:S(2)}, u32[]{:S(2)}) %collective-permute-start.35) | collective-permute-done | bytes 688160 | tf_op jit(solution)/shard_map/ppermute | solution.py:547
  206.4 5.4 %shard_map.163 = (f32[1,128,256]{2,1,0:T(8,128)}, bf16[1,128,256]{2,1,0:T(8,128)(2,1)}, bf16[1,128,256]{2,1,0:T(8,128)(2,1)}, bf16[1,128,256]{2,1,0:T(8,128)(2,1...) custom-call(s32[2]{0:T(128)} %owner.65, bf16[256,2048]{1,0:T(8,128)(2,1)} %refs_0_.19, bf16[256,2048]{1,0:T(8,128)(2,1)} %refs_1_.19, ...), custom_call_target="tpu_custom_call" | custom-call | flops 704643072 | bytes 5177344 | tf_op jit(solution)/shard_map/pallas_call | solution.py:351
  212.7 4.5 %shard_map.166 = (f32[1,128,256]{2,1,0:T(8,128)}, bf16[1,128,256]{2,1,0:T(8,128)(2,1)}, bf16[1,128,256]{2,1,0:T(8,128)(2,1)}, bf16[1,128,256]{2,1,0:T(8,128)(2,1)}, f32[8,128]{1,0:T(8,128)}) custom-call(s32[2]{0:T(128)} %owner.65, bf16[256,2048]{1,0:T(8,128)(2,1)} %refs_0_.19, bf16[256,2048]{1,0:T(8,128)(2,1)} %refs_1_.19, ...), custom_call_target="tpu_custom_call" | custom-call | flops 704643072 | bytes 5177344 | tf_op jit(solution)/shard_map/pallas_call | solution.py:351
  238.9 3.2 %collective-permute-done.46 = f32[2,8,128]{2,1,0:T(8,128)S(1)} collective-permute-done((f32[2,8,128]{2,1,0:T(8,128)S(1)}, f32[2,8,128]{2,1,0:T(8,128)S(1)}, u32[]{:S(2)}, u32[]{:S(2)}) %collective-permute-start.46) | collective-permute-done | bytes 8224 | tf_op jit(solution)/shard_map/ppermute | solution.py:565
  (122 shorter events, 111.2 us)
Async XLA Ops:
  21.2 58.9 %collective-permute-start.2 = (bf16[512,7168]{1,0:T(8,128)(2,1)}, bf16[512,7168]{1,0:T(8,128)(2,1)}, u32[]{:S(2)}, u32[]{:S(2)}) collective-permute-start(bf16[512,7168]{1,0:T(8,128)(2,1)} %pad_maximum_fusion), channel_id=1, source_target_pairs={{0,4},{4,0},{8,12},{12,8},{16,20},{20,16},{24,28},{28,24},{1,5},{5... | collective-permute-start | bytes 22020104 | tf_op jit(solution)/shard_map/ppermute | solution.py:503
  24.1 20.1 %collective-permute-start.3 = (bf16[2,128,2688]{2,1,0:T(8,128)(2,1)}, bf16[2,128,2688]{2,1,0:T(8,128)(2,1)}, u32[]{:S(2)}, u32[]{:S(2)}) collective-permute-start(bf16[2,128,2688]{2,1,0:T(8,128)(2,1)} %get-tuple-element.57), channel_id=1, source_target_pairs={{0,4},{4,0},{8,12},{12,8},{16,20},{20,16},{24,28},{28,24},{1,5},{5... | collective-permute-start | bytes 4128776 | tf_op jit(solution)/shard_map/ppermute | solution.py:491
  24.3 16.3 %collective-permute-start.6 = (bf16[128,2688]{1,0:T(8,128)(2,1)}, bf16[128,2688]{1,0:T(8,128)(2,1)}, u32[]{:S(2)}, u32[]{:S(2)}) collective-permute-start(bf16[128,2688]{1,0:T(8,128)(2,1)} %shard_map.129.rest_1_.refs_9_), channel_id=1, source_target_pairs={{0,8},{4,20},{8,24},{12,4},{24,16},{28,12},{16,0},{20,28},{1,9},{5... | collective-permute-start | bytes 2064392 | tf_op jit(solution)/shard_map/ppermute | solution.py:547
  53.0 27.1 %collective-permute-start.7 = (bf16[256,7168]{1,0:T(8,128)(2,1)}, bf16[256,7168]{1,0:T(8,128)(2,1)}, u32[]{:S(2)}, u32[]{:S(2)}) collective-permute-start(bf16[256,7168]{1,0:T(8,128)(2,1)} %refs_2_.15), channel_id=1, source_target_pairs={{0,4},{4,0},{8,12},{12,8},{16,20},{20,16},{24,28},{28,24},{1,5},{5... | collective-permute-start | bytes 11010056 | tf_op jit(solution)/shard_map/ppermute | solution.py:503
  53.2 18.4 %collective-permute-start.10 = (bf16[128,2688]{1,0:T(8,128)(2,1)}, bf16[128,2688]{1,0:T(8,128)(2,1)}, u32[]{:S(2)}, u32[]{:S(2)}) collective-permute-start(bf16[128,2688]{1,0:T(8,128)(2,1)} %shard_map.135.rest_0_.refs_7_.refs_6_.refs_5_), channel_id=1, source_target_pairs={{0,8},{4,20},{8,24},{12,4},{24,16},{28,12},{16,0},{20,28},{1,9},{5... | collective-permute-start | bytes 2064392 | tf_op jit(solution)/shard_map/ppermute | solution.py:547
  54.7 31.7 %collective-permute-start.9 = (bf16[2,128,2688]{2,1,0:T(8,128)(2,1)}, bf16[2,128,2688]{2,1,0:T(8,128)(2,1)}, u32[]{:S(2)}, u32[]{:S(2)}) collective-permute-start(bf16[2,128,2688]{2,1,0:T(8,128)(2,1)} %get-tuple-element.63), channel_id=1, source_target_pairs={{0,4},{4,0},{8,12},{12,8},{16,20},{20,16},{24,28},{28,24},{1,5},{5... | collective-permute-start | bytes 4128776 | tf_op jit(solution)/shard_map/ppermute | solution.py:491
  65.1 13.9 %collective-permute-start.13 = (bf16[128,2688]{1,0:T(8,128)(2,1)}, bf16[128,2688]{1,0:T(8,128)(2,1)}, u32[]{:S(2)}, u32[]{:S(2)}) collective-permute-start(bf16[128,2688]{1,0:T(8,128)(2,1)} %shard_map.137.rest_1_.refs_11_.refs_10_.refs_9_), channel_id=1, source_target_pairs={{0,8},{4,20},{8,24},{12,4},{24,16},{28,12},{16,0},{20,28},{1,9},{5... | collective-permute-start | bytes 2064392 | tf_op jit(solution)/shard_map/ppermute | solution.py:547
  79.9 13.9 %collective-permute-start.15 = (bf16[128,2688]{1,0:T(8,128)(2,1)}, bf16[128,2688]{1,0:T(8,128)(2,1)}, u32[]{:S(2)}, u32[]{:S(2)}) collective-permute-start(bf16[128,2688]{1,0:T(8,128)(2,1)} %shard_map.140.refs_12_.refs_14_.refs_11_.refs_10_.refs_9_), channel_id=1, source_target_pairs={{0,8},{4,20},{8,24},{12,4},{24,16},{28,12},{16,0},{20,28},{1,9},{5... | collective-permute-start | bytes 2064392 | tf_op jit(solution)/shard_map/ppermute | solution.py:547
  89.2 27.3 %collective-permute-start.8 = (bf16[2,128,2688]{2,1,0:T(8,128)(2,1)}, bf16[2,128,2688]{2,1,0:T(8,128)(2,1)}, u32[]{:S(2)}, u32[]{:S(2)}) collective-permute-start(bf16[2,128,2688]{2,1,0:T(8,128)(2,1)} %get-tuple-element.62), channel_id=1, source_target_pairs={{0,4},{4,0},{8,12},{12,8},{16,20},{20,16},{24,28},{28,24},{1,5},{5... | collective-permute-start | bytes 4128776 | tf_op jit(solution)/shard_map/ppermute | solution.py:491
  94.6 13.9 %collective-permute-start.17 = (bf16[128,2688]{1,0:T(8,128)(2,1)}, bf16[128,2688]{1,0:T(8,128)(2,1)}, u32[]{:S(2)}, u32[]{:S(2)}) collective-permute-start(bf16[128,2688]{1,0:T(8,128)(2,1)} %shard_map.143.refs_12_.refs_15_.refs_11_.refs_10_.refs_9_), channel_id=1, source_target_pairs={{0,8},{4,20},{8,24},{12,4},{24,16},{28,12},{16,0},{20,28},{1,9},{5... | collective-permute-start | bytes 2064392 | tf_op jit(solution)/shard_map/ppermute | solution.py:547
  109.4 13.9 %collective-permute-start.19 = (bf16[128,2688]{1,0:T(8,128)(2,1)}, bf16[128,2688]{1,0:T(8,128)(2,1)}, u32[]{:S(2)}, u32[]{:S(2)}) collective-permute-start(bf16[128,2688]{1,0:T(8,128)(2,1)} %shard_map.146.refs_12_.refs_15_.refs_11_.refs_10_.refs_9_), channel_id=1, source_target_pairs={{0,8},{4,20},{8,24},{12,4},{24,16},{28,12},{16,0},{20,28},{1,9},{5... | collective-permute-start | bytes 2064392 | tf_op jit(solution)/shard_map/ppermute | solution.py:547
  124.1 13.9 %collective-permute-start.22 = (bf16[128,2688]{1,0:T(8,128)(2,1)}, bf16[128,2688]{1,0:T(8,128)(2,1)}, u32[]{:S(2)}, u32[]{:S(2)}) collective-permute-start(bf16[128,2688]{1,0:T(8,128)(2,1)} %shard_map.149.refs_12_.refs_15_.refs_11_.refs_10_.refs_9_), channel_id=1, source_target_pairs={{0,8},{4,20},{8,24},{12,4},{24,16},{28,12},{16,0},{20,28},{1,9},{5... | collective-permute-start | bytes 2064392 | tf_op jit(solution)/shard_map/ppermute | solution.py:547
  124.3 23.4 %collective-permute-start.20 = (bf16[1,128,2688]{2,1,0:T(8,128)(2,1)}, bf16[1,128,2688]{2,1,0:T(8,128)(2,1)}, u32[]{:S(2)}, u32[]{:S(2)}) collective-permute-start(bf16[1,128,2688]{2,1,0:T(8,128)(2,1)} %get-tuple-element.72), channel_id=1, source_target_pairs={{0,4},{4,0},{8,12},{12,8},{16,20},{20,16},{24,28},{28,24},{1,5},{5... | collective-permute-start | bytes 2064392 | tf_op jit(solution)/shard_map/ppermute | solution.py:491
  138.9 15.4 %collective-permute-start.25 = (bf16[128,2688]{1,0:T(8,128)(2,1)}, bf16[128,2688]{1,0:T(8,128)(2,1)}, u32[]{:S(2)}, u32[]{:S(2)}) collective-permute-start(bf16[128,2688]{1,0:T(8,128)(2,1)} %shard_map.152.refs_12_.refs_15_.refs_11_.refs_10_.refs_9_), channel_id=1, source_target_pairs={{0,8},{4,20},{8,24},{12,4},{24,16},{28,12},{16,0},{20,28},{1,9},{5... | collective-permute-start | bytes 2064392 | tf_op jit(solution)/shard_map/ppermute | solution.py:547
  139.1 23.1 %collective-permute-start.23 = (bf16[1,128,2688]{2,1,0:T(8,128)(2,1)}, bf16[1,128,2688]{2,1,0:T(8,128)(2,1)}, u32[]{:S(2)}, u32[]{:S(2)}) collective-permute-start(bf16[1,128,2688]{2,1,0:T(8,128)(2,1)} %get-tuple-element.75), channel_id=1, source_target_pairs={{0,4},{4,0},{8,12},{12,8},{16,20},{20,16},{24,28},{28,24},{1,5},{5... | collective-permute-start | bytes 2064392 | tf_op jit(solution)/shard_map/ppermute | solution.py:491
  155.1 13.9 %collective-permute-start.27 = (bf16[128,2688]{1,0:T(8,128)(2,1)}, bf16[128,2688]{1,0:T(8,128)(2,1)}, u32[]{:S(2)}, u32[]{:S(2)}) collective-permute-start(bf16[128,2688]{1,0:T(8,128)(2,1)} %shard_map.155.refs_12_.refs_15_.refs_11_.refs_10_.refs_8_), channel_id=1, source_target_pairs={{0,8},{4,20},{8,24},{12,4},{24,16},{28,12},{16,0},{20,28},{1,9},{5... | collective-permute-start | bytes 2064392 | tf_op jit(solution)/shard_map/ppermute | solution.py:547
  169.9 13.9 %collective-permute-start.28 = (bf16[128,2688]{1,0:T(8,128)(2,1)}, bf16[128,2688]{1,0:T(8,128)(2,1)}, u32[]{:S(2)}, u32[]{:S(2)}) collective-permute-start(bf16[128,2688]{1,0:T(8,128)(2,1)} %shard_map.158.refs_12_.refs_15_.refs_11_.refs_9_.refs_8_), channel_id=1, source_target_pairs={{0,8},{4,20},{8,24},{12,4},{24,16},{28,12},{16,0},{20,28},{1,9},{5... | collective-permute-start | bytes 2064392 | tf_op jit(solution)/shard_map/ppermute | solution.py:547
  169.9 32.5 %collective-permute-start.32 = (bf16[256,2048]{1,0:T(8,128)(2,1)}, bf16[256,2048]{1,0:T(8,128)(2,1)}, u32[]{:S(2)}, u32[]{:S(2)}) collective-permute-start(bf16[256,2048]{1,0:T(8,128)(2,1)} %refs_0_.19), channel_id=1, source_target_pairs={{0,4},{4,0},{8,12},{12,8},{16,20},{20,16},{24,28},{28,24},{1,5},{5... | collective-permute-start | bytes 3145736 | tf_op jit(solution)/shard_map/ppermute | solution.py:503
  170.4 34.6 %collective-permute-start.33 = (bf16[256,2048]{1,0:T(8,128)(2,1)}, bf16[256,2048]{1,0:T(8,128)(2,1)}, u32[]{:S(2)}, u32[]{:S(2)}) collective-permute-start(bf16[256,2048]{1,0:T(8,128)(2,1)} %refs_1_.19), channel_id=1, source_target_pairs={{0,4},{4,0},{8,12},{12,8},{16,20},{20,16},{24,28},{28,24},{1,5},{5... | collective-permute-start | bytes 3145736 | tf_op jit(solution)/shard_map/ppermute | solution.py:503
  184.6 14.0 %collective-permute-start.35 = (bf16[128,2688]{1,0:T(8,128)(2,1)}, bf16[128,2688]{1,0:T(8,128)(2,1)}, u32[]{:S(2)}, u32[]{:S(2)}) collective-permute-start(bf16[128,2688]{1,0:T(8,128)(2,1)} %shard_map.161.refs_12_.refs_15_.refs_10_.refs_9_), channel_id=1, source_target_pairs={{0,8},{4,20},{8,24},{12,4},{24,16},{28,12},{16,0},{20,28},{1,9},{5... | collective-permute-start | bytes 2064392 | tf_op jit(solution)/shard_map/ppermute | solution.py:547
  193.3 18.5 %collective-permute-start.39 = (bf16[128,1408]{1,0:T(8,128)(2,1)}, bf16[128,1408]{1,0:T(8,128)(2,1)}, u32[]{:S(2)}, u32[]{:S(2)}) collective-permute-start(bf16[128,1408]{1,0:T(8,128)(2,1)} %shard_map.164), channel_id=1, source_target_pairs={{0,8},{4,20},{8,24},{12,4},{24,16},{28,12},{16,0},{20,28},{1,9},{5... | collective-permute-start | bytes 1081352 | tf_op jit(solution)/shard_map/ppermute | solution.py:550
  200.3 17.2 %collective-permute-start.29 = (bf16[2,128,256]{2,1,0:T(8,128)(2,1)}, bf16[2,128,256]{2,1,0:T(8,128)(2,1)S(1)}, u32[]{:S(2)}, u32[]{:S(2)}) collective-permute-start(bf16[2,128,256]{2,1,0:T(8,128)(2,1)} %get-tuple-element.82), channel_id=1, source_target_pairs={{0,1},{1,2},{2,3},{3,0},{4,5},{5,6},{6,7},{7,4},{8,9},{9,10},{10,1... | collective-permute-start | bytes 393224 | tf_op jit(solution)/shard_map/ppermute | solution.py:521
  202.5 18.0 %collective-permute-start.30 = (bf16[2,128,256]{2,1,0:T(8,128)(2,1)}, bf16[2,128,256]{2,1,0:T(8,128)(2,1)}, u32[]{:S(2)}, u32[]{:S(2)}) collective-permute-start(bf16[2,128,256]{2,1,0:T(8,128)(2,1)} %get-tuple-element.83), channel_id=1, source_target_pairs={{0,2},{1,3},{2,0},{3,1},{4,6},{5,7},{6,4},{7,5},{8,10},{9,11},{10,... | collective-permute-start | bytes 393224 | tf_op jit(solution)/shard_map/ppermute | solution.py:521
  205.0 16.0 %collective-permute-start.31 = (bf16[2,128,256]{2,1,0:T(8,128)(2,1)}, bf16[2,128,256]{2,1,0:T(8,128)(2,1)}, u32[]{:S(2)}, u32[]{:S(2)}) collective-permute-start(bf16[2,128,256]{2,1,0:T(8,128)(2,1)} %get-tuple-element.84), channel_id=1, source_target_pairs={{0,3},{1,0},{2,1},{3,2},{4,7},{5,4},{6,5},{7,6},{8,11},{9,8},{10,9... | collective-permute-start | bytes 393224 | tf_op jit(solution)/shard_map/ppermute | solution.py:521
  (27 other events, 249.5 us)
